TPU v7x, 32 devices: a whole 2x2x4 slice. The times are simulated.
32 devices in a mesh: rep: 4 (over x, core), shard: 8 (over z, y).
Axes of the slice: x: 2, y: 2, z: 4, core: 2. Of those that a mesh axis runs over, the one named last changes fastest.
Arguments:
- tokens: bfloat16 [16384, 1024], P(('rep', 'shard')), may hold values from -6 to 6
- cotangent: bfloat16 [16384, 1024], P(('rep', 'shard')), may hold values from -6 to 6
- seq_lengths: int32 [32, 8], P(('rep', 'shard')), may hold values from 0 to 512, as said below
- mixer_in: float32 [1024, 4120], P('shard'), may hold values from -0.1875 to 0.1875
- mixer_in_mean: float32 [1024, 4120], P('shard'), may hold values from -20 to 20
- mixer_in_square: float32 [1024, 4120], P('shard'), may hold values from 52.4288 to 206.4384
- mixer_out: float32 [2048, 1024], P('shard'), may hold values from -0.1875 to 0.1875
- mixer_out_mean: float32 [2048, 1024], P('shard'), may hold values from -64 to 64
- mixer_out_square: float32 [2048, 1024], P('shard'), may hold values from 573.44 to 2293.76
- swiglu_in: float32 [1024, 4096], P('shard'), may hold values from -0.1875 to 0.1875
- swiglu_in_mean: float32 [1024, 4096], P('shard'), may hold values from -32 to 32
- swiglu_in_square: float32 [1024, 4096], P('shard'), may hold values from 144.1792 to 573.44
- swiglu_out: float32 [2048, 1024], P('shard'), may hold values from -0.125 to 0.125
- swiglu_out_mean: float32 [2048, 1024], P('shard'), may hold values from -40 to 40
- swiglu_out_square: float32 [2048, 1024], P('shard'), may hold values from 206.4384 to 819.2
- gains: float32 [3584], P('shard'), may hold values from 0.5 to 1.5
- gains_mean: float32 [3584], P('shard'), may hold values from -64 to 64
- gains_square: float32 [3584], P('shard'), may hold values from 573.44 to 2293.76
- conv_kernel: float32 [5, 1792], P(None, 'shard'), may hold values from -3 to 3
- conv_kernel_mean: float32 [5, 1792], P(None, 'shard'), may hold values from -32 to 32
- conv_kernel_square: float32 [5, 1792], P(None, 'shard'), may hold values from 144.1792 to 573.44
- head_params: float32 [3, 24], replicated, may hold values from -4 to 2.7, as said below
- head_params_mean: float32 [3, 24], replicated, may hold values from -224 to 224
- head_params_square: float32 [3, 24], replicated, may hold values from 5242.88 to 20643.84
Outputs:
- block_out: bfloat16 [16384, 1024], P(('rep', 'shard'))
- tokens_grad: float32 [16384, 1024], P(('rep', 'shard'))
- mixer_in_new: float32 [1024, 4120], P('shard')
- mixer_in_mean_new: float32 [1024, 4120], P('shard')
- mixer_in_square_new: float32 [1024, 4120], P('shard')
- mixer_out_new: float32 [2048, 1024], P('shard')
- mixer_out_mean_new: float32 [2048, 1024], P('shard')
- mixer_out_square_new: float32 [2048, 1024], P('shard')
- swiglu_in_new: float32 [1024, 4096], P('shard')
- swiglu_in_mean_new: float32 [1024, 4096], P('shard')
- swiglu_in_square_new: float32 [1024, 4096], P('shard')
- swiglu_out_new: float32 [2048, 1024], P('shard')
- swiglu_out_mean_new: float32 [2048, 1024], P('shard')
- swiglu_out_square_new: float32 [2048, 1024], P('shard')
- gains_new: float32 [3584], P('shard')
- gains_mean_new: float32 [3584], P('shard')
- gains_square_new: float32 [3584], P('shard')
- conv_kernel_new: float32 [5, 1792], P(None, 'shard')
- conv_kernel_mean_new: float32 [5, 1792], P(None, 'shard')
- conv_kernel_square_new: float32 [5, 1792], P(None, 'shard')
- head_params_new: float32 [3, 24], replicated
- head_params_mean_new: float32 [3, 24], replicated
- head_params_square_new: float32 [3, 24], replicated
Inputs may be any that keep to these rules, and one draw needn't show every extreme that they name: `seq_lengths`: row b gives the lengths of the sequences of block b in order, 0 for unused entries; a row sums to 128 or more and 512 or less; some block holds one sequence of 512 tokens. `head_params`: row 0 within -4 to -1, row 1 within -0.5 to 2.7, row 2 within 0.5 to 1.5.
All inputs are finite; a program needn't handle non-finite values.
Results may differ from a plain program's by a relative error of at most 0.012.
The roundings to bfloat16 on the way count: a program that leaves them out, or rounds other values in their place, can miss the bound.
Values may be sent and summed in bfloat16 or wider, within the bound.
No kernel may reach another device: no remote copies, remote signals or barrier semaphores. Data moves between devices by JAX's collectives and lax.ppermute only.
A program may use at most 256 MiB of HBM per device.

v0:
```python
import jax
import jax.numpy as jnp
from jax import lax
from jax.sharding import PartitionSpec as P

D = 1024
FF = 2048
QUERY_HEADS = 8
KEY_VALUE_HEADS = 2
HEAD_SIZE = 64
MH = 24
MP = 64
NS = 128
KC = 4
STEP = 10


NORM_EPS = 1e-05
ROPE_BASE = 100000000000.0
BETA_MEAN = 0.9
BETA_SQUARE = 0.95
ADAM_EPS = 1e-08
DECAY = 0.1
MATRIX_RATE = 0.03
VECTOR_RATE = 0.5


def make_rounders():

    def round_value(values):
        return lax.optimization_barrier(values.astype(jnp.bfloat16)).astype(jnp.float32)

    def pass_value(values):
        return values

    value_rounder = jax.custom_vjp(round_value)
    grad_rounder = jax.custom_vjp(pass_value)

    def value_keep(values):
        return (round_value(values), None)

    def value_pass(kept, grad):
        return (grad,)

    def grad_keep(values):
        return (values, None)

    def grad_round(kept, grad):
        return (round_value(grad),)

    value_rounder.defvjp(value_keep, value_pass)
    grad_rounder.defvjp(grad_keep, grad_round)
    return (value_rounder, grad_rounder)


def normalize(values, gain):
    return values * lax.rsqrt(jnp.mean(values * values, axis=-1, keepdims=True) + NORM_EPS) * gain


def layout(seq_row, span_length):
    count = seq_row.shape[0]
    ends = jnp.cumsum(seq_row)
    starts = ends - seq_row
    slots = jnp.arange(span_length, dtype=jnp.int32)
    segment = jnp.sum((slots[:, None] >= ends[None, :]).astype(jnp.int32), axis=1)
    valid = slots < ends[count - 1]
    segment = jnp.where(valid, segment, count + slots)
    match = segment[:, None] == jnp.arange(count, dtype=jnp.int32)[None, :]
    first = jnp.sum(jnp.where(match, starts[None, :], 0), axis=1)
    token_position = jnp.where(valid, slots - first, 0)
    return (segment, token_position, valid)


def apply_rotary(values, token_position):
    half = HEAD_SIZE // 2
    freq = ROPE_BASE ** (-(jnp.arange(half, dtype=jnp.float32) * 2.0 / HEAD_SIZE))
    angle = token_position.astype(jnp.float32)[:, None] * freq[None, :]
    cosine = jnp.cos(angle)[:, None, :]
    sine = jnp.sin(angle)[:, None, :]
    first_half = values[..., :half]
    second_half = values[..., half:]
    return jnp.concatenate(
        [first_half * cosine - second_half * sine, second_half * cosine + first_half * sine],
        axis=-1,
    )


def block_forward(block_tokens, weights, head_params, segment, token_position, low, low_back):
    w_in, w_out, w_up, w_down, gain_all, kernel = weights
    span_length = block_tokens.shape[0]
    normed = low(normalize(block_tokens, gain_all[:D]))
    projected_input = low_back(jnp.dot(normed, w_in, precision=None))
    key_offset = QUERY_HEADS * HEAD_SIZE
    value_offset = key_offset + KEY_VALUE_HEADS * HEAD_SIZE
    gate_offset = value_offset + KEY_VALUE_HEADS * HEAD_SIZE
    offset_c = gate_offset + MH * MP
    offset_t = offset_c + MH * MP + 2 * NS
    query_matrix = projected_input[:, :key_offset].reshape(span_length, QUERY_HEADS, HEAD_SIZE)
    key_matrix = projected_input[:, key_offset:value_offset].reshape(
        span_length, KEY_VALUE_HEADS, HEAD_SIZE
    )
    value_matrix = low(
        projected_input[:, value_offset:gate_offset].reshape(
            span_length, KEY_VALUE_HEADS, HEAD_SIZE
        )
    )
    query_matrix = low(apply_rotary(query_matrix, token_position)).reshape(
        span_length, KEY_VALUE_HEADS, QUERY_HEADS // KEY_VALUE_HEADS, HEAD_SIZE
    )
    key_matrix = low(apply_rotary(key_matrix, token_position))
    slots = jnp.arange(span_length, dtype=jnp.int32)
    allowed = (segment[:, None] == segment[None, :]) & (slots[None, :] <= slots[:, None])
    scores = jnp.einsum("tagd,sad->agts", query_matrix, key_matrix, precision=None) * HEAD_SIZE ** (
        -0.5
    )
    scores = low_back(scores)
    scores = jnp.where(allowed[None, None], scores, -1000000000.0)
    probs = low(jax.nn.softmax(scores, axis=-1))
    context = low_back(jnp.einsum("agts,sad->tagd", probs, value_matrix, precision=None))
    context = low(context.reshape(span_length, QUERY_HEADS * HEAD_SIZE))
    gate_z = projected_input[:, gate_offset:offset_c]
    conv_in = projected_input[:, offset_c:offset_t]
    step_raw = projected_input[:, offset_t:]
    width = conv_in.shape[1]
    summed = jnp.zeros_like(conv_in) + kernel[KC][None, :]
    for lag in range(KC):
        shifted = jnp.concatenate(
            [jnp.zeros((lag, width), jnp.float32), conv_in[: span_length - lag]], axis=0
        )
        earlier = jnp.concatenate(
            [jnp.full((lag,), -1, jnp.int32), segment[: span_length - lag]], axis=0
        )
        keep = earlier == segment
        summed = summed + kernel[KC - 1 - lag][None, :] * jnp.where(keep[:, None], shifted, 0.0)
    conv_out = jax.nn.silu(summed)
    scan_x = low(conv_out[:, : MH * MP]).reshape(span_length, MH, MP)
    scan_b = low(conv_out[:, MH * MP : MH * MP + NS])
    scan_c = low(conv_out[:, MH * MP + NS :])
    step_size = jax.nn.softplus(step_raw + head_params[0][None, :])
    cumulative = jnp.cumsum(-step_size * jnp.exp(head_params[1])[None, :], axis=0)
    intersection = low_back(jnp.dot(scan_c, scan_b.T, precision=None))
    cum_heads = cumulative.T
    spread = cum_heads[:, :, None] - cum_heads[:, None, :]
    decay_matrix = jnp.exp(jnp.where(allowed[None], spread, -10000.0))
    mixing = low(intersection[None] * decay_matrix * step_size.T[:, None, :])
    scan_out = low_back(jnp.einsum("hts,shp->thp", mixing, scan_x, precision=None))
    scan_out = scan_out + head_params[2][None, :, None] * scan_x
    gated = scan_out.reshape(span_length, MH * MP) * jax.nn.silu(gate_z)
    mamba_out = low(normalize(gated, gain_all[2 * D :]))
    joined = jnp.concatenate([context, mamba_out], axis=1)
    hidden = block_tokens + low_back(jnp.dot(joined, w_out, precision=None))
    normed_ff = low(normalize(hidden, gain_all[D : 2 * D]))
    gate_up = low_back(jnp.dot(normed_ff, w_up, precision=None))
    activated = low(jax.nn.silu(gate_up[:, :FF]) * gate_up[:, FF:])
    return hidden + low_back(jnp.dot(activated, w_down, precision=None))


def adamw(weight, mean, square, grad, rate):
    mean_new = BETA_MEAN * mean + (1.0 - BETA_MEAN) * grad
    square_new = BETA_SQUARE * square + (1.0 - BETA_SQUARE) * grad * grad
    corrected = (
        mean_new
        / (1.0 - BETA_MEAN**STEP)
        / (jnp.sqrt(square_new / (1.0 - BETA_SQUARE**STEP)) + ADAM_EPS)
    )
    return (weight - rate * (corrected + DECAY * weight), mean_new, square_new)


def on_device(
    tokens,
    cotangent,
    seq_lengths,
    mixer_in,
    mixer_in_mean,
    mixer_in_square,
    mixer_out,
    mixer_out_mean,
    mixer_out_square,
    swiglu_in,
    swiglu_in_mean,
    swiglu_in_square,
    swiglu_out,
    swiglu_out_mean,
    swiglu_out_square,
    gains,
    gains_mean,
    gains_square,
    conv_kernel,
    conv_kernel_mean,
    conv_kernel_square,
    head_params,
    head_params_mean,
    head_params_square,
):
    value_rounder, grad_rounder = make_rounders()
    gathered = (
        lax.all_gather(mixer_in.astype(jnp.bfloat16), "shard", axis=0, tiled=True),
        lax.all_gather(mixer_out.astype(jnp.bfloat16), "shard", axis=0, tiled=True),
        lax.all_gather(swiglu_in.astype(jnp.bfloat16), "shard", axis=0, tiled=True),
        lax.all_gather(swiglu_out.astype(jnp.bfloat16), "shard", axis=0, tiled=True),
        lax.all_gather(gains.astype(jnp.bfloat16), "shard", axis=0, tiled=True),
        lax.all_gather(conv_kernel.astype(jnp.bfloat16), "shard", axis=1, tiled=True),
    )
    weights = tuple((piece.astype(jnp.float32) for piece in gathered))
    segment, token_position, valid = layout(seq_lengths[0], tokens.shape[0])
    cot_rows = cotangent.astype(jnp.float32) * valid[:, None].astype(jnp.float32)

    def forward(values, weight_set, params):
        return block_forward(
            values, weight_set, params, segment, token_position, value_rounder, grad_rounder
        )

    output, pull = jax.vjp(forward, tokens.astype(jnp.float32), weights, head_params)
    token_grad, weight_grads, param_grad = pull(cot_rows)
    partial_sums = (
        lax.psum_scatter(weight_grads[0], "shard", scatter_dimension=0, tiled=True),
        lax.psum_scatter(weight_grads[1], "shard", scatter_dimension=0, tiled=True),
        lax.psum_scatter(weight_grads[2], "shard", scatter_dimension=0, tiled=True),
        lax.psum_scatter(weight_grads[3], "shard", scatter_dimension=0, tiled=True),
        lax.psum_scatter(weight_grads[4], "shard", scatter_dimension=0, tiled=True),
        lax.psum_scatter(weight_grads[5], "shard", scatter_dimension=1, tiled=True),
    )
    owned = lax.psum(
        (
            partial_sums[0],
            partial_sums[1],
            partial_sums[2],
            partial_sums[3],
            partial_sums[4],
            partial_sums[5],
        ),
        "rep",
    )
    head_grad = lax.psum(param_grad, ("rep", "shard"))
    masters = (mixer_in, mixer_out, swiglu_in, swiglu_out, gains, conv_kernel)
    means = (
        mixer_in_mean,
        mixer_out_mean,
        swiglu_in_mean,
        swiglu_out_mean,
        gains_mean,
        conv_kernel_mean,
    )
    squares = (
        mixer_in_square,
        mixer_out_square,
        swiglu_in_square,
        swiglu_out_square,
        gains_square,
        conv_kernel_square,
    )
    rates = (MATRIX_RATE, MATRIX_RATE, MATRIX_RATE, MATRIX_RATE, VECTOR_RATE, VECTOR_RATE)
    updated = [
        adamw(masters[index], means[index], squares[index], owned[index], rates[index])
        for index in range(6)
    ]
    head_new = adamw(head_params, head_params_mean, head_params_square, head_grad, VECTOR_RATE)
    return (
        output.astype(jnp.bfloat16),
        token_grad,
        updated[0][0],
        updated[0][1],
        updated[0][2],
        updated[1][0],
        updated[1][1],
        updated[1][2],
        updated[2][0],
        updated[2][1],
        updated[2][2],
        updated[3][0],
        updated[3][1],
        updated[3][2],
        updated[4][0],
        updated[4][1],
        updated[4][2],
        updated[5][0],
        updated[5][1],
        updated[5][2],
        head_new[0],
        head_new[1],
        head_new[2],
    )


def solution(mesh):
    return jax.shard_map(
        on_device,
        mesh=mesh,
        in_specs=(
            P(("rep", "shard"), None),
            P(("rep", "shard"), None),
            P(("rep", "shard"), None),
            P("shard", None),
            P("shard", None),
            P("shard", None),
            P("shard", None),
            P("shard", None),
            P("shard", None),
            P("shard", None),
            P("shard", None),
            P("shard", None),
            P("shard", None),
            P("shard", None),
            P("shard", None),
            P("shard"),
            P("shard"),
            P("shard"),
            P(None, "shard"),
            P(None, "shard"),
            P(None, "shard"),
            P(),
            P(),
            P(),
        ),
        out_specs=(
            P(("rep", "shard"), None),
            P(("rep", "shard"), None),
            P("shard", None),
            P("shard", None),
            P("shard", None),
            P("shard", None),
            P("shard", None),
            P("shard", None),
            P("shard", None),
            P("shard", None),
            P("shard", None),
            P("shard", None),
            P("shard", None),
            P("shard", None),
            P("shard"),
            P("shard"),
            P("shard"),
            P(None, "shard"),
            P(None, "shard"),
            P(None, "shard"),
            P(),
            P(),
            P(),
        ),
        check_vma=False,
    )
```

profile of v0, /device:TPU:1, one launch (start us, length us, event | category | flops | bytes accessed | tf_op | source)
XLA Modules:
  0.0 1581.6 jit_solution(9917525899148609855)
XLA Ops:
  16.9 19.7 %all-reduce.34 = bf16[3584]{0:T(1024)(128)(2,1)S(1)} all-reduce(bf16[3584]{0:T(1024)(128)(2,1)S(1)} %dynamic-update-slice), channel_id=1, replica_groups=mesh['rep'=4,'shard'=8] {'shard'}, use_global_device_ids=true, to_apply=%add.34 | all-reduce | flops 3584 | bytes 14336
  41.4 24.2 %all-gather = bf16[8,224,5]{1,2,0:T(8,128)(2,1)S(1)} all-gather(bf16[1,224,5]{1,2,0:T(8,128)(2,1)S(1)} %convert_bitcast_fusion), channel_id=1, replica_groups=mesh['rep'=4,'shard'=8] {'shard'}, dimensions={0}, use_global_device_ids=true | all-gather | bytes 20160 | tf_op jit(solution)/shard_map/all_gather | solution.py:202
  70.4 69.4 %all-gather.6.cloned.1.call-done = bf16[1024,4120]{0,1:T(8,128)(2,1)} async-done(((bf16[128,4120]{0,1:T(8,128)(2,1)}), bf16[1024,4120]{0,1:T(8,128)(2,1)}) %all-gather.6.cloned.1.call-update) | async-done | bytes 8437776 | tf_op jit(solution)/shard_map/all_gather | solution.py:197
  180.5 8.6 multiply_convert_fusion
  189.2 8.5 bitcast_add_fusion.1
  204.4 8.8 all-gather.8.cloned.1.call-done
  221.3 118.8 %all-gather.10.cloned.1.call-done = bf16[1024,4096]{1,0:T(8,128)(2,1)} async-done(((bf16[128,4096]{1,0:T(8,128)(2,1)}), bf16[1024,4096]{1,0:T(8,128)(2,1)}) %all-gather.10.cloned.1.call-update) | async-done | bytes 8388624 | tf_op jit(solution)/shard_map/all_gather | solution.py:199
  340.1 11.4 fusion.108
  351.5 61.9 %all-gather.12.cloned.1.call-done = bf16[2048,1024]{1,0:T(8,128)(2,1)} async-done(((bf16[256,1024]{1,0:T(8,128)(2,1)}), bf16[2048,1024]{1,0:T(8,128)(2,1)}) %all-gather.12.cloned.1.call-update) | async-done | bytes 4194320 | tf_op jit(solution)/shard_map/all_gather | solution.py:200
  413.5 11.5 fusion.51
  428.1 9.4 multiply_reduce_fusion.11
  453.9 12.9 fusion.112
  495.3 18.3 %fusion.3 = (f32[24,512]{1,0:T(8,128)S(1)}, f32[24,512]{1,0:T(8,128)S(1)}, f32[24,512]{1,0:T(8,128)S(1)}, bf16[512,512]{1,0:T(8,128)(2,1)S(1)}) fusion(f32[24,512]{1,0:T(8,128)S(1)} %copy-done.71, f32[24,512]{1,0:T(8,128)S(1)} %copy-done.69, f32[512,512]{1,0:T(8,128)S(1)} %copy-done.35, pred[512,512]{1,0:T(8,128)(4,1)S(1)} %copy-done.60, ...), kind=kOutput, calls=%fused_computation.8 | convolution fusion | flops 886796288 | bytes 5226496 | tf_op jit(solution)/shard_map/transpose(jvp(hts,shp->thp))/dot_general | solution.py:146
  541.8 8.3 multiply_reduce_fusion.6
  559.2 8.4 fusion.111
  569.9 24.9 %reduce-scatter.10.cloned.1.call-done = f32[256,1024]{1,0:T(8,128)} async-done(((f32[2048,1024]{1,0:T(8,128)}), f32[256,1024]{1,0:T(8,128)}) %reduce-scatter.10.cloned.1.call-update) | async-done | bytes 1048592 | tf_op jit(solution)/shard_map/reduce_scatter | solution.py:217
  594.8 152.0 %reduce-scatter.14.cloned.1.call-done = f32[256,1024]{1,0:T(8,128)} async-done(((f32[2048,1024]{1,0:T(8,128)}), f32[256,1024]{1,0:T(8,128)}) %reduce-scatter.14.cloned.1.call-update) | async-done | bytes 1048592 | tf_op jit(solution)/shard_map/reduce_scatter | solution.py:219
  746.7 285.5 %reduce-scatter.12.cloned.1.call-done = f32[128,4096]{1,0:T(8,128)} async-done(((f32[1024,4096]{1,0:T(8,128)}), f32[128,4096]{1,0:T(8,128)}) %reduce-scatter.12.cloned.1.call-update) | async-done | bytes 2097168 | tf_op jit(solution)/shard_map/reduce_scatter | solution.py:218
  1032.3 333.1 %reduce-scatter.8.cloned.1.call-done = f32[128,4120]{0,1:T(8,128)} async-done(((f32[1024,4120]{0,1:T(8,128)}), f32[128,4120]{0,1:T(8,128)}) %reduce-scatter.8.cloned.1.call-update) | async-done | bytes 2109456 | tf_op jit(solution)/shard_map/reduce_scatter | solution.py:216
  1365.5 11.1 fusion.29
  1376.6 30.7 %all-reduce.35 = f32[3584]{0:T(1024)S(1)} all-reduce(f32[3584]{0:T(1024)S(1)} %pad_add_fusion.3), channel_id=6, replica_groups=mesh['rep'=4,'shard'=8] {'shard'}, use_global_device_ids=true, to_apply=%region_31.32.clone | all-reduce | flops 3584 | bytes 28672
  1407.5 44.5 %psum.55 = f32[3,24]{1,0:T(4,128)S(1)} all-reduce(f32[3,24]{1,0:T(4,128)S(1)} %pad_add_fusion.4), channel_id=1, replica_groups=mesh['rep'=4,'shard'=8] {'rep','shard'}, use_global_device_ids=true, to_apply=%region_44.45 | all-reduce | flops 72 | bytes 576 | tf_op jit(solution)/shard_map/psum | solution.py:234
  1463.0 11.7 all-reduce.36
  1476.0 81.9 %all-reduce.40.cloned.1.call-done = (f32[128,4120]{0,1:T(8,128)}, f32[256,1024]{1,0:T(8,128)}, f32[128,4096]{1,0:T(8,128)}, f32[256,1024]{1,0:T(8,128)}) async-done(((f32[128,4120]{0,1:T(8,128)}, f32[256,1024]{1,0:T(8,128)}, f32[128,4096]{1,0:T(8,128)}, f32[256,1024]{1,0:T(8,128)}), (f32[128,4120]{0,1:T(8,128)}, f32[256,1024]{1,0:T(8,128)}, f32[128,4096]{1,0:T(8,128)}, ...) | async-done | bytes 6303760 | tf_op jit(solution)/shard_map/psum | solution.py:223
  (429 shorter events, 188.8 us)
Async XLA Ops:
  7.2 132.6 %all-gather.6.cloned.1.call-start = ((), (), s32[]{:S(2)}) async-start(), calls=%async_computation.5 | async-start | bytes 9492480 | tf_op jit(solution)/shard_map/all_gather | solution.py:197
  10.1 203.1 %all-gather.8.cloned.1.call-start = ((), (), s32[]{:S(2)}) async-start(), calls=%async_computation.6 | async-start | bytes 4718592 | tf_op jit(solution)/shard_map/all_gather | solution.py:198
  11.1 329.0 %all-gather.10.cloned.1.call-start = ((), (), s32[]{:S(2)}) async-start(), calls=%async_computation.7 | async-start | bytes 9437184 | tf_op jit(solution)/shard_map/all_gather | solution.py:199
  12.3 401.2 %all-gather.12.cloned.1.call-start = ((), (), s32[]{:S(2)}) async-start(), calls=%async_computation.8 | async-start | bytes 4718592 | tf_op jit(solution)/shard_map/all_gather | solution.py:200
  14.5 580.3 %reduce-scatter.10.cloned.1.call-start = ((), (), s32[]{:S(2)}) async-start(), calls=%async_computation.10 | async-start | bytes 9437184 | tf_op jit(solution)/shard_map/reduce_scatter | solution.py:217
  38.6 108.3 %copy-start.101 = (f32[512]{0:T(512)}, f32[512]{0:T(512)S(1)}, u32[]{:S(2)}) copy-start(f32[512]{0:T(512)S(1)} %fusion.73) | copy-start | bytes 6148
  41.4 105.6 %copy-start.57 = (bf16[512,1024]{1,0:T(8,128)(2,1)}, bf16[512,1024]{1,0:T(8,128)(2,1)S(1)}, u32[]{:S(2)}) copy-start(bf16[512,1024]{1,0:T(8,128)(2,1)S(1)} %fusion.28) | copy-start | bytes 3145732
  69.6 85.3 %copy-start.41 = (f32[512,32]{0,1:T(8,128)}, f32[512,32]{0,1:T(8,128)S(1)}, u32[]{:S(2)}) copy-start(f32[512,32]{0,1:T(8,128)S(1)} %get-tuple-element.100) | copy-start | bytes 196612
  70.4 94.8 %copy-start.117 = (pred[512]{0:T(512)(128)(4,1)}, pred[512]{0:T(512)(128)(4,1)S(1)}, u32[]{:S(2)}) copy-start(pred[512]{0:T(512)(128)(4,1)S(1)} %get-tuple-element.105) | copy-start | bytes 1540
  70.4 94.8 %copy-start.119 = (pred[512]{0:T(512)(128)(4,1)}, pred[512]{0:T(512)(128)(4,1)S(1)}, u32[]{:S(2)}) copy-start(pred[512]{0:T(512)(128)(4,1)S(1)} %get-tuple-element.106) | copy-start | bytes 1540
  70.4 94.8 %copy-start.121 = (pred[512]{0:T(512)(128)(4,1)}, pred[512]{0:T(512)(128)(4,1)S(1)}, u32[]{:S(2)}) copy-start(pred[512]{0:T(512)(128)(4,1)S(1)} %get-tuple-element.107) | copy-start | bytes 1540
  446.0 300.7 %reduce-scatter.14.cloned.1.call-start = ((), (), s32[]{:S(2)}) async-start(), calls=%async_computation.12 | async-start | bytes 9437184 | tf_op jit(solution)/shard_map/reduce_scatter | solution.py:219
  453.8 578.4 %reduce-scatter.12.cloned.1.call-start = ((), (), s32[]{:S(2)}) async-start(), calls=%async_computation.11 | async-start | bytes 18874368 | tf_op jit(solution)/shard_map/reduce_scatter | solution.py:218
  466.8 898.6 %reduce-scatter.8.cloned.1.call-start = ((), (), s32[]{:S(2)}) async-start(), calls=%async_computation.9 | async-start | bytes 18984960 | tf_op jit(solution)/shard_map/reduce_scatter | solution.py:216
  567.6 894.5 %reduce-scatter.16.cloned.1.call-start = ((), (), s32[]{:S(2)}) async-start(), calls=%async_computation.13 | async-start | bytes 1032192
  569.0 796.4 %copy-start.20 = (bf16[512,1024]{1,0:T(8,128)(2,1)S(1)}, bf16[512,1024]{1,0:T(8,128)(2,1)}, u32[]{:S(2)}) copy-start(bf16[512,1024]{1,0:T(8,128)(2,1)} %param.24) | copy-start | bytes 3145732
  569.0 796.4 %copy-start.83 = (f32[1024]{0:T(1024)S(1)}, f32[1024]{0:T(1024)}, u32[]{:S(2)}) copy-start(f32[1024]{0:T(1024)} %copy-done.82) | copy-start | bytes 12292
  569.0 796.4 %copy-start.96 = (f32[512]{0:T(512)S(1)}, f32[512]{0:T(512)}, u32[]{:S(2)}) copy-start(f32[512]{0:T(512)} %copy-done.95) | copy-start | bytes 6148
  569.0 988.8 %all-reduce.40.cloned.1.call-start = ((), (), s32[]{:S(2)}) async-start(), calls=%async_computation.14 | async-start | bytes 12607488 | tf_op jit(solution)/shard_map/psum | solution.py:223
  1365.4 86.5 %copy-start.98 = (f32[512]{0:T(512)S(1)}, f32[512]{0:T(512)}, u32[]{:S(2)}) copy-start(f32[512]{0:T(512)} %copy-done.97) | copy-start | bytes 6148
  1365.4 86.5 %copy-start.124 = (f32[3,24]{1,0:T(4,128)S(1)}, f32[3,24]{1,0:T(4,128)}, u32[]{:S(2)}) copy-start(f32[3,24]{1,0:T(4,128)} %param.46) | copy-start | bytes 868
  1365.5 86.5 %copy-start.125 = (f32[3,24]{1,0:T(4,128)S(1)}, f32[3,24]{1,0:T(4,128)}, u32[]{:S(2)}) copy-start(f32[3,24]{1,0:T(4,128)} %param.47) | copy-start | bytes 868
  1365.5 87.1 %copy-start.27 = (f32[512,1024]{1,0:T(8,128)S(1)}, f32[512,1024]{1,0:T(8,128)}, u32[]{:S(2)}) copy-start(f32[512,1024]{1,0:T(8,128)} %get-tuple-element.76) | copy-start | bytes 6291460
  1457.0 100.9 %copy-start.21 = (f32[128,4120]{0,1:T(8,128)S(1)}, f32[128,4120]{0,1:T(8,128)}, u32[]{:S(2)}) copy-start(f32[128,4120]{0,1:T(8,128)} %param.27) | copy-start | bytes 6328324
  (125 other events, 1036.5 us)
Sparse Core Ops, SparseCore 0:
  10.7 129.1 all-gather.5
  142.5 70.6 all-gather.7
  216.0 124.0 all-gather.9
  342.6 70.7 all-gather.11
  446.2 148.5 reduce-scatter.9
  598.7 148.0 reduce-scatter.13
  750.5 281.6 reduce-scatter.11
  1036.2 329.0 reduce-scatter.7
  1369.6 63.5 reduce-scatter.15
  1435.7 122.0 all-reduce.39
where the time goes:
time: 1590 us; the launch traced here: 1580 us
  waiting for transfers between devices  1140 us (72%)
  matrix products  148 us (9%)
  blocking collectives  131 us (8%)
  other arithmetic  104 us (7%)
  local copies, waits for them, and re-layouts  43.6 us (3%)
  between operations  17.4 us (1%)
    reduce_scatter x1, waiting for transfers between devices, on_device(): lax.psum_scatter(weight_grads[0], 'shard', scatter_dimension=0, tiled=True)  333 us
    reduce_scatter x1, waiting for transfers between devices, on_device(): lax.psum_scatter(weight_grads[2], 'shard', scatter_dimension=0, tiled=True)  286 us
    reduce_scatter x1, waiting for transfers between devices, on_device(): lax.psum_scatter(weight_grads[3], 'shard', scatter_dimension=0, tiled=True)  152 us
    all_gather x1, waiting for transfers between devices, on_device(): lax.all_gather(swiglu_in.astype(jnp.bfloat16), 'shard', axis=0, tiled=True)  119 us
    psum x1, waiting for transfers between devices, on_device(): lax.psum((partial_sums[0], partial_sums[1], partial_sums[2], partial_sums...  81.9 us
    all_gather x1, waiting for transfers between devices, on_device(): lax.all_gather(mixer_in.astype(jnp.bfloat16), 'shard', axis=0, tiled=True)  69.4 us
    all_gather x1, waiting for transfers between devices, on_device(): lax.all_gather(swiglu_out.astype(jnp.bfloat16), 'shard', axis=0, tiled=True)  61.9 us
    unnamed x2, blocking collectives  50.5 us
  transfers between devices with their start and end apart: 10, of which 9 were waited for; matrix products, arithmetic and copies ran while one was open for 15% of the time, Pallas kernels for 0%

commit v1 on v0

--- a/solution.py
+++ b/solution.py
@@ -164,6 +164,54 @@
         / (jnp.sqrt(square_new / (1.0 - BETA_SQUARE**STEP)) + ADAM_EPS)
     )
     return (weight - rate * (corrected + DECAY * weight), mean_new, square_new)
+
+
+BOTH = ("shard", "rep")
+
+
+def gather_matrices(masters):
+    copies = lax.axis_size("rep")
+    copy = lax.axis_index("rep")
+    pieces = []
+    for master in masters:
+        rows = master.shape[0] // copies
+        own = lax.dynamic_slice_in_dim(master, copy * rows, rows, 0).astype(jnp.bfloat16)
+        pieces.append(lax.all_gather(own, BOTH, axis=0, tiled=True))
+    return tuple(pieces)
+
+
+def gather_vectors(gains, conv_kernel):
+    owners = lax.axis_size("shard")
+    width = conv_kernel.shape[1]
+    own = jnp.concatenate([gains, conv_kernel.reshape(-1)]).astype(jnp.bfloat16)
+    every = lax.all_gather(own, "shard", axis=0, tiled=False)
+    gains_all = every[:, : gains.shape[0]].reshape(-1)
+    taps = every[:, gains.shape[0] :].reshape(owners, KC + 1, width)
+    return (gains_all, jnp.swapaxes(taps, 0, 1).reshape(KC + 1, owners * width))
+
+
+def reduce_matrices(grads):
+    results = []
+    for grad in grads:
+        piece = lax.psum_scatter(
+            grad.astype(jnp.bfloat16), BOTH, scatter_dimension=0, tiled=True
+        )
+        results.append(lax.all_gather(piece, "rep", axis=0, tiled=True).astype(jnp.float32))
+    return tuple(results)
+
+
+def reduce_vectors(gains_grad, conv_grad, head_grad):
+    owners = lax.axis_size("shard")
+    owner = lax.axis_index("shard")
+    count, taps = gains_grad.shape[0], conv_grad.size
+    flat = jnp.concatenate([gains_grad, conv_grad.reshape(-1), head_grad.reshape(-1)])
+    total = lax.psum(flat, ("rep", "shard"))
+    own_gains = lax.dynamic_slice_in_dim(total[:count], owner * (count // owners), count // owners)
+    width = conv_grad.shape[1] // owners
+    own_taps = lax.dynamic_slice_in_dim(
+        total[count : count + taps].reshape(conv_grad.shape), owner * width, width, 1
+    )
+    return ((own_gains, own_taps), total[count + taps :].reshape(head_grad.shape))
 
 
 def on_device(
@@ -193,14 +241,8 @@
     head_params_square,
 ):
     value_rounder, grad_rounder = make_rounders()
-    gathered = (
-        lax.all_gather(mixer_in.astype(jnp.bfloat16), "shard", axis=0, tiled=True),
-        lax.all_gather(mixer_out.astype(jnp.bfloat16), "shard", axis=0, tiled=True),
-        lax.all_gather(swiglu_in.astype(jnp.bfloat16), "shard", axis=0, tiled=True),
-        lax.all_gather(swiglu_out.astype(jnp.bfloat16), "shard", axis=0, tiled=True),
-        lax.all_gather(gains.astype(jnp.bfloat16), "shard", axis=0, tiled=True),
-        lax.all_gather(conv_kernel.astype(jnp.bfloat16), "shard", axis=1, tiled=True),
-    )
+    gathered = gather_matrices((mixer_in, mixer_out, swiglu_in, swiglu_out))
+    gathered = gathered + gather_vectors(gains, conv_kernel)
     weights = tuple((piece.astype(jnp.float32) for piece in gathered))
     segment, token_position, valid = layout(seq_lengths[0], tokens.shape[0])
     cot_rows = cotangent.astype(jnp.float32) * valid[:, None].astype(jnp.float32)
@@ -212,26 +254,9 @@
 
     output, pull = jax.vjp(forward, tokens.astype(jnp.float32), weights, head_params)
     token_grad, weight_grads, param_grad = pull(cot_rows)
-    partial_sums = (
-        lax.psum_scatter(weight_grads[0], "shard", scatter_dimension=0, tiled=True),
-        lax.psum_scatter(weight_grads[1], "shard", scatter_dimension=0, tiled=True),
-        lax.psum_scatter(weight_grads[2], "shard", scatter_dimension=0, tiled=True),
-        lax.psum_scatter(weight_grads[3], "shard", scatter_dimension=0, tiled=True),
-        lax.psum_scatter(weight_grads[4], "shard", scatter_dimension=0, tiled=True),
-        lax.psum_scatter(weight_grads[5], "shard", scatter_dimension=1, tiled=True),
-    )
-    owned = lax.psum(
-        (
-            partial_sums[0],
-            partial_sums[1],
-            partial_sums[2],
-            partial_sums[3],
-            partial_sums[4],
-            partial_sums[5],
-        ),
-        "rep",
-    )
-    head_grad = lax.psum(param_grad, ("rep", "shard"))
+    owned = reduce_matrices(weight_grads[:4])
+    vector_grads, head_grad = reduce_vectors(weight_grads[4], weight_grads[5], param_grad)
+    owned = owned + vector_grads
     masters = (mixer_in, mixer_out, swiglu_in, swiglu_out, gains, conv_kernel)
     means = (
         mixer_in_mean,

time: 1590 us -> 1040 us (0.65)
  waiting for transfers between devices: 1140 us -> 611 us
  blocking collectives: 131 us -> 92.9 us
  local copies, waits for them, and re-layouts: 43.6 us -> 62.9 us
    reduce_scatter x4, waiting for transfers between devices: 795 us -> 428 us  [reduce_matrices(): lax.psum_scatter(grad.astype(jnp.bfloat16), BOTH, scatter_dimension=0, ti...]
    psum x1 -> x0, waiting for transfers between devices: 81.9 us -> none  [on_device(): lax.psum((partial_sums[0], partial_sums[1], partial_sums[2], partial_sums...]
    all_gather x4 -> x6, waiting for transfers between devices: 259 us -> 182 us  [the longest x4 162 us: gather_matrices(): pieces.append(lax.all_gather(own, BOTH, axis=0, tiled=True))]
    unnamed x2 -> x0, blocking collectives: 50.5 us -> none
    all_gather x1 -> x3, blocking collectives: 24.2 us -> 51 us  [the longest x1 25.7 us: gather_vectors(): every = lax.all_gather(own, 'shard', axis=0, tiled=False)]
    psum x2 -> x1, blocking collectives: 56.1 us -> 41.9 us  [reduce_vectors(): total = lax.psum(flat, ('rep', 'shard'))]
    unnamed x285 -> x260, local copies, waits for them, and re-layouts: 24.7 us -> 37.8 us
  transfers between devices with their start and end apart: 10 -> 10, of which waited for: 9 -> 10; matrix products, arithmetic and copies ran while one was open for 15% -> 16% of each run, Pallas kernels for 0% -> 0%
where the time goes in v1:
time: 1040 us; the launch traced here: 1030 us
  waiting for transfers between devices  611 us (59%)
  matrix products  143 us (14%)
  other arithmetic  106 us (10%)
  blocking collectives  92.9 us (9%)
  local copies, waits for them, and re-layouts  62.9 us (6%)
  between operations  16.3 us (2%)
    reduce_scatter x4, waiting for transfers between devices, reduce_matrices(): lax.psum_scatter(grad.astype(jnp.bfloat16), BOTH, scatter_dimension=0, ti...  428 us
    all_gather x4, waiting for transfers between devices, gather_matrices(): pieces.append(lax.all_gather(own, BOTH, axis=0, tiled=True))  162 us
    psum x1, blocking collectives, reduce_vectors(): total = lax.psum(flat, ('rep', 'shard'))  41.9 us
    unnamed x260, local copies, waits for them, and re-layouts  37.8 us
    dot_general x3, matrix products, block_forward(): gate_up = low_back(jnp.dot(normed_ff, w_up, precision=None))  30.1 us
    dot_general x3, matrix products, block_forward(): jnp.einsum('hts,shp->thp', mixing, scan_x, precision=None)  29 us
    dot_general x3, matrix products, block_forward(): projected_input = low_back(jnp.dot(normed, w_in, precision=None))  26.1 us
    all_gather x1, blocking collectives, gather_vectors(): every = lax.all_gather(own, 'shard', axis=0, tiled=False)  25.7 us
  transfers between devices with their start and end apart: 10, of which 10 were waited for; matrix products, arithmetic and copies ran while one was open for 16% of the time, Pallas kernels for 0%

profile of v1, /device:TPU:1, one launch (start us, length us, event | category | flops | bytes accessed | tf_op | source)
XLA Modules:
  0.0 1031.5 jit_solution(9674410639322554160)
XLA Ops:
  16.7 25.7 %all-gather = bf16[8,1,1568]{2,1,0:T(2,128)(2,1)S(1)} all-gather(bf16[1,1,1568]{2,1,0:T(2,128)(2,1)S(1)} %maximum_bitcast_fusion), channel_id=1, replica_groups=mesh['rep'=4,'shard'=8] {'shard'}, dimensions={0}, use_global_device_ids=true | all-gather | bytes 28224 | tf_op jit(solution)/shard_map/all_gather | solution.py:187
  54.4 38.1 %all-gather.8.cloned.1.call-done = bf16[1024,4120]{1,0:T(8,128)(2,1)} async-done(((bf16[32,4120]{1,0:T(8,128)(2,1)}), bf16[1024,4120]{1,0:T(8,128)(2,1)}) %all-gather.8.cloned.1.call-update) | async-done | bytes 8437776 | tf_op jit(solution)/shard_map/all_gather | solution.py:179
  92.5 7.4 fusion.112
  122.0 7.4 multiply_convert_fusion.2
  132.4 8.3 multiply_convert_fusion
  140.8 8.5 bitcast_add_fusion.1
  164.7 71.4 %all-gather.12.cloned.1.call-done = bf16[1024,4096]{1,0:T(8,128)(2,1)} async-done(((bf16[32,4096]{1,0:T(8,128)(2,1)}), bf16[1024,4096]{1,0:T(8,128)(2,1)}) %all-gather.12.cloned.1.call-update) | async-done | bytes 8388624 | tf_op jit(solution)/shard_map/all_gather | solution.py:179
  236.1 11.5 %fusion.114 = f32[512,4096]{1,0:T(8,128)} fusion(bf16[512,1024]{1,0:T(8,128)(2,1)} %multiply_convert_fusion.4, bf16[1024,4096]{1,0:T(8,128)(2,1)} %all-gather.12.cloned.1.call-done), kind=kOutput, calls=%fused_computation.243 | convolution fusion | flops 4294967296 | bytes 17825792 | tf_op jit(solution)/shard_map/jvp()/dot_general | solution.py:153
  247.6 52.4 %all-gather.14.cloned.1.call-done = bf16[2048,1024]{1,0:T(8,128)(2,1)} async-done(((bf16[64,1024]{1,0:T(8,128)(2,1)}), bf16[2048,1024]{1,0:T(8,128)(2,1)}) %all-gather.14.cloned.1.call-update) | async-done | bytes 4194320 | tf_op jit(solution)/shard_map/all_gather | solution.py:179
  300.0 11.6 %fusion.54 = (f32[512,2048]{1,0:T(8,128)S(1)}, f32[512,2048]{1,0:T(8,128)}, bf16[512,2048]{1,0:T(8,128)(2,1)}) fusion(f32[512,4096]{1,0:T(8,128)} %fusion.114, bf16[512,1024]{1,0:T(8,128)(2,1)} %fusion.35, bf16[2048,1024]{1,0:T(8,128)(2,1)} %all-gather.14.cloned.1.call-done), kind=kOutput, calls=%fused_computation.135 | convolution fusion | flops 2162163712 | bytes 24117248 | tf_op jit(solution)/shard_map/transpose(jvp())/dot_general | solution.py:155
  314.7 9.4 multiply_reduce_fusion.11
  348.9 18.4 %fusion.3 = (f32[24,512]{1,0:T(8,128)}, f32[24,512]{1,0:T(8,128)}, f32[24,512]{1,0:T(8,128)}, bf16[512,512]{1,0:T(8,128)(2,1)S(1)}) fusion(f32[24,512]{1,0:T(8,128)S(1)} %copy-done.55, f32[24,512]{1,0:T(8,128)S(1)} %copy-done.52, f32[512,512]{1,0:T(8,128)S(1)} %copy-done.25, pred[512,512]{1,0:T(8,128)(4,1)S(1)} %copy-done.42, ...), kind=kOutput, calls=%fused_computation.8 | convolution fusion | flops 886796288 | bytes 5226496 | tf_op jit(solution)/shard_map/transpose(jvp(hts,shp->thp))/dot_general | solution.py:146
  397.7 9.6 multiply_reduce_fusion.6
  417.2 7.1 convolution_convert_fusion
  438.4 9.3 convolution_convert_fusion.1
  455.2 11.6 %fusion.30 = (f32[1024]{0:T(1024)S(1)}, f32[512]{0:T(512)S(1)}, f32[512,1024]{1,0:T(8,128)}) fusion(bf16[512,1024]{1,0:T(8,128)(2,1)S(1)} %copy-done.14, f32[512]{0:T(512)S(1)} %copy-done.83, f32[1024]{0:T(1024)S(1)} %copy-done.71, bf16[512,4120]{0,1:T(8,128)(2,1)} %copy-done.20, bf16[1024,4120]{1,0:T(8,128)(2,1)} %all-gather.8.cloned.1.call-done), kind=kOutput, calls=%fused_computation.89 | convolution fusion | flops 4323801600 | bytes 15814656 | tf_op jit(solution)/shard_map/transpose(jvp())/dot_general | solution.py:92
  466.9 41.9 %psum.7 = f32[12616]{0:T(1024)S(1)} all-reduce(f32[12616]{0:T(1024)S(1)} %pad_maximum_fusion.5), channel_id=1, replica_groups=mesh['rep'=4,'shard'=8] {'rep','shard'}, use_global_device_ids=true, to_apply=%region_36.37 | all-reduce | flops 12616 | bytes 100928 | tf_op jit(solution)/shard_map/psum | solution.py:208
  514.5 39.6 %reduce-scatter.5.cloned.1.call-done = bf16[32,4120]{1,0:T(8,128)(2,1)} async-done(((bf16[1024,4120]{1,0:T(8,128)(2,1)}), bf16[32,4120]{1,0:T(8,128)(2,1)}) %reduce-scatter.5.cloned.1.call-update) | async-done | bytes 263696 | tf_op jit(solution)/shard_map/reduce_scatter | solution.py:196
  561.0 131.9 %reduce-scatter.7.cloned.1.call-done = bf16[64,1024]{1,0:T(8,128)(2,1)} async-done(((bf16[2048,1024]{1,0:T(8,128)(2,1)}), bf16[64,1024]{1,0:T(8,128)(2,1)}) %reduce-scatter.7.cloned.1.call-update) | async-done | bytes 131088 | tf_op jit(solution)/shard_map/reduce_scatter | solution.py:196
  692.9 12.7 %all_gather.34 = bf16[256,1024]{1,0:T(8,128)(2,1)S(1)} all-gather(bf16[64,1024]{1,0:T(8,128)(2,1)} %reduce-scatter.7.cloned.1.call-done), channel_id=1, replica_groups=mesh['rep'=4,'shard'=8] {'rep'}, dimensions={0}, use_global_device_ids=true | all-gather | bytes 655360 | tf_op jit(solution)/shard_map/all_gather | solution.py:199
  705.6 126.4 %reduce-scatter.11.cloned.1.call-done = bf16[64,1024]{1,0:T(8,128)(2,1)} async-done(((bf16[2048,1024]{1,0:T(8,128)(2,1)}), bf16[64,1024]{1,0:T(8,128)(2,1)}) %reduce-scatter.11.cloned.1.call-update) | async-done | bytes 131088 | tf_op jit(solution)/shard_map/reduce_scatter | solution.py:196
  832.0 12.6 %all_gather.36 = bf16[256,1024]{1,0:T(8,128)(2,1)S(1)} all-gather(bf16[64,1024]{1,0:T(8,128)(2,1)} %reduce-scatter.11.cloned.1.call-done), channel_id=1, replica_groups=mesh['rep'=4,'shard'=8] {'rep'}, dimensions={0}, use_global_device_ids=true | all-gather | bytes 655360 | tf_op jit(solution)/shard_map/all_gather | solution.py:199
  848.8 130.0 %reduce-scatter.9.cloned.1.call-done = bf16[32,4096]{1,0:T(8,128)(2,1)} async-done(((bf16[1024,4096]{1,0:T(8,128)(2,1)}), bf16[32,4096]{1,0:T(8,128)(2,1)}) %reduce-scatter.9.cloned.1.call-update) | async-done | bytes 262160 | tf_op jit(solution)/shard_map/reduce_scatter | solution.py:196
  982.9 16.2 %all-gather.16.cloned.1.call-done = bf16[128,4120]{1,0:T(8,128)(2,1)} async-done(((bf16[32,4120]{1,0:T(8,128)(2,1)}), bf16[128,4120]{1,0:T(8,128)(2,1)}) %all-gather.16.cloned.1.call-update) | async-done | bytes 1054736 | tf_op jit(solution)/shard_map/all_gather | solution.py:199
  (422 shorter events, 196.1 us)
Async XLA Ops:
  7.2 85.2 %all-gather.8.cloned.1.call-start = ((), (), s32[]{:S(2)}) async-start(), calls=%async_computation.4 | async-start | bytes 8921088 | tf_op jit(solution)/shard_map/all_gather | solution.py:179
  10.4 146.2 %all-gather.10.cloned.1.call-start = ((), (), s32[]{:S(2)}) async-start(), calls=%async_computation.5 | async-start | bytes 4325376 | tf_op jit(solution)/shard_map/all_gather | solution.py:179
  12.1 223.9 %all-gather.12.cloned.1.call-start = ((), (), s32[]{:S(2)}) async-start(), calls=%async_computation.6 | async-start | bytes 8650752 | tf_op jit(solution)/shard_map/all_gather | solution.py:179
  14.0 286.0 %all-gather.14.cloned.1.call-start = ((), (), s32[]{:S(2)}) async-start(), calls=%async_computation.7 | async-start | bytes 4325376 | tf_op jit(solution)/shard_map/all_gather | solution.py:179
  15.7 538.4 %reduce-scatter.5.cloned.1.call-start = ((), (), s32[]{:S(2)}) async-start(), calls=%async_computation.8 | async-start | bytes 8921088 | tf_op jit(solution)/shard_map/reduce_scatter | solution.py:196
  48.1 71.6 %copy-start.58 = (f32[1792]{0:T(1024)}, f32[1792]{0:T(1024)S(1)}, u32[]{:S(2)}) copy-start(f32[1792]{0:T(1024)S(1)} %mul.814) | copy-start | bytes 21508
  48.2 71.6 %copy-start.60 = (f32[1792]{0:T(1024)}, f32[1792]{0:T(1024)S(1)}, u32[]{:S(2)}) copy-start(f32[1792]{0:T(1024)S(1)} %mul.817) | copy-start | bytes 21508
  48.3 71.5 %copy-start.64 = (f32[1792]{0:T(1024)}, f32[1792]{0:T(1024)S(1)}, u32[]{:S(2)}) copy-start(f32[1792]{0:T(1024)S(1)} %mul.820) | copy-start | bytes 21508
  48.3 71.4 %copy-start.62 = (f32[1792]{0:T(1024)}, f32[1792]{0:T(1024)S(1)}, u32[]{:S(2)}) copy-start(f32[1792]{0:T(1024)S(1)} %mul.823) | copy-start | bytes 21508
  48.4 81.2 %copy-start.100 = (f32[24]{0:T(128)}, f32[24]{0:T(128)S(1)}, u32[]{:S(2)}) copy-start(f32[24]{0:T(128)S(1)} %get-tuple-element.189) | copy-start | bytes 292
  48.5 81.2 %copy-start.102 = (f32[24]{0:T(128)}, f32[24]{0:T(128)S(1)}, u32[]{:S(2)}) copy-start(f32[24]{0:T(128)S(1)} %get-tuple-element.190) | copy-start | bytes 292
  48.5 92.3 %copy-start.80 = (f32[24]{0:T(128)}, f32[24]{0:T(128)S(1)}, u32[]{:S(2)}) copy-start(f32[24]{0:T(128)S(1)} %get-tuple-element.188) | copy-start | bytes 292
  48.9 83.5 %copy-start.41 = (pred[512,512]{1,0:T(8,128)(4,1)}, pred[512,512]{1,0:T(8,128)(4,1)S(1)}, u32[]{:S(2)}) copy-start(pred[512,512]{1,0:T(8,128)(4,1)S(1)} %copy.96) | copy-start | bytes 786436
  52.1 67.6 %copy-start.104 = (pred[512]{0:T(512)(128)(4,1)}, pred[512]{0:T(512)(128)(4,1)S(1)}, u32[]{:S(2)}) copy-start(pred[512]{0:T(512)(128)(4,1)S(1)} %get-tuple-element.191) | copy-start | bytes 1540
  52.1 67.6 %copy-start.106 = (pred[512]{0:T(512)(128)(4,1)}, pred[512]{0:T(512)(128)(4,1)S(1)}, u32[]{:S(2)}) copy-start(pred[512]{0:T(512)(128)(4,1)S(1)} %get-tuple-element.192) | copy-start | bytes 1540
  52.1 67.6 %copy-start.108 = (pred[512]{0:T(512)(128)(4,1)}, pred[512]{0:T(512)(128)(4,1)S(1)}, u32[]{:S(2)}) copy-start(pred[512]{0:T(512)(128)(4,1)S(1)} %get-tuple-element.193) | copy-start | bytes 1540
  424.4 268.5 %reduce-scatter.7.cloned.1.call-start = ((), (), s32[]{:S(2)}) async-start(), calls=%async_computation.10 | async-start | bytes 4325376 | tf_op jit(solution)/shard_map/reduce_scatter | solution.py:196
  430.6 401.4 %reduce-scatter.11.cloned.1.call-start = ((), (), s32[]{:S(2)}) async-start(), calls=%async_computation.13 | async-start | bytes 4325376 | tf_op jit(solution)/shard_map/reduce_scatter | solution.py:196
  437.1 541.7 %reduce-scatter.9.cloned.1.call-start = ((), (), s32[]{:S(2)}) async-start(), calls=%async_computation.11 | async-start | bytes 8650752 | tf_op jit(solution)/shard_map/reduce_scatter | solution.py:196
  447.7 551.5 %all-gather.16.cloned.1.call-start = ((), (), s32[]{:S(2)}) async-start(), calls=%async_computation.9 | async-start | bytes 1351680 | tf_op jit(solution)/shard_map/all_gather | solution.py:199
  455.2 54.3 %copy-start.79 = (f32[5,224]{1,0:T(8,128)S(1)}, f32[5,224]{1,0:T(8,128)}, u32[]{:S(2)}) copy-start(f32[5,224]{1,0:T(8,128)} %param.42) | copy-start | bytes 13444
  455.2 54.3 %copy-start.92 = (f32[5,224]{1,0:T(8,128)S(1)}, f32[5,224]{1,0:T(8,128)}, u32[]{:S(2)}) copy-start(f32[5,224]{1,0:T(8,128)} %param.43) | copy-start | bytes 13444
  554.1 463.2 %all-gather.18.cloned.1.call-start = ((), (), s32[]{:S(2)}) async-start(), calls=%async_computation.12 | async-start | bytes 1310720 | tf_op jit(solution)/shard_map/all_gather | solution.py:199
  848.8 150.3 %copy-start.12 = (f32[128,4120]{1,0:T(8,128)S(1)}, f32[128,4120]{1,0:T(8,128)}, u32[]{:S(2)}) copy-start(f32[128,4120]{1,0:T(8,128)} %copy-done.11) | copy-start | bytes 6328324
  (112 other events, 1207.4 us)
Sparse Core Ops, SparseCore 0:
  11.5 80.8 all-gather.7
  95.9 60.6 all-gather.9
  160.0 75.9 all-gather.11
  239.4 60.6 all-gather.13
  424.5 129.4 reduce-scatter.4
  556.2 136.6 reduce-scatter.6
  695.2 136.8 reduce-scatter.10
  834.3 144.3 reduce-scatter.8
  980.3 18.7 all-gather.15
  1000.5 16.7 all-gather.17

commit v2 on v0

--- a/solution.py
+++ b/solution.py
@@ -1,6 +1,8 @@
 import jax
 import jax.numpy as jnp
 from jax import lax
+from jax.experimental import pallas as pl
+from jax.experimental.pallas import tpu as pltpu
 from jax.sharding import PartitionSpec as P
 
 D = 1024
@@ -86,21 +88,20 @@
 
 
 def block_forward(block_tokens, weights, head_params, segment, token_position, low, low_back):
-    w_in, w_out, w_up, w_down, gain_all, kernel = weights
+    w_conv, w_qkv, w_gate, w_out, w_up, w_down, gain_all, kernel = weights
     span_length = block_tokens.shape[0]
     normed = low(normalize(block_tokens, gain_all[:D]))
-    projected_input = low_back(jnp.dot(normed, w_in, precision=None))
+    projected_qkv = low_back(jnp.dot(normed, w_qkv, precision=None))
+    projected_conv = low_back(jnp.dot(normed, w_conv, precision=None))
     key_offset = QUERY_HEADS * HEAD_SIZE
     value_offset = key_offset + KEY_VALUE_HEADS * HEAD_SIZE
-    gate_offset = value_offset + KEY_VALUE_HEADS * HEAD_SIZE
-    offset_c = gate_offset + MH * MP
-    offset_t = offset_c + MH * MP + 2 * NS
-    query_matrix = projected_input[:, :key_offset].reshape(span_length, QUERY_HEADS, HEAD_SIZE)
-    key_matrix = projected_input[:, key_offset:value_offset].reshape(
+    conv_width = MH * MP + 2 * NS
+    query_matrix = projected_qkv[:, :key_offset].reshape(span_length, QUERY_HEADS, HEAD_SIZE)
+    key_matrix = projected_qkv[:, key_offset:value_offset].reshape(
         span_length, KEY_VALUE_HEADS, HEAD_SIZE
     )
     value_matrix = low(
-        projected_input[:, value_offset:gate_offset].reshape(
+        projected_qkv[:, value_offset:].reshape(
             span_length, KEY_VALUE_HEADS, HEAD_SIZE
         )
     )
@@ -118,9 +119,9 @@
     probs = low(jax.nn.softmax(scores, axis=-1))
     context = low_back(jnp.einsum("agts,sad->tagd", probs, value_matrix, precision=None))
     context = low(context.reshape(span_length, QUERY_HEADS * HEAD_SIZE))
-    gate_z = projected_input[:, gate_offset:offset_c]
-    conv_in = projected_input[:, offset_c:offset_t]
-    step_raw = projected_input[:, offset_t:]
+    gate_z = low_back(jnp.dot(normed, w_gate, precision=None))
+    conv_in = projected_conv[:, :conv_width]
+    step_raw = projected_conv[:, conv_width : conv_width + MH]
     width = conv_in.shape[1]
     summed = jnp.zeros_like(conv_in) + kernel[KC][None, :]
     for lag in range(KC):
@@ -166,6 +167,218 @@
     return (weight - rate * (corrected + DECAY * weight), mean_new, square_new)
 
 
+QKV = (QUERY_HEADS + 2 * KEY_VALUE_HEADS) * HEAD_SIZE
+GATE = MH * MP
+CONV = MH * MP + 2 * NS
+STEP_LANES = 128
+BOTH = ("shard", "rep")
+ALL = ("rep", "shard")
+
+
+def general_gather(own):
+    copies = lax.axis_size("rep")
+    rows = own.shape[0] // copies
+    part = lax.dynamic_slice_in_dim(own, lax.axis_index("rep") * rows, rows, 0)
+    return lax.all_gather(part, BOTH, axis=0, tiled=True)
+
+
+def general_reduce(grad):
+    piece = lax.psum_scatter(grad, BOTH, scatter_dimension=0, tiled=True)
+    return lax.all_gather(piece, "rep", axis=0, tiled=True)
+
+
+def place():
+    rep, shard = lax.axis_index("rep"), lax.axis_index("shard")
+    return (rep // 2, rep % 2, shard // 2, shard % 2)
+
+
+def send(values, dx=0, dcore=0, dz=0, dy=0):
+    pairs = []
+    for x in range(2):
+        for core in range(2):
+            for z in range(4):
+                for y in range(2):
+                    start = (x * 2 + core) * 8 + z * 2 + y
+                    end = ((x ^ dx) * 2 + (core ^ dcore)) * 8 + ((z + dz) % 4) * 2 + (y ^ dy)
+                    pairs.append((start, end))
+    return lax.ppermute(values, ALL, pairs)
+
+
+def pick(values, index, axis):
+    return lax.dynamic_index_in_dim(values, index, axis, keepdims=False)
+
+
+def assemble(held, rows):
+    quarter = rows // 8
+    columns = held[0].shape[-1]
+
+    def kernel(*refs):
+        sources, target, sems = refs[:8], refs[8], refs[9]
+        rep, shard = lax.axis_index("rep"), lax.axis_index("shard")
+        x, core, z, y = rep // 2, rep % 2, shard // 2, shard % 2
+        copies = []
+        for other_core in range(2):
+            half = core if other_core == 0 else 1 - core
+            for other_y in range(2):
+                row = y if other_y == 0 else 1 - y
+                for turn in range(4):
+                    owner = ((z + 4 - turn) % 4) * 2 + row
+                    base = owner * rows + half * (rows // 2)
+                    main = sources[other_core * 4 + other_y].at[turn]
+                    cross = sources[other_core * 4 + 2 + other_y].at[turn]
+                    for piece, start, count in (
+                        (main.at[pl.ds(0, quarter)], base + x * quarter, quarter),
+                        (main.at[pl.ds(quarter, 2 * quarter)], base + 2 * quarter, 2 * quarter),
+                        (cross, base + (1 - x) * quarter, quarter),
+                    ):
+                        place_at = pl.ds(pl.multiple_of(start, 16), count)
+                        copies.append(
+                            pltpu.make_async_copy(piece, target.at[place_at], sems.at[len(copies)])
+                        )
+        for copy in copies:
+            copy.start()
+        for copy in copies:
+            copy.wait()
+
+    return pl.pallas_call(
+        kernel,
+        out_shape=jax.ShapeDtypeStruct((8 * rows, columns), jnp.bfloat16),
+        in_specs=[pl.BlockSpec(memory_space=pl.ANY)] * 8,
+        out_specs=pl.BlockSpec(memory_space=pl.ANY),
+        scratch_shapes=[pltpu.SemaphoreType.DMA((48,))],
+        name="assemble",
+    )(*held)
+
+
+def tuned_gather(own):
+    rows = own.shape[0]
+    quarter = rows // 8
+    x, core, z, y = place()
+    half = lax.dynamic_slice_in_dim(own, core * (rows // 2), rows // 2, 0)
+    mine = jnp.concatenate(
+        [lax.dynamic_slice_in_dim(half, x * quarter, quarter, 0), half[2 * quarter :]], axis=0
+    )
+    along_z = jnp.stack([mine] + [send(mine, dz=turn) for turn in range(1, 4)])
+    across_y = send(along_z, dy=1)
+    held = [along_z, across_y]
+    held += [send(group[:, :quarter], dx=1) for group in held]
+    held += [send(group, dcore=1) for group in held]
+    return assemble(held, rows)
+
+
+def add_low(left, right):
+    return (left.astype(jnp.float32) + right.astype(jnp.float32)).astype(jnp.bfloat16)
+
+
+def tuned_reduce(grad):
+    rows, columns = grad.shape[0] // 8, grad.shape[1]
+    quarter = rows // 8
+    x, core, z, y = place()
+    parts = grad.reshape(4, 2, 2, rows // 2, columns)
+    half = add_low(pick(parts, core, 2), send(pick(parts, 1 - core, 2), dcore=1))
+    far = lax.dynamic_slice_in_dim(half, (1 - x) * quarter, quarter, 2)
+    near = add_low(lax.dynamic_slice_in_dim(half, x * quarter, quarter, 2), send(far, dx=1))
+    both = half[:, :, 2 * quarter :]
+    there = jnp.concatenate([pick(near, 1 - y, 1), pick(both, 1 - y, 1)], axis=1)
+    here = jnp.concatenate([pick(near, y, 1), pick(both, y, 1)], axis=1)
+    column = add_low(here, send(there, dy=1))
+    total = pick(column, z, 0).astype(jnp.float32)
+    for turn in range(1, 4):
+        total = total + send(pick(column, (z + turn) % 4, 0), dz=turn).astype(jnp.float32)
+    total = total.astype(jnp.bfloat16)
+    across = send(total, dx=1)
+    own_x, other_x = total[:quarter], across[:quarter]
+    owned = jnp.concatenate(
+        [
+            jnp.where(x == 0, own_x, other_x),
+            jnp.where(x == 0, other_x, own_x),
+            add_low(total[quarter:], across[quarter:]),
+        ],
+        axis=0,
+    )
+    beside = send(owned, dcore=1)
+    return jnp.concatenate(
+        [jnp.where(core == 0, owned, beside), jnp.where(core == 0, beside, owned)], axis=0
+    )
+
+
+def tuned():
+    return lax.axis_size("rep") == 4 and lax.axis_size("shard") == 8
+
+
+def gather_weights(mixer_in, mixer_out, swiglu_in, swiglu_out, gains, conv_kernel):
+    gather = tuned_gather if tuned() else general_gather
+    rows = mixer_in.shape[0]
+    owners = lax.axis_size("shard")
+    width = conv_kernel.shape[1]
+    count = gains.shape[0] + conv_kernel.size
+    lanes = -(-count // rows)
+    vector = jnp.concatenate([gains, conv_kernel.reshape(-1)])
+    vector = jnp.pad(vector, (0, lanes * rows - count)).reshape(rows, lanes)
+    low_in = mixer_in.astype(jnp.bfloat16)
+    tail = STEP_LANES - MH - lanes
+    conv_piece = jnp.concatenate(
+        [low_in[:, QKV + GATE :], vector.astype(jnp.bfloat16), jnp.zeros((rows, tail), jnp.bfloat16)],
+        axis=1,
+    )
+    w_conv = gather(conv_piece)
+    w_qkv = gather(low_in[:, :QKV])
+    w_gate = gather(low_in[:, QKV : QKV + GATE])
+    w_out = gather(mixer_out.astype(jnp.bfloat16))
+    w_up = gather(swiglu_in.astype(jnp.bfloat16))
+    w_down = gather(swiglu_out.astype(jnp.bfloat16))
+    every = w_conv[:, CONV + MH : CONV + MH + lanes].reshape(owners, rows * lanes)
+    gains_all = every[:, : gains.shape[0]].reshape(-1)
+    taps = every[:, gains.shape[0] : count].reshape(owners, KC + 1, width)
+    taps = jnp.swapaxes(taps, 0, 1).reshape(KC + 1, owners * width)
+    return (w_conv, w_qkv, w_gate, w_out, w_up, w_down, gains_all, taps)
+
+
+def reduce_grads(grads, head_grad):
+    reduce = tuned_reduce if tuned() else general_reduce
+    owners = lax.axis_size("shard")
+    conv_g, qkv_g, gate_g, out_g, up_g, down_g, gains_g, taps_g = grads
+    down = reduce(down_g.astype(jnp.bfloat16))
+    up = reduce(up_g.astype(jnp.bfloat16))
+    out = reduce(out_g.astype(jnp.bfloat16))
+    gate = reduce(gate_g.astype(jnp.bfloat16))
+    qkv = reduce(qkv_g.astype(jnp.bfloat16))
+    rows = conv_g.shape[0] // owners
+    width = taps_g.shape[1] // owners
+    vector = jnp.concatenate(
+        [
+            gains_g.reshape(owners, -1),
+            jnp.swapaxes(taps_g.reshape(KC + 1, owners, width), 0, 1).reshape(owners, -1),
+            jnp.broadcast_to(head_grad.reshape(1, -1), (owners, head_grad.size)),
+        ],
+        axis=1,
+    )
+    count = vector.shape[1]
+    lanes = -(-count // rows)
+    vector = jnp.pad(vector, ((0, 0), (0, lanes * rows - count))).reshape(owners * rows, lanes)
+    used = CONV + MH
+    conv_g = jnp.concatenate(
+        [conv_g[:, :used], vector, jnp.zeros((owners * rows, STEP_LANES - MH - lanes), jnp.float32)],
+        axis=1,
+    )
+    conv = reduce(conv_g.astype(jnp.bfloat16))
+    flat = conv[:, used : used + lanes].astype(jnp.float32).reshape(-1)
+    own_gains = gains_g.shape[0] // owners
+    own_taps = (KC + 1) * width
+    matrix = jnp.concatenate([qkv, gate, conv[:, :used]], axis=1)
+    return (
+        (
+            matrix.astype(jnp.float32),
+            out.astype(jnp.float32),
+            up.astype(jnp.float32),
+            down.astype(jnp.float32),
+            flat[:own_gains],
+            flat[own_gains : own_gains + own_taps].reshape(KC + 1, width),
+        ),
+        flat[own_gains + own_taps : count].reshape(head_grad.shape),
+    )
+
+
 def on_device(
     tokens,
     cotangent,
@@ -193,14 +406,7 @@
     head_params_square,
 ):
     value_rounder, grad_rounder = make_rounders()
-    gathered = (
-        lax.all_gather(mixer_in.astype(jnp.bfloat16), "shard", axis=0, tiled=True),
-        lax.all_gather(mixer_out.astype(jnp.bfloat16), "shard", axis=0, tiled=True),
-        lax.all_gather(swiglu_in.astype(jnp.bfloat16), "shard", axis=0, tiled=True),
-        lax.all_gather(swiglu_out.astype(jnp.bfloat16), "shard", axis=0, tiled=True),
-        lax.all_gather(gains.astype(jnp.bfloat16), "shard", axis=0, tiled=True),
-        lax.all_gather(conv_kernel.astype(jnp.bfloat16), "shard", axis=1, tiled=True),
-    )
+    gathered = gather_weights(mixer_in, mixer_out, swiglu_in, swiglu_out, gains, conv_kernel)
     weights = tuple((piece.astype(jnp.float32) for piece in gathered))
     segment, token_position, valid = layout(seq_lengths[0], tokens.shape[0])
     cot_rows = cotangent.astype(jnp.float32) * valid[:, None].astype(jnp.float32)
@@ -212,26 +418,7 @@
 
     output, pull = jax.vjp(forward, tokens.astype(jnp.float32), weights, head_params)
     token_grad, weight_grads, param_grad = pull(cot_rows)
-    partial_sums = (
-        lax.psum_scatter(weight_grads[0], "shard", scatter_dimension=0, tiled=True),
-        lax.psum_scatter(weight_grads[1], "shard", scatter_dimension=0, tiled=True),
-        lax.psum_scatter(weight_grads[2], "shard", scatter_dimension=0, tiled=True),
-        lax.psum_scatter(weight_grads[3], "shard", scatter_dimension=0, tiled=True),
-        lax.psum_scatter(weight_grads[4], "shard", scatter_dimension=0, tiled=True),
-        lax.psum_scatter(weight_grads[5], "shard", scatter_dimension=1, tiled=True),
-    )
-    owned = lax.psum(
-        (
-            partial_sums[0],
-            partial_sums[1],
-            partial_sums[2],
-            partial_sums[3],
-            partial_sums[4],
-            partial_sums[5],
-        ),
-        "rep",
-    )
-    head_grad = lax.psum(param_grad, ("rep", "shard"))
+    owned, head_grad = reduce_grads(weight_grads, param_grad)
     masters = (mixer_in, mixer_out, swiglu_in, swiglu_out, gains, conv_kernel)
     means = (
         mixer_in_mean,

time: 1590 us -> 1540 us (0.969)
  waiting for transfers between devices: 1140 us -> 230 us
  Pallas kernels: 0 us -> 780 us
  starting transfers between devices: 0.63 us -> 139 us
  blocking collectives: 131 us -> 0 us
  local copies, waits for them, and re-layouts: 43.6 us -> 112 us
  other arithmetic: 104 us -> 127 us
  matrix products: 148 us -> 132 us
    reduce_scatter x4 -> x0, waiting for transfers between devices: 795 us -> none  [the longest x1 333 us: on_device(): lax.psum_scatter(weight_grads[0], 'shard', scatter_dimension=0, tiled=True)]
    pallas_call x0 -> x6, Pallas kernels: none -> 780 us  [assemble(): pl.pallas_call(kernel, out_shape=jax.ShapeDtypeStruct((8 * rows, columns)...]
    all_gather x4 -> x0, waiting for transfers between devices: 259 us -> none  [the longest x1 119 us: on_device(): lax.all_gather(swiglu_in.astype(jnp.bfloat16), 'shard', axis=0, tiled=True)]
    ppermute x0 -> x108, waiting for transfers between devices: none -> 230 us  [send(): return lax.ppermute(values, ALL, pairs)]
    ppermute x0 -> x108, starting transfers between devices: none -> 139 us  [send(): return lax.ppermute(values, ALL, pairs)]
    psum x1 -> x0, waiting for transfers between devices: 81.9 us -> none  [on_device(): lax.psum((partial_sums[0], partial_sums[1], partial_sums[2], partial_sums...]
    psum x2 -> x0, blocking collectives: 56.1 us -> none  [the longest x1 44.5 us: on_device(): head_grad = lax.psum(param_grad, ('rep', 'shard'))]
    unnamed x2 -> x0, blocking collectives: 50.5 us -> none
  transfers between devices with their start and end apart: 10 -> 108, of which waited for: 9 -> 35; matrix products, arithmetic and copies ran while one was open for 15% -> 12% of each run, Pallas kernels for 0% -> 34%
where the time goes in v2:
time: 1540 us; the launch traced here: 1520 us
  Pallas kernels  780 us (51%)
  waiting for transfers between devices  230 us (15%)
  starting transfers between devices  139 us (9%)
  matrix products  132 us (9%)
  other arithmetic  127 us (8%)
  local copies, waits for them, and re-layouts  112 us (7%)
    pallas_call x6, Pallas kernels, assemble(): pl.pallas_call(kernel, out_shape=jax.ShapeDtypeStruct((8 * rows, columns)...  780 us
    ppermute x108, waiting for transfers between devices, send(): return lax.ppermute(values, ALL, pairs)  230 us
    ppermute x108, starting transfers between devices, send(): return lax.ppermute(values, ALL, pairs)  139 us
    unnamed x396, local copies, waits for them, and re-layouts  36.2 us
  transfers between devices with their start and end apart: 108, of which 35 were waited for; matrix products, arithmetic and copies ran while one was open for 12% of the time, Pallas kernels for 34%

profile of v2, /device:TPU:1, one launch (start us, length us, event | category | flops | bytes accessed | tf_op | source)
XLA Modules:
  0.0 1524.1 jit_solution(7089841719473690271)
XLA Ops:
  39.8 9.0 collective-permute-done.1
  55.1 10.3 collective-permute-done.31
  74.4 16.3 %collective-permute-done.51 = bf16[96,1024]{1,0:T(8,128)(2,1)S(1)} collective-permute-done((bf16[96,1024]{1,0:T(8,128)(2,1)S(1)}, bf16[96,1024]{1,0:T(8,128)(2,1)S(1)}, u32[]{:S(2)}, u32[]{:S(2)}) %collective-permute-start.51) | collective-permute-done | bytes 196640 | tf_op jit(solution)/shard_map/ppermute | solution.py:204
  138.3 10.0 collective-permute-done.33.refs_1_
  174.5 49.2 %assemble.7 = bf16[1024,768]{1,0:T(8,128)(2,1)} custom-call(bf16[4,48,768]{2,1,0:T(8,128)(2,1)} %copy-done.54, bf16[4,48,768]{2,1,0:T(8,128)(2,1)} %copy-done.92, bf16[4,16,768]{2,1,0:T(8,128)(2,1)} %copy-done.121, bf16[4,16,768]{2,1,0:T(8,128)(2,1)} %copy-done.122, bf16[4,48,768]{2,1,0:T(8,128)(2,1)} %copy-done.106, bf16[4,48,768]{2,1,0:T(8,128)(2,1)} %copy-done.107, ...), custom_call_target="tpu_custom_call" | custom-call | tf_op jit(solution)/shard_map/assemble/pallas_call | solution.py:243
  227.1 96.8 %assemble.8 = bf16[1024,1536]{1,0:T(8,128)(2,1)} custom-call(bf16[4,48,1536]{2,1,0:T(8,128)(2,1)} %copy-done.41, bf16[4,48,1536]{2,1,0:T(8,128)(2,1)} %collective-permute-done.23.refs_1_, bf16[4,16,1536]{2,1,0:T(8,128)(2,1)} %copy-done.115, bf16[4,16,1536]{2,1,0:T(8,128)(2,1)} %copy-done.117, bf16[4,48,1536]{2,1,0:T(8,128)(2,1)} %copy-done.85, ...), custom_call_target="tpu_custom_call" | custom-call | tf_op jit(solution)/shard_map/assemble/pallas_call | solution.py:243
  325.1 120.7 %assemble.6 = bf16[1024,1920]{1,0:T(8,128)(2,1)} custom-call(bf16[4,48,1920]{2,1,0:T(8,128)(2,1)} %copy-done.40, bf16[4,48,1920]{2,1,0:T(8,128)(2,1)} %collective-permute-done.3.refs_1_, bf16[4,16,1920]{2,1,0:T(8,128)(2,1)} %copy-done.112, bf16[4,16,1920]{2,1,0:T(8,128)(2,1)} %collective-permute-done.5.refs_3_, ...), custom_call_target="tpu_custom_call" | custom-call | tf_op jit(solution)/shard_map/assemble/pallas_call | solution.py:243
  461.0 9.0 multiply_convert_fusion.2
  481.0 8.2 multiply_convert_fusion
  489.2 8.5 bitcast_add_fusion.1
  533.1 128.6 %assemble.9 = bf16[2048,1024]{1,0:T(8,128)(2,1)} custom-call(bf16[4,96,1024]{2,1,0:T(8,128)(2,1)} %pad_maximum_fusion.7.refs_0_, bf16[4,96,1024]{2,1,0:T(8,128)(2,1)} %collective-permute-done.33.refs_1_, bf16[4,32,1024]{2,1,0:T(8,128)(2,1)} %copy-done.109, bf16[4,32,1024]{2,1,0:T(8,128)(2,1)} %collective-permute-done.35.refs_3_, ...), custom_call_target="tpu_custom_call" | custom-call | tf_op jit(solution)/shard_map/assemble/pallas_call | solution.py:243
  679.1 128.6 %assemble.11 = bf16[2048,1024]{1,0:T(8,128)(2,1)} custom-call(bf16[4,96,1024]{2,1,0:T(8,128)(2,1)} %pad_maximum_fusion.8.refs_0_, bf16[4,96,1024]{2,1,0:T(8,128)(2,1)} %collective-permute-done.53.refs_1_, bf16[4,32,1024]{2,1,0:T(8,128)(2,1)} %collective-permute-done.54.refs_2_, bf16[4,32,1024]{2,1,0:T(8,128)(2,1)} %collective-permute-done.55.refs_3_, ...), custom_call_target="tpu_custom_call" | custom-call | tf_op jit(solution)/shard_map/assemble/pallas_call | solution.py:243
  807.8 255.7 %assemble.10 = bf16[1024,4096]{1,0:T(8,128)(2,1)} custom-call(bf16[4,48,4096]{2,1,0:T(8,128)(2,1)} %pad_maximum_fusion.1.refs_0_, bf16[4,48,4096]{2,1,0:T(8,128)(2,1)} %collective-permute-done.43.refs_1_, bf16[4,16,4096]{2,1,0:T(8,128)(2,1)} %collective-permute-done.44.refs_2_, bf16[4,16,4096]{2,1,0:T(8,128)(2,1)} %collective-permute-done.45.refs_3_, ...), custom_call_target="tpu_custom_call" | custom-call | tf_op jit(solution)/shard_map/assemble/pallas_call | solution.py:243
  1063.5 11.7 fusion.150
  1075.2 8.7 fusion.65
  1090.3 7.4 multiply_reduce_fusion.11
  1116.3 18.0 %fusion.3 = (f32[24,512]{1,0:T(8,128)}, f32[24,512]{1,0:T(8,128)}, f32[24,512]{1,0:T(8,128)}, bf16[512,512]{1,0:T(8,128)(2,1)S(1)}) fusion(f32[24,512]{1,0:T(8,128)S(1)} %copy-done.114, f32[24,512]{1,0:T(8,128)S(1)} %copy-done.98, f32[512,512]{1,0:T(8,128)S(1)} %copy-done.39, pred[512,512]{1,0:T(8,128)(4,1)S(1)} %copy-done.73, ...), kind=kOutput, calls=%fused_computation.8 | convolution fusion | flops 886796288 | bytes 5226496 | tf_op jit(solution)/shard_map/transpose(jvp(hts,shp->thp))/dot_general | solution.py:147
  1167.7 9.8 multiply_reduce_fusion.6
  1304.1 7.9 collective-permute-done.101
  1313.3 10.0 collective-permute-done.85
  1344.3 8.0 collective-permute-done.80
  1405.3 23.0 %collective-permute-done.93 = bf16[4,2,16,4096]{3,2,1,0:T(8,128)(2,1)} collective-permute-done((bf16[4,2,16,4096]{3,2,1,0:T(8,128)(2,1)}, bf16[4,2,16,4096]{3,2,1,0:T(8,128)(2,1)}, u32[]{:S(2)}, u32[]{:S(2)}) %collective-permute-start.93) | collective-permute-done | bytes 1048608 | tf_op jit(solution)/shard_map/ppermute | solution.py:204
  1447.1 20.5 %collective-permute-done.94 = bf16[4,48,4096]{2,1,0:T(8,128)(2,1)} collective-permute-done((bf16[4,48,4096]{2,1,0:T(8,128)(2,1)}, bf16[4,48,4096]{2,1,0:T(8,128)(2,1)}, u32[]{:S(2)}, u32[]{:S(2)}) %collective-permute-start.94) | collective-permute-done | bytes 1572896 | tf_op jit(solution)/shard_map/ppermute | solution.py:204
  1484.3 18.6 %collective-permute-done.96 = bf16[48,4096]{1,0:T(8,128)(2,1)S(1)} collective-permute-done((bf16[48,4096]{1,0:T(8,128)(2,1)S(1)}, bf16[48,4096]{1,0:T(8,128)(2,1)S(1)}, u32[]{:S(2)}, u32[]{:S(2)}) %collective-permute-start.96) | collective-permute-done | bytes 393248 | tf_op jit(solution)/shard_map/ppermute | solution.py:204
  (910 shorter events, 525.5 us)
Async XLA Ops:
  48.8 41.9 %collective-permute-start.51 = (bf16[96,1024]{1,0:T(8,128)(2,1)S(1)}, bf16[96,1024]{1,0:T(8,128)(2,1)S(1)}, u32[]{:S(2)}, u32[]{:S(2)}) collective-permute-start(bf16[96,1024]{1,0:T(8,128)(2,1)S(1)} %get-tuple-element.229), channel_id=1, source_target_pairs={{0,4},{1,5},{2,6},{3,7},{4,0},{5,1},{6,2},{7,3},{8,12},{9,13},{10,... | collective-permute-start | bytes 589832 | tf_op jit(solution)/shard_map/ppermute | solution.py:204
  121.3 43.8 %collective-permute-start.53 = (bf16[4,96,1024]{2,1,0:T(8,128)(2,1)}, bf16[4,96,1024]{2,1,0:T(8,128)(2,1)}, u32[]{:S(2)}, u32[]{:S(2)}) collective-permute-start(bf16[4,96,1024]{2,1,0:T(8,128)(2,1)} %pad_maximum_fusion.8.refs_0_), channel_id=1, source_target_pairs={{0,1},{1,0},{2,3},{3,2},{4,5},{5,4},{6,7},{7,6},{8,9},{9,8},{10,11... | collective-permute-start | bytes 2359304 | tf_op jit(solution)/shard_map/ppermute | solution.py:204
  136.2 188.3 %collective-permute-start.6 = (bf16[4,48,1920]{2,1,0:T(8,128)(2,1)S(1)}, bf16[4,48,1920]{2,1,0:T(8,128)(2,1)}, u32[]{:S(2)}, u32[]{:S(2)}) collective-permute-start(bf16[4,48,1920]{2,1,0:T(8,128)(2,1)S(1)} %pad_maximum_fusion.11.refs_0_), channel_id=1, source_target_pairs={{0,8},{1,9},{2,10},{3,11},{4,12},{5,13},{6,14},{7,15},{8,0},{9,1},... | collective-permute-start | bytes 2211848 | tf_op jit(solution)/shard_map/ppermute | solution.py:204
  148.2 176.8 %collective-permute-start.7 = (bf16[4,48,1920]{2,1,0:T(8,128)(2,1)}, bf16[4,48,1920]{2,1,0:T(8,128)(2,1)}, u32[]{:S(2)}, u32[]{:S(2)}) collective-permute-start(bf16[4,48,1920]{2,1,0:T(8,128)(2,1)} %collective-permute-done.3.refs_1_), channel_id=1, source_target_pairs={{0,8},{1,9},{2,10},{3,11},{4,12},{5,13},{6,14},{7,15},{8,0},{9,1},... | collective-permute-start | bytes 2211848 | tf_op jit(solution)/shard_map/ppermute | solution.py:204
  168.6 155.3 %collective-permute-start.54 = (bf16[4,32,1024]{2,1,0:T(8,128)(2,1)}, bf16[4,32,1024]{2,1,0:T(8,128)(2,1)}, u32[]{:S(2)}, u32[]{:S(2)}) collective-permute-start(bf16[4,32,1024]{2,1,0:T(8,128)(2,1)} %slice.440), channel_id=1, source_target_pairs={{0,16},{1,17},{2,18},{3,19},{4,20},{5,21},{6,22},{7,23},{8,24},{9,... | collective-permute-start | bytes 786440 | tf_op jit(solution)/shard_map/ppermute | solution.py:204
  169.8 154.5 %collective-permute-start.8 = (bf16[4,16,1920]{2,1,0:T(8,128)(2,1)}, bf16[4,16,1920]{2,1,0:T(8,128)(2,1)}, u32[]{:S(2)}, u32[]{:S(2)}) collective-permute-start(bf16[4,16,1920]{2,1,0:T(8,128)(2,1)} %copy-done.112), channel_id=1, source_target_pairs={{0,8},{1,9},{2,10},{3,11},{4,12},{5,13},{6,14},{7,15},{8,0},{9,1},... | collective-permute-start | bytes 737288 | tf_op jit(solution)/shard_map/ppermute | solution.py:204
  170.1 154.9 %collective-permute-start.9 = (bf16[4,16,1920]{2,1,0:T(8,128)(2,1)}, bf16[4,16,1920]{2,1,0:T(8,128)(2,1)}, u32[]{:S(2)}, u32[]{:S(2)}) collective-permute-start(bf16[4,16,1920]{2,1,0:T(8,128)(2,1)} %collective-permute-done.5.refs_3_), channel_id=1, source_target_pairs={{0,8},{1,9},{2,10},{3,11},{4,12},{5,13},{6,14},{7,15},{8,0},{9,1},... | collective-permute-start | bytes 737288 | tf_op jit(solution)/shard_map/ppermute | solution.py:204
  323.9 200.1 %collective-permute-start.36 = (bf16[4,96,1024]{2,1,0:T(8,128)(2,1)}, bf16[4,96,1024]{2,1,0:T(8,128)(2,1)}, u32[]{:S(2)}, u32[]{:S(2)}) collective-permute-start(bf16[4,96,1024]{2,1,0:T(8,128)(2,1)} %pad_maximum_fusion.7.refs_0_), channel_id=1, source_target_pairs={{0,8},{1,9},{2,10},{3,11},{4,12},{5,13},{6,14},{7,15},{8,0},{9,1},... | collective-permute-start | bytes 2359304 | tf_op jit(solution)/shard_map/ppermute | solution.py:204
  324.3 201.4 %collective-permute-start.43 = (bf16[4,48,4096]{2,1,0:T(8,128)(2,1)}, bf16[4,48,4096]{2,1,0:T(8,128)(2,1)}, u32[]{:S(2)}, u32[]{:S(2)}) collective-permute-start(bf16[4,48,4096]{2,1,0:T(8,128)(2,1)} %pad_maximum_fusion.1.refs_0_), channel_id=1, source_target_pairs={{0,1},{1,0},{2,3},{3,2},{4,5},{5,4},{6,7},{7,6},{8,9},{9,8},{10,11... | collective-permute-start | bytes 4718600 | tf_op jit(solution)/shard_map/ppermute | solution.py:204
  324.5 194.0 %collective-permute-start.38 = (bf16[4,32,1024]{2,1,0:T(8,128)(2,1)}, bf16[4,32,1024]{2,1,0:T(8,128)(2,1)}, u32[]{:S(2)}, u32[]{:S(2)}) collective-permute-start(bf16[4,32,1024]{2,1,0:T(8,128)(2,1)} %copy-done.109), channel_id=1, source_target_pairs={{0,8},{1,9},{2,10},{3,11},{4,12},{5,13},{6,14},{7,15},{8,0},{9,1},... | collective-permute-start | bytes 786440 | tf_op jit(solution)/shard_map/ppermute | solution.py:204
  325.0 194.3 %collective-permute-start.58 = (bf16[4,32,1024]{2,1,0:T(8,128)(2,1)}, bf16[4,32,1024]{2,1,0:T(8,128)(2,1)}, u32[]{:S(2)}, u32[]{:S(2)}) collective-permute-start(bf16[4,32,1024]{2,1,0:T(8,128)(2,1)} %collective-permute-done.54.refs_2_), channel_id=1, source_target_pairs={{0,8},{1,9},{2,10},{3,11},{4,12},{5,13},{6,14},{7,15},{8,0},{9,1},... | collective-permute-start | bytes 786440 | tf_op jit(solution)/shard_map/ppermute | solution.py:204
  325.1 194.3 %collective-permute-start.35 = (bf16[4,32,1024]{2,1,0:T(8,128)(2,1)}, bf16[4,32,1024]{2,1,0:T(8,128)(2,1)}, u32[]{:S(2)}, u32[]{:S(2)}) collective-permute-start(bf16[4,32,1024]{2,1,0:T(8,128)(2,1)} %slice.434), channel_id=1, source_target_pairs={{0,16},{1,17},{2,18},{3,19},{4,20},{5,21},{6,22},{7,23},{8,24},{9,... | collective-permute-start | bytes 786440 | tf_op jit(solution)/shard_map/ppermute | solution.py:204
  519.3 144.1 %collective-permute-start.56 = (bf16[4,96,1024]{2,1,0:T(8,128)(2,1)}, bf16[4,96,1024]{2,1,0:T(8,128)(2,1)}, u32[]{:S(2)}, u32[]{:S(2)}) collective-permute-start(bf16[4,96,1024]{2,1,0:T(8,128)(2,1)} %pad_maximum_fusion.8.refs_0_), channel_id=1, source_target_pairs={{0,8},{1,9},{2,10},{3,11},{4,12},{5,13},{6,14},{7,15},{8,0},{9,1},... | collective-permute-start | bytes 2359304 | tf_op jit(solution)/shard_map/ppermute | solution.py:204
  524.0 283.8 %collective-permute-start.46 = (bf16[4,48,4096]{2,1,0:T(8,128)(2,1)}, bf16[4,48,4096]{2,1,0:T(8,128)(2,1)}, u32[]{:S(2)}, u32[]{:S(2)}) collective-permute-start(bf16[4,48,4096]{2,1,0:T(8,128)(2,1)} %pad_maximum_fusion.1.refs_0_), channel_id=1, source_target_pairs={{0,8},{1,9},{2,10},{3,11},{4,12},{5,13},{6,14},{7,15},{8,0},{9,1},... | collective-permute-start | bytes 4718600 | tf_op jit(solution)/shard_map/ppermute | solution.py:204
  524.1 138.7 %collective-permute-start.44 = (bf16[4,16,4096]{2,1,0:T(8,128)(2,1)}, bf16[4,16,4096]{2,1,0:T(8,128)(2,1)}, u32[]{:S(2)}, u32[]{:S(2)}) collective-permute-start(bf16[4,16,4096]{2,1,0:T(8,128)(2,1)} %slice.436), channel_id=1, source_target_pairs={{0,16},{1,17},{2,18},{3,19},{4,20},{5,21},{6,22},{7,23},{8,24},{9,... | collective-permute-start | bytes 1572872 | tf_op jit(solution)/shard_map/ppermute | solution.py:204
  525.5 137.3 %collective-permute-start.55 = (bf16[4,32,1024]{2,1,0:T(8,128)(2,1)}, bf16[4,32,1024]{2,1,0:T(8,128)(2,1)}, u32[]{:S(2)}, u32[]{:S(2)}) collective-permute-start(bf16[4,32,1024]{2,1,0:T(8,128)(2,1)} %slice.441), channel_id=1, source_target_pairs={{0,16},{1,17},{2,18},{3,19},{4,20},{5,21},{6,22},{7,23},{8,24},{9,... | collective-permute-start | bytes 786440 | tf_op jit(solution)/shard_map/ppermute | solution.py:204
  525.6 282.1 %collective-permute-start.47 = (bf16[4,48,4096]{2,1,0:T(8,128)(2,1)}, bf16[4,48,4096]{2,1,0:T(8,128)(2,1)}, u32[]{:S(2)}, u32[]{:S(2)}) collective-permute-start(bf16[4,48,4096]{2,1,0:T(8,128)(2,1)} %collective-permute-done.43.refs_1_), channel_id=1, source_target_pairs={{0,8},{1,9},{2,10},{3,11},{4,12},{5,13},{6,14},{7,15},{8,0},{9,1},... | collective-permute-start | bytes 4718600 | tf_op jit(solution)/shard_map/ppermute | solution.py:204
  670.4 137.4 %collective-permute-start.48 = (bf16[4,16,4096]{2,1,0:T(8,128)(2,1)}, bf16[4,16,4096]{2,1,0:T(8,128)(2,1)}, u32[]{:S(2)}, u32[]{:S(2)}) collective-permute-start(bf16[4,16,4096]{2,1,0:T(8,128)(2,1)} %collective-permute-done.44.refs_2_), channel_id=1, source_target_pairs={{0,8},{1,9},{2,10},{3,11},{4,12},{5,13},{6,14},{7,15},{8,0},{9,1},... | collective-permute-start | bytes 1572872 | tf_op jit(solution)/shard_map/ppermute | solution.py:204
  677.0 130.8 %collective-permute-start.49 = (bf16[4,16,4096]{2,1,0:T(8,128)(2,1)}, bf16[4,16,4096]{2,1,0:T(8,128)(2,1)}, u32[]{:S(2)}, u32[]{:S(2)}) collective-permute-start(bf16[4,16,4096]{2,1,0:T(8,128)(2,1)} %collective-permute-done.45.refs_3_), channel_id=1, source_target_pairs={{0,8},{1,9},{2,10},{3,11},{4,12},{5,13},{6,14},{7,15},{8,0},{9,1},... | collective-permute-start | bytes 1572872 | tf_op jit(solution)/shard_map/ppermute | solution.py:204
  1230.3 50.7 %collective-permute-start.76 = (bf16[4,2,64,1920]{3,2,1,0:T(8,128)(2,1)}, bf16[4,2,64,1920]{3,2,1,0:T(8,128)(2,1)}, u32[]{:S(2)}, u32[]{:S(2)}) collective-permute-start(bf16[4,2,64,1920]{3,2,1,0:T(8,128)(2,1)} %dynamic-slice_bitcast_fusion.3), channel_id=1, source_target_pairs={{0,8},{1,9},{2,10},{3,11},{4,12},{5,13},{6,14},{7,15},{8,0},{9,1},... | collective-permute-start | bytes 5898248 | tf_op jit(solution)/shard_map/ppermute | solution.py:204
  1234.4 56.3 %collective-permute-start.100 = (bf16[4,2,128,1024]{3,2,1,0:T(8,128)(2,1)}, bf16[4,2,128,1024]{3,2,1,0:T(8,128)(2,1)S(1)}, u32[]{:S(2)}, u32[]{:S(2)}) collective-permute-start(bf16[4,2,128,1024]{3,2,1,0:T(8,128)(2,1)} %dynamic-slice_bitcast_fusion.1), channel_id=1, source_target_pairs={{0,8},{1,9},{2,10},{3,11},{4,12},{5,13},{6,14},{7,15},{8,0},{9,1},... | collective-permute-start | bytes 6291464 | tf_op jit(solution)/shard_map/ppermute | solution.py:204
  1266.2 130.2 %collective-permute-start.92 = (bf16[4,2,64,4096]{3,2,1,0:T(8,128)(2,1)S(1)}, bf16[4,2,64,4096]{3,2,1,0:T(8,128)(2,1)}, u32[]{:S(2)}, u32[]{:S(2)}) collective-permute-start(bf16[4,2,64,4096]{3,2,1,0:T(8,128)(2,1)S(1)} %dynamic-slice_bitcast_fusion), channel_id=1, source_target_pairs={{0,8},{1,9},{2,10},{3,11},{4,12},{5,13},{6,14},{7,15},{8,0},{9,1},... | collective-permute-start | bytes 12582920 | tf_op jit(solution)/shard_map/ppermute | solution.py:204
  1389.4 114.1 %collective-permute-start.107 = (bf16[128,1024]{1,0:T(8,128)(2,1)}, bf16[128,1024]{1,0:T(8,128)(2,1)}, u32[]{:S(2)}, u32[]{:S(2)}) collective-permute-start(bf16[128,1024]{1,0:T(8,128)(2,1)} %pad_maximum_fusion.23), channel_id=1, source_target_pairs={{0,8},{1,9},{2,10},{3,11},{4,12},{5,13},{6,14},{7,15},{8,0},{9,1},... | collective-permute-start | bytes 786440 | tf_op jit(solution)/shard_map/ppermute | solution.py:204
  1395.0 120.0 %collective-permute-start.91 = (bf16[128,1024]{1,0:T(8,128)(2,1)}, bf16[128,1024]{1,0:T(8,128)(2,1)}, u32[]{:S(2)}, u32[]{:S(2)}) collective-permute-start(bf16[128,1024]{1,0:T(8,128)(2,1)} %pad_maximum_fusion.22), channel_id=1, source_target_pairs={{0,8},{1,9},{2,10},{3,11},{4,12},{5,13},{6,14},{7,15},{8,0},{9,1},... | collective-permute-start | bytes 786440 | tf_op jit(solution)/shard_map/ppermute | solution.py:204
  (280 other events, 6344.9 us)

commit v3 on v2

--- a/solution.py
+++ b/solution.py
@@ -87,23 +87,32 @@
     )
 
 
-def block_forward(block_tokens, weights, head_params, segment, token_position, low, low_back):
-    w_conv, w_qkv, w_gate, w_out, w_up, w_down, gain_all, kernel = weights
-    span_length = block_tokens.shape[0]
-    normed = low(normalize(block_tokens, gain_all[:D]))
-    projected_qkv = low_back(jnp.dot(normed, w_qkv, precision=None))
-    projected_conv = low_back(jnp.dot(normed, w_conv, precision=None))
+def rows_of(matrix):
+    return matrix.astype(jnp.bfloat16)
+
+
+def dot(left, right):
+    return jnp.dot(left, right, preferred_element_type=jnp.float32)
+
+
+def dot_left(left, right):
+    return lax.dot_general(left, right, (((0,), (0,)), ((), ())), preferred_element_type=jnp.float32)
+
+
+def dot_right(left, right):
+    return lax.dot_general(left, right, (((1,), (1,)), ((), ())), preferred_element_type=jnp.float32)
+
+
+def attention(projected, segment, token_position, low, low_back):
+    span_length = projected.shape[0]
     key_offset = QUERY_HEADS * HEAD_SIZE
     value_offset = key_offset + KEY_VALUE_HEADS * HEAD_SIZE
-    conv_width = MH * MP + 2 * NS
-    query_matrix = projected_qkv[:, :key_offset].reshape(span_length, QUERY_HEADS, HEAD_SIZE)
-    key_matrix = projected_qkv[:, key_offset:value_offset].reshape(
+    query_matrix = projected[:, :key_offset].reshape(span_length, QUERY_HEADS, HEAD_SIZE)
+    key_matrix = projected[:, key_offset:value_offset].reshape(
         span_length, KEY_VALUE_HEADS, HEAD_SIZE
     )
     value_matrix = low(
-        projected_qkv[:, value_offset:].reshape(
-            span_length, KEY_VALUE_HEADS, HEAD_SIZE
-        )
+        projected[:, value_offset:].reshape(span_length, KEY_VALUE_HEADS, HEAD_SIZE)
     )
     query_matrix = low(apply_rotary(query_matrix, token_position)).reshape(
         span_length, KEY_VALUE_HEADS, QUERY_HEADS // KEY_VALUE_HEADS, HEAD_SIZE
@@ -118,15 +127,19 @@
     scores = jnp.where(allowed[None, None], scores, -1000000000.0)
     probs = low(jax.nn.softmax(scores, axis=-1))
     context = low_back(jnp.einsum("agts,sad->tagd", probs, value_matrix, precision=None))
-    context = low(context.reshape(span_length, QUERY_HEADS * HEAD_SIZE))
-    gate_z = low_back(jnp.dot(normed, w_gate, precision=None))
-    conv_in = projected_conv[:, :conv_width]
-    step_raw = projected_conv[:, conv_width : conv_width + MH]
-    width = conv_in.shape[1]
+    return low(context.reshape(span_length, QUERY_HEADS * HEAD_SIZE))
+
+
+def state_space(projected, kernel, head_params, segment, low, low_back):
+    span_length = projected.shape[0]
+    conv_in = projected[:, :CONV]
+    step_raw = projected[:, CONV : CONV + MH]
+    slots = jnp.arange(span_length, dtype=jnp.int32)
+    allowed = (segment[:, None] == segment[None, :]) & (slots[None, :] <= slots[:, None])
     summed = jnp.zeros_like(conv_in) + kernel[KC][None, :]
     for lag in range(KC):
         shifted = jnp.concatenate(
-            [jnp.zeros((lag, width), jnp.float32), conv_in[: span_length - lag]], axis=0
+            [jnp.zeros((lag, CONV), jnp.float32), conv_in[: span_length - lag]], axis=0
         )
         earlier = jnp.concatenate(
             [jnp.full((lag,), -1, jnp.int32), segment[: span_length - lag]], axis=0
@@ -146,14 +159,15 @@
     mixing = low(intersection[None] * decay_matrix * step_size.T[:, None, :])
     scan_out = low_back(jnp.einsum("hts,shp->thp", mixing, scan_x, precision=None))
     scan_out = scan_out + head_params[2][None, :, None] * scan_x
-    gated = scan_out.reshape(span_length, MH * MP) * jax.nn.silu(gate_z)
-    mamba_out = low(normalize(gated, gain_all[2 * D :]))
-    joined = jnp.concatenate([context, mamba_out], axis=1)
-    hidden = block_tokens + low_back(jnp.dot(joined, w_out, precision=None))
-    normed_ff = low(normalize(hidden, gain_all[D : 2 * D]))
-    gate_up = low_back(jnp.dot(normed_ff, w_up, precision=None))
-    activated = low(jax.nn.silu(gate_up[:, :FF]) * gate_up[:, FF:])
-    return hidden + low_back(jnp.dot(activated, w_down, precision=None))
+    return scan_out.reshape(span_length, MH * MP)
+
+
+def gating(scan_out, gate_z, gain, low):
+    return low(normalize(scan_out * jax.nn.silu(gate_z), gain))
+
+
+def activation(gate_up, low):
+    return low(jax.nn.silu(gate_up[:, :FF]) * gate_up[:, FF:])
 
 
 def adamw(weight, mean, square, grad, rate):
@@ -206,6 +220,20 @@
 
 def pick(values, index, axis):
     return lax.dynamic_index_in_dim(values, index, axis, keepdims=False)
+
+
+def fence(values, after):
+    def kernel(*refs):
+        del refs
+
+    return pl.pallas_call(
+        kernel,
+        out_shape=[jax.ShapeDtypeStruct(value.shape, value.dtype) for value in values],
+        in_specs=[pl.BlockSpec(memory_space=pl.ANY)] * (len(values) + len(after)),
+        out_specs=[pl.BlockSpec(memory_space=pl.ANY)] * len(values),
+        input_output_aliases={index: index for index in range(len(values))},
+        name="fence",
+    )(*values, *after)
 
 
 def assemble(held, rows):
@@ -244,26 +272,33 @@
         kernel,
         out_shape=jax.ShapeDtypeStruct((8 * rows, columns), jnp.bfloat16),
         in_specs=[pl.BlockSpec(memory_space=pl.ANY)] * 8,
-        out_specs=pl.BlockSpec(memory_space=pl.ANY),
+        out_specs=pl.BlockSpec(memory_space=pltpu.VMEM),
         scratch_shapes=[pltpu.SemaphoreType.DMA((48,))],
+        compiler_params=pltpu.CompilerParams(vmem_limit_bytes=24 * 1024 * 1024),
         name="assemble",
     )(*held)
 
 
-def tuned_gather(own):
-    rows = own.shape[0]
-    quarter = rows // 8
+def tuned_gather(pieces):
     x, core, z, y = place()
-    half = lax.dynamic_slice_in_dim(own, core * (rows // 2), rows // 2, 0)
-    mine = jnp.concatenate(
-        [lax.dynamic_slice_in_dim(half, x * quarter, quarter, 0), half[2 * quarter :]], axis=0
-    )
-    along_z = jnp.stack([mine] + [send(mine, dz=turn) for turn in range(1, 4)])
-    across_y = send(along_z, dy=1)
-    held = [along_z, across_y]
-    held += [send(group[:, :quarter], dx=1) for group in held]
-    held += [send(group, dcore=1) for group in held]
-    return assemble(held, rows)
+    results, after = [], None
+    for own in pieces:
+        rows = own.shape[0]
+        quarter = rows // 8
+        half = lax.dynamic_slice_in_dim(own, core * (rows // 2), rows // 2, 0)
+        mine = jnp.concatenate(
+            [lax.dynamic_slice_in_dim(half, x * quarter, quarter, 0), half[2 * quarter :]], axis=0
+        )
+        if after is not None:
+            mine = fence([mine], after)[0]
+        after = [send(mine, dz=turn) for turn in range(1, 4)]
+        along_z = jnp.stack([mine] + after)
+        across_y = send(along_z, dy=1)
+        held = [along_z, across_y]
+        held += [send(group[:, :quarter], dx=1) for group in held]
+        held += [send(group, dcore=1) for group in held]
+        results.append(assemble(held, rows))
+    return results
 
 
 def add_low(left, right):
@@ -275,17 +310,24 @@
     quarter = rows // 8
     x, core, z, y = place()
     parts = grad.reshape(4, 2, 2, rows // 2, columns)
-    half = add_low(pick(parts, core, 2), send(pick(parts, 1 - core, 2), dcore=1))
+    far = pick(parts, 1 - core, 2)
+    yield [far]
+    half = add_low(pick(parts, core, 2), send(far, dcore=1))
     far = lax.dynamic_slice_in_dim(half, (1 - x) * quarter, quarter, 2)
+    yield [far]
     near = add_low(lax.dynamic_slice_in_dim(half, x * quarter, quarter, 2), send(far, dx=1))
     both = half[:, :, 2 * quarter :]
     there = jnp.concatenate([pick(near, 1 - y, 1), pick(both, 1 - y, 1)], axis=1)
     here = jnp.concatenate([pick(near, y, 1), pick(both, y, 1)], axis=1)
+    yield [there]
     column = add_low(here, send(there, dy=1))
+    turns = [pick(column, (z + turn) % 4, 0) for turn in range(1, 4)]
+    yield turns
     total = pick(column, z, 0).astype(jnp.float32)
     for turn in range(1, 4):
-        total = total + send(pick(column, (z + turn) % 4, 0), dz=turn).astype(jnp.float32)
+        total = total + send(turns[turn - 1], dz=turn).astype(jnp.float32)
     total = total.astype(jnp.bfloat16)
+    yield [total]
     across = send(total, dx=1)
     own_x, other_x = total[:quarter], across[:quarter]
     owned = jnp.concatenate(
@@ -296,18 +338,59 @@
         ],
         axis=0,
     )
+    yield [owned]
     beside = send(owned, dcore=1)
     return jnp.concatenate(
         [jnp.where(core == 0, owned, beside), jnp.where(core == 0, beside, owned)], axis=0
     )
 
 
+def general_stages(grad):
+    yield []
+    return general_reduce(grad)
+
+
+class Reductions:
+
+    def __init__(self):
+        self.tuned = tuned()
+        self.running, self.results = {}, {}
+
+    def add(self, name, grad):
+        grad = grad.astype(jnp.bfloat16)
+        self.running[name] = tuned_reduce(grad) if self.tuned else general_stages(grad)
+
+    def step(self, values):
+        after = []
+        for name in list(self.running):
+            try:
+                after += next(self.running[name])
+            except StopIteration as stop:
+                self.results[name] = stop.value
+                del self.running[name]
+        if not after:
+            return values
+        return fence(values, after)
+
+    def finish(self):
+        while self.running:
+            self.step_free()
+        return self.results
+
+    def step_free(self):
+        for name in list(self.running):
+            try:
+                next(self.running[name])
+            except StopIteration as stop:
+                self.results[name] = stop.value
+                del self.running[name]
+
+
 def tuned():
     return lax.axis_size("rep") == 4 and lax.axis_size("shard") == 8
 
 
 def gather_weights(mixer_in, mixer_out, swiglu_in, swiglu_out, gains, conv_kernel):
-    gather = tuned_gather if tuned() else general_gather
     rows = mixer_in.shape[0]
     owners = lax.axis_size("shard")
     width = conv_kernel.shape[1]
@@ -321,28 +404,27 @@
         [low_in[:, QKV + GATE :], vector.astype(jnp.bfloat16), jnp.zeros((rows, tail), jnp.bfloat16)],
         axis=1,
     )
-    w_conv = gather(conv_piece)
-    w_qkv = gather(low_in[:, :QKV])
-    w_gate = gather(low_in[:, QKV : QKV + GATE])
-    w_out = gather(mixer_out.astype(jnp.bfloat16))
-    w_up = gather(swiglu_in.astype(jnp.bfloat16))
-    w_down = gather(swiglu_out.astype(jnp.bfloat16))
-    every = w_conv[:, CONV + MH : CONV + MH + lanes].reshape(owners, rows * lanes)
+    pieces = [
+        conv_piece,
+        low_in[:, :QKV],
+        low_in[:, QKV : QKV + GATE],
+        mixer_out.astype(jnp.bfloat16),
+        swiglu_in.astype(jnp.bfloat16),
+        swiglu_out.astype(jnp.bfloat16),
+    ]
+    if tuned():
+        pieces = tuned_gather(pieces)
+    else:
+        pieces = [general_gather(piece) for piece in pieces]
+    every = pieces[0][:, CONV + MH : CONV + MH + lanes].reshape(owners, rows * lanes)
     gains_all = every[:, : gains.shape[0]].reshape(-1)
     taps = every[:, gains.shape[0] : count].reshape(owners, KC + 1, width)
     taps = jnp.swapaxes(taps, 0, 1).reshape(KC + 1, owners * width)
-    return (w_conv, w_qkv, w_gate, w_out, w_up, w_down, gains_all, taps)
-
-
-def reduce_grads(grads, head_grad):
-    reduce = tuned_reduce if tuned() else general_reduce
+    return pieces + [gains_all.astype(jnp.float32), taps.astype(jnp.float32)]
+
+
+def with_vectors(conv_g, gains_g, taps_g, head_grad):
     owners = lax.axis_size("shard")
-    conv_g, qkv_g, gate_g, out_g, up_g, down_g, gains_g, taps_g = grads
-    down = reduce(down_g.astype(jnp.bfloat16))
-    up = reduce(up_g.astype(jnp.bfloat16))
-    out = reduce(out_g.astype(jnp.bfloat16))
-    gate = reduce(gate_g.astype(jnp.bfloat16))
-    qkv = reduce(qkv_g.astype(jnp.bfloat16))
     rows = conv_g.shape[0] // owners
     width = taps_g.shape[1] // owners
     vector = jnp.concatenate(
@@ -357,26 +439,85 @@
     lanes = -(-count // rows)
     vector = jnp.pad(vector, ((0, 0), (0, lanes * rows - count))).reshape(owners * rows, lanes)
     used = CONV + MH
-    conv_g = jnp.concatenate(
-        [conv_g[:, :used], vector, jnp.zeros((owners * rows, STEP_LANES - MH - lanes), jnp.float32)],
-        axis=1,
-    )
-    conv = reduce(conv_g.astype(jnp.bfloat16))
+    vector = jnp.pad(vector, ((0, 0), (MH, STEP_LANES - MH - lanes)))
+    return jnp.concatenate([conv_g[:, :CONV], conv_g[:, CONV:] + vector], axis=1)
+
+
+def split_vectors(conv, own_gains, width, head_shape):
+    rows = conv.shape[0]
+    count = own_gains + (KC + 1) * width + head_shape[0] * head_shape[1]
+    lanes = -(-count // rows)
+    used = CONV + MH
     flat = conv[:, used : used + lanes].astype(jnp.float32).reshape(-1)
-    own_gains = gains_g.shape[0] // owners
-    own_taps = (KC + 1) * width
-    matrix = jnp.concatenate([qkv, gate, conv[:, :used]], axis=1)
+    taps_end = own_gains + (KC + 1) * width
     return (
-        (
-            matrix.astype(jnp.float32),
-            out.astype(jnp.float32),
-            up.astype(jnp.float32),
-            down.astype(jnp.float32),
-            flat[:own_gains],
-            flat[own_gains : own_gains + own_taps].reshape(KC + 1, width),
-        ),
-        flat[own_gains + own_taps : count].reshape(head_grad.shape),
-    )
+        flat[:own_gains],
+        flat[own_gains:taps_end].reshape(KC + 1, width),
+        flat[taps_end:count].reshape(head_shape),
+    )
+
+
+def forward_backward(tokens, cotangent, seq_row, weights, head_params):
+    low, low_back = make_rounders()
+    w_conv, w_qkv, w_gate, w_out, w_up, w_down, gain_all, taps = weights
+    segment, token_position, valid = layout(seq_row, tokens.shape[0])
+    values = tokens.astype(jnp.float32)
+
+    normed, pull_norm = jax.vjp(lambda v, g: low(normalize(v, g)), values, gain_all[:D])
+    normed_low = rows_of(normed)
+    scan_out, pull_scan = jax.vjp(
+        lambda p, k, h: state_space(p, k, h, segment, low, low_back),
+        dot(normed_low, w_conv),
+        taps,
+        head_params,
+    )
+    context, pull_context = jax.vjp(
+        lambda p: attention(p, segment, token_position, low, low_back), dot(normed_low, w_qkv)
+    )
+    mamba_out, pull_gating = jax.vjp(
+        lambda s, z, g: gating(s, z, g, low), scan_out, dot(normed_low, w_gate), gain_all[2 * D :]
+    )
+    joined = jnp.concatenate([rows_of(context), rows_of(mamba_out)], axis=1)
+    hidden = values + dot(joined, w_out)
+    normed_ff, pull_ff = jax.vjp(lambda v, g: low(normalize(v, g)), hidden, gain_all[D : 2 * D])
+    normed_ff_low = rows_of(normed_ff)
+    activated, pull_active = jax.vjp(lambda g: activation(g, low), dot(normed_ff_low, w_up))
+    activated_low = rows_of(activated)
+    output = (hidden + dot(activated_low, w_down)).astype(jnp.bfloat16)
+
+    moving = Reductions()
+    cot = jnp.where(valid[:, None], cotangent, jnp.zeros_like(cotangent))
+    (up_cot,) = pull_active(dot_right(cot, w_down))
+    up_cot = rows_of(up_cot)
+    moving.add("down", dot_left(activated_low, cot))
+    (up_cot,) = moving.step([up_cot])
+    moving.add("up", dot_left(normed_ff_low, up_cot))
+    (ff_cot,) = moving.step([dot_right(up_cot, w_up)])
+    hidden_part, gain_ff = pull_ff(ff_cot)
+    hidden_cot = cot.astype(jnp.float32) + hidden_part
+    hidden_low = rows_of(hidden_cot)
+    moving.add("out", dot_left(joined, hidden_low))
+    (joined_cot,) = moving.step([dot_right(hidden_low, w_out)])
+    scan_cot, gate_cot, gain_scan = pull_gating(joined_cot[:, QUERY_HEADS * HEAD_SIZE :])
+    gate_cot = rows_of(gate_cot)
+    moving.add("gate", dot_left(normed_low, gate_cot))
+    (scan_cot,) = moving.step([scan_cot])
+    conv_cot, taps_grad, head_grad = pull_scan(scan_cot)
+    conv_cot = rows_of(conv_cot)
+    (context_cot,) = moving.step([fence([joined_cot[:, : QUERY_HEADS * HEAD_SIZE]], [conv_cot])[0]])
+    (qkv_cot,) = pull_context(context_cot)
+    qkv_cot = rows_of(qkv_cot)
+    normed_cot = (
+        dot_right(qkv_cot, w_qkv) + dot_right(gate_cot, w_gate) + dot_right(conv_cot, w_conv)
+    )
+    tokens_part, gain_in = pull_norm(normed_cot)
+    token_grad = hidden_cot + tokens_part
+    gains_grad = jnp.concatenate([gain_in, gain_ff, gain_scan])
+    moving.add(
+        "conv", with_vectors(dot_left(normed_low, conv_cot), gains_grad, taps_grad, head_grad)
+    )
+    moving.add("qkv", dot_left(normed_low, qkv_cot))
+    return output, token_grad, moving.finish()
 
 
 def on_device(
@@ -405,20 +546,22 @@
     head_params_mean,
     head_params_square,
 ):
-    value_rounder, grad_rounder = make_rounders()
-    gathered = gather_weights(mixer_in, mixer_out, swiglu_in, swiglu_out, gains, conv_kernel)
-    weights = tuple((piece.astype(jnp.float32) for piece in gathered))
-    segment, token_position, valid = layout(seq_lengths[0], tokens.shape[0])
-    cot_rows = cotangent.astype(jnp.float32) * valid[:, None].astype(jnp.float32)
-
-    def forward(values, weight_set, params):
-        return block_forward(
-            values, weight_set, params, segment, token_position, value_rounder, grad_rounder
-        )
-
-    output, pull = jax.vjp(forward, tokens.astype(jnp.float32), weights, head_params)
-    token_grad, weight_grads, param_grad = pull(cot_rows)
-    owned, head_grad = reduce_grads(weight_grads, param_grad)
+    weights = gather_weights(mixer_in, mixer_out, swiglu_in, swiglu_out, gains, conv_kernel)
+    output, token_grad, sums = forward_backward(
+        tokens, cotangent, seq_lengths[0], weights, head_params
+    )
+    own_gains, own_taps, head_grad = split_vectors(
+        sums["conv"], gains.shape[0], conv_kernel.shape[1], head_params.shape
+    )
+    matrix = jnp.concatenate([sums["qkv"], sums["gate"], sums["conv"][:, : CONV + MH]], axis=1)
+    owned = (
+        matrix.astype(jnp.float32),
+        sums["out"].astype(jnp.float32),
+        sums["up"].astype(jnp.float32),
+        sums["down"].astype(jnp.float32),
+        own_gains,
+        own_taps,
+    )
     masters = (mixer_in, mixer_out, swiglu_in, swiglu_out, gains, conv_kernel)
     means = (
         mixer_in_mean,
@@ -443,7 +586,7 @@
     ]
     head_new = adamw(head_params, head_params_mean, head_params_square, head_grad, VECTOR_RATE)
     return (
-        output.astype(jnp.bfloat16),
+        output,
         token_grad,
         updated[0][0],
         updated[0][1],

time: 1540 us -> 797 us (0.52)
  Pallas kernels: 780 us -> 22.8 us
  waiting for transfers between devices: 230 us -> 163 us
  local copies, waits for them, and re-layouts: 112 us -> 157 us
  other arithmetic: 127 us -> 170 us
    pallas_call x6, Pallas kernels: 780 us -> 22.8 us  [assemble(): pl.pallas_call(kernel, out_shape=jax.ShapeDtypeStruct((8 * rows, columns)...]
    ppermute x108, waiting for transfers between devices: 230 us -> 163 us  [send(): return lax.ppermute(values, ALL, pairs)]
    unnamed x396 -> x464, local copies, waits for them, and re-layouts: 36.2 us -> 60.4 us
  transfers between devices with their start and end apart: 108 -> 108, of which waited for: 35 -> 31; matrix products, arithmetic and copies ran while one was open for 12% -> 48% of each run, Pallas kernels for 34% -> 2%
where the time goes in v3:
time: 797 us; the launch traced here: 788 us
  other arithmetic  170 us (21%)
  waiting for transfers between devices  163 us (20%)
  local copies, waits for them, and re-layouts  157 us (20%)
  matrix products  140 us (18%)
  starting transfers between devices  130 us (16%)
  Pallas kernels  22.8 us (3%)
    ppermute x108, waiting for transfers between devices, send(): return lax.ppermute(values, ALL, pairs)  163 us
    ppermute x108, starting transfers between devices, send(): return lax.ppermute(values, ALL, pairs)  130 us
    unnamed x464, local copies, waits for them, and re-layouts  60.4 us
    dot_general x3, matrix products, state_space(): jnp.einsum('hts,shp->thp', mixing, scan_x, precision=None)  38 us
    dot_general x6, matrix products, dot(): return jnp.dot(left, right, preferred_element_type=jnp.float32)  29.6 us
    dot_general x6, matrix products, dot_right(): lax.dot_general(left, right, (((1,), (1,)), ((), ())), preferred_element_...  28.5 us
    pallas_call x6, Pallas kernels, assemble(): pl.pallas_call(kernel, out_shape=jax.ShapeDtypeStruct((8 * rows, columns)...  22.8 us
    another operation x13, other arithmetic  22.1 us
  transfers between devices with their start and end apart: 108, of which 31 were waited for; matrix products, arithmetic and copies ran while one was open for 48% of the time, Pallas kernels for 2%

profile of v3, /device:TPU:1, one launch (start us, length us, event | category | flops | bytes accessed | tf_op | source)
XLA Modules:
  0.0 787.8 jit_solution(11060366920453231569)
XLA Ops:
  65.9 11.0 %collective-permute-done.31.refs_2_ = bf16[96,1024]{1,0:T(8,128)(2,1)S(1)} collective-permute-done((bf16[96,1024]{1,0:T(8,128)(2,1)}, bf16[96,1024]{1,0:T(8,128)(2,1)S(1)}, u32[]{:S(2)}, u32[]{:S(2)}) %collective-permute-start.31) | collective-permute-done | bytes 196640 | tf_op jit(solution)/shard_map/ppermute | solution.py:218
  95.6 19.1 %collective-permute-done.41.refs_2_ = bf16[48,4096]{1,0:T(8,128)(2,1)S(1)} collective-permute-done((bf16[48,4096]{1,0:T(8,128)(2,1)}, bf16[48,4096]{1,0:T(8,128)(2,1)S(1)}, u32[]{:S(2)}, u32[]{:S(2)}) %collective-permute-start.41) | collective-permute-done | bytes 393248 | tf_op jit(solution)/shard_map/ppermute | solution.py:218
  126.2 11.4 %collective-permute-done.51 = bf16[96,1024]{1,0:T(8,128)(2,1)S(1)} collective-permute-done((bf16[96,1024]{1,0:T(8,128)(2,1)}, bf16[96,1024]{1,0:T(8,128)(2,1)S(1)}, u32[]{:S(2)}, u32[]{:S(2)}) %collective-permute-start.51) | collective-permute-done | bytes 196640 | tf_op jit(solution)/shard_map/ppermute | solution.py:218
  193.3 9.0 %multiply_convert_fusion.2 = (bf16[512,1792]{1,0:T(8,128)(2,1)S(1)}, f32[512,1792]{1,0:T(8,128)}) fusion(f32[509,1792]{1,0:T(8,128)} %slice.435, pred[512]{0:T(512)(128)(4,1)S(1)} %copy-done.212, f32[1792]{0:T(1024)S(1)} %mul.838, f32[510,1792]{1,0:T(8,128)} %slice.433, pred[512]{0:T(512)(128)(4,1)S(1)} %copy-done.210, f32[1792]{0:T(1024)S(1)} %mul.835, ...), kind=kLoop, calls=%fused_computation.70 | loop fusion | flops 14680064 | bytes 20179456 | tf_op jit(solution)/shard_map/convert.23
  229.6 9.6 %multiply_convert_fusion = bf16[24,512,512]{2,1,0:T(8,128)(2,1)} fusion(f32[24,512]{1,0:T(8,128)} %copy.169, f32[24,512]{1,0:T(8,128)S(1)} %copy_bitcast_fusion, f32[512,512]{1,0:T(8,128)S(1)} %fusion.152, pred[512,512]{1,0:T(8,128)(4,1)} %copy.166), kind=kLoop, calls=%fused_computation.4 | loop fusion | flops 31457280 | bytes 13991936 | tf_op jit(solution)/shard_map/jvp()/convert_element_type | solution.py:33
  246.7 7.4 fusion.145
  254.2 6.7 divide_convert_fusion
  260.9 10.1 %bitcast_add_fusion.1 = f32[512,24,64]{0,2,1:T(8,128)} fusion(f32[512,24,64]{0,2,1:T(8,128)S(1)} %bitcast.371, bf16[512,24,64]{0,2,1:T(8,128)(2,1)S(1)} %bitcast.377, bf16[24,512,512]{2,1,0:T(8,128)(2,1)} %multiply_convert_fusion, f32[24]{0:T(128)S(1)} %copy-done.191), kind=kOutput, calls=%fused_computation.85 | convolution fusion | flops 806879232 | bytes 20447328 | tf_op jit(solution)/shard_map/jvp(hts,shp->thp)/dot_general | solution.py:160
  276.0 7.0 multiply_reduce_fusion.10
  312.2 8.9 %collective-permute-done.45.refs_3_ = bf16[4,16,4096]{2,1,0:T(8,128)(2,1)S(1)} collective-permute-done((bf16[4,16,4096]{2,1,0:T(8,128)(2,1)S(1)}, bf16[4,16,4096]{2,1,0:T(8,128)(2,1)S(1)}, u32[]{:S(2)}, u32[]{:S(2)}) %collective-permute-start.45) | collective-permute-done | bytes 524320 | tf_op jit(solution)/shard_map/ppermute | solution.py:218
  334.3 6.7 fusion.153
  341.0 6.6 fusion.74
  356.3 7.2 convolution_convert_fusion
  369.6 8.5 %fusion.154.refs_0_ = f32[512,1024]{1,0:T(8,128)} fusion(bf16[512,4096]{1,0:T(8,128)(2,1)S(1)} %copy-done.55, bf16[1024,4096]{1,0:T(8,128)(2,1)} %copy-done), kind=kOutput, calls=%fused_computation.433 | convolution fusion | flops 4294967296 | bytes 14680064 | tf_op jit(solution)/shard_map/dot_general | solution.py:103
  474.2 8.5 %bitcast_add_fusion = f32[512,24,64]{0,2,1:T(8,128)} fusion(f32[512,24,64]{0,2,1:T(8,128)S(1)} %bitcast.367, bf16[24,512,512]{2,1,0:T(8,128)(2,1)} %multiply_convert_fusion, bf16[512,24,64]{0,2,1:T(8,128)(2,1)S(1)} %convert_element_type.576, f32[24]{0:T(128)S(1)} %copy-done.192), kind=kOutput, calls=%fused_computation.84 | convolution fusion | flops 806879232 | bytes 20447328 | tf_op jit(solution)/shard_map/transpose(jvp(hts,shp->thp))/dot_general | solution.py:160
  482.8 19.3 %fusion.3 = (f32[24,512]{1,0:T(8,128)S(1)}, f32[24,512]{1,0:T(8,128)}, f32[24,512]{1,0:T(8,128)S(1)}, bf16[512,512]{1,0:T(8,128)(2,1)S(1)}) fusion(f32[24,512]{1,0:T(8,128)S(1)} %copy-done.163, f32[24,512]{1,0:T(8,128)S(1)} %copy-done.159, f32[512,512]{1,0:T(8,128)S(1)} %copy-done.85, pred[512,512]{1,0:T(8,128)(4,1)S(1)} %copy-done.127, ...), kind=kOutput, calls=%fused_computation.8 | convolution fusion | flops 886796288 | bytes 5226496 | tf_op jit(solution)/shard_map/transpose(jvp(hts,shp->thp))/dot_general | solution.py:160
  506.5 10.2 %multiply_reduce_fusion.6 = (f32[1792]{0:T(1024)S(1)}, f32[1792]{0:T(1024)S(1)}, f32[1792]{0:T(1024)S(1)}, f32[1792]{0:T(1024)S(1)}, f32[1792]{0:T(1024)S(1)}, /*index=5*/f32[512,1792]{1,0:T(8,128)S(1)}) fusion(f32[509,1792]{1,0:T(8,128)} %slice.435, pred[512]{0:T(512)(128)(4,1)} %get-tuple-element.213, f32[512,1920]{1,0:T(8,128)} %copy-done.41, ...), kind=kLoop, calls=%fused_computation.68 | loop fusion | flops 21093632 | bytes 25684480 | tf_op jit(solution)/shard_map/transpose(jvp())/reduce_sum | solution.py:148
  529.8 7.9 %multiply_add_fusion = f32[512,1792]{1,0:T(8,128)} fusion(f32[512,1792]{1,0:T(8,128)} %copy-done.40, f32[511,1792]{1,0:T(8,128)} %fusion.23, f32[510,1792]{1,0:T(8,128)} %fusion.24, f32[509,1792]{1,0:T(8,128)} %fusion.25, f32[1792]{0:T(1024)S(1)} %copy-done.173), kind=kLoop, calls=%fused_computation.69 | loop fusion | flops 3670016 | bytes 18314240 | tf_op jit(solution)/shard_map/transpose(jvp())/add_any | solution.py:141
  556.7 7.9 collective-permute-done.97
  564.6 9.0 %collective-permute-start.66 = (bf16[96,1024]{1,0:T(8,128)(2,1)S(1)}, bf16[96,1024]{1,0:T(8,128)(2,1)S(1)}, u32[]{:S(2)}, u32[]{:S(2)}) collective-permute-start(bf16[96,1024]{1,0:T(8,128)(2,1)S(1)} %copy-done.144), channel_id=1, source_target_pairs={{0,2},{1,3},{2,4},{3,5},{4,6},{5,7},{6,0},{7,1},{8,10},{9,11},{10,... | collective-permute-start | bytes 589832 | tf_op jit(solution)/shard_map/ppermute | solution.py:218
  681.2 11.1 %collective-permute-done.83 = bf16[48,1536]{1,0:T(8,128)(2,1)S(1)} collective-permute-done((bf16[48,1536]{1,0:T(8,128)(2,1)S(1)}, bf16[48,1536]{1,0:T(8,128)(2,1)S(1)}, u32[]{:S(2)}, u32[]{:S(2)}) %collective-permute-start.83) | collective-permute-done | bytes 147488 | tf_op jit(solution)/shard_map/ppermute | solution.py:218
  726.5 12.9 %collective-permute-done.89 = bf16[4,48,1920]{2,1,0:T(8,128)(2,1)S(1)} collective-permute-done((bf16[4,48,1920]{2,1,0:T(8,128)(2,1)S(1)}, bf16[4,48,1920]{2,1,0:T(8,128)(2,1)S(1)}, u32[]{:S(2)}, u32[]{:S(2)}) %collective-permute-start.89) | collective-permute-done | bytes 737312 | tf_op jit(solution)/shard_map/ppermute | solution.py:218
  744.1 12.7 %collective-permute-done.91 = bf16[48,1920]{1,0:T(8,128)(2,1)S(1)} collective-permute-done((bf16[48,1920]{1,0:T(8,128)(2,1)S(1)}, bf16[48,1920]{1,0:T(8,128)(2,1)S(1)}, u32[]{:S(2)}, u32[]{:S(2)}) %collective-permute-start.91) | collective-permute-done | bytes 184352 | tf_op jit(solution)/shard_map/ppermute | solution.py:218
  770.5 7.1 multiply_subtract_fusion
  (987 shorter events, 547.8 us)
Async XLA Ops:
  46.8 42.7 %collective-permute-start.3 = (bf16[4,48,1920]{2,1,0:T(8,128)(2,1)}, bf16[4,48,1920]{2,1,0:T(8,128)(2,1)}, u32[]{:S(2)}, u32[]{:S(2)}) collective-permute-start(bf16[4,48,1920]{2,1,0:T(8,128)(2,1)} %pad_maximum_fusion.11.refs_0_), channel_id=1, source_target_pairs={{0,1},{1,0},{2,3},{3,2},{4,5},{5,4},{6,7},{7,6},{8,9},{9,8},{10,11... | collective-permute-start | bytes 2211848 | tf_op jit(solution)/shard_map/ppermute | solution.py:218
  84.3 34.6 %collective-permute-start.23 = (bf16[4,48,1536]{2,1,0:T(8,128)(2,1)S(1)}, bf16[4,48,1536]{2,1,0:T(8,128)(2,1)S(1)}, u32[]{:S(2)}, u32[]{:S(2)}) collective-permute-start(bf16[4,48,1536]{2,1,0:T(8,128)(2,1)S(1)} %pad_maximum_fusion.13.refs_0_), channel_id=1, source_target_pairs={{0,1},{1,0},{2,3},{3,2},{4,5},{5,4},{6,7},{7,6},{8,9},{9,8},{10,11... | collective-permute-start | bytes 1769480 | tf_op jit(solution)/shard_map/ppermute | solution.py:218
  85.6 29.2 %collective-permute-start.41 = (bf16[48,4096]{1,0:T(8,128)(2,1)}, bf16[48,4096]{1,0:T(8,128)(2,1)S(1)}, u32[]{:S(2)}, u32[]{:S(2)}) collective-permute-start(bf16[48,4096]{1,0:T(8,128)(2,1)} %fence.14), channel_id=1, source_target_pairs={{0,4},{1,5},{2,6},{3,7},{4,0},{5,1},{6,2},{7,3},{8,12},{9,13},{10,... | collective-permute-start | bytes 1179656 | tf_op jit(solution)/shard_map/ppermute | solution.py:218
  86.6 30.2 %collective-permute-start.40 = (bf16[48,4096]{1,0:T(8,128)(2,1)}, bf16[48,4096]{1,0:T(8,128)(2,1)}, u32[]{:S(2)}, u32[]{:S(2)}) collective-permute-start(bf16[48,4096]{1,0:T(8,128)(2,1)} %fence.14), channel_id=1, source_target_pairs={{0,2},{1,3},{2,4},{3,5},{4,6},{5,7},{6,0},{7,1},{8,10},{9,11},{10,... | collective-permute-start | bytes 1179656 | tf_op jit(solution)/shard_map/ppermute | solution.py:218
  89.5 31.5 %collective-permute-start.26 = (bf16[4,48,1536]{2,1,0:T(8,128)(2,1)S(1)}, bf16[4,48,1536]{2,1,0:T(8,128)(2,1)S(1)}, u32[]{:S(2)}, u32[]{:S(2)}) collective-permute-start(bf16[4,48,1536]{2,1,0:T(8,128)(2,1)S(1)} %pad_maximum_fusion.13.refs_0_), channel_id=1, source_target_pairs={{0,8},{1,9},{2,10},{3,11},{4,12},{5,13},{6,14},{7,15},{8,0},{9,1},... | collective-permute-start | bytes 1769480 | tf_op jit(solution)/shard_map/ppermute | solution.py:218
  115.5 38.4 %collective-permute-start.33 = (bf16[4,96,1024]{2,1,0:T(8,128)(2,1)S(1)}, bf16[4,96,1024]{2,1,0:T(8,128)(2,1)}, u32[]{:S(2)}, u32[]{:S(2)}) collective-permute-start(bf16[4,96,1024]{2,1,0:T(8,128)(2,1)S(1)} %pad_maximum_fusion.7.refs_0_), channel_id=1, source_target_pairs={{0,1},{1,0},{2,3},{3,2},{4,5},{5,4},{6,7},{7,6},{8,9},{9,8},{10,11... | collective-permute-start | bytes 2359304 | tf_op jit(solution)/shard_map/ppermute | solution.py:218
  119.0 36.2 %collective-permute-start.27 = (bf16[4,48,1536]{2,1,0:T(8,128)(2,1)S(1)}, bf16[4,48,1536]{2,1,0:T(8,128)(2,1)S(1)}, u32[]{:S(2)}, u32[]{:S(2)}) collective-permute-start(bf16[4,48,1536]{2,1,0:T(8,128)(2,1)S(1)} %collective-permute-done.23.refs_1_), channel_id=1, source_target_pairs={{0,8},{1,9},{2,10},{3,11},{4,12},{5,13},{6,14},{7,15},{8,0},{9,1},... | collective-permute-start | bytes 1769480 | tf_op jit(solution)/shard_map/ppermute | solution.py:218
  137.6 31.8 %collective-permute-start.6 = (bf16[4,48,1920]{2,1,0:T(8,128)(2,1)}, bf16[4,48,1920]{2,1,0:T(8,128)(2,1)}, u32[]{:S(2)}, u32[]{:S(2)}) collective-permute-start(bf16[4,48,1920]{2,1,0:T(8,128)(2,1)} %pad_maximum_fusion.11.refs_0_), channel_id=1, source_target_pairs={{0,8},{1,9},{2,10},{3,11},{4,12},{5,13},{6,14},{7,15},{8,0},{9,1},... | collective-permute-start | bytes 2211848 | tf_op jit(solution)/shard_map/ppermute | solution.py:218
  138.6 32.8 %collective-permute-start.7 = (bf16[4,48,1920]{2,1,0:T(8,128)(2,1)}, bf16[4,48,1920]{2,1,0:T(8,128)(2,1)}, u32[]{:S(2)}, u32[]{:S(2)}) collective-permute-start(bf16[4,48,1920]{2,1,0:T(8,128)(2,1)} %collective-permute-done.3.refs_1_), channel_id=1, source_target_pairs={{0,8},{1,9},{2,10},{3,11},{4,12},{5,13},{6,14},{7,15},{8,0},{9,1},... | collective-permute-start | bytes 2211848 | tf_op jit(solution)/shard_map/ppermute | solution.py:218
  168.9 106.3 %collective-permute-start.36 = (bf16[4,96,1024]{2,1,0:T(8,128)(2,1)S(1)}, bf16[4,96,1024]{2,1,0:T(8,128)(2,1)}, u32[]{:S(2)}, u32[]{:S(2)}) collective-permute-start(bf16[4,96,1024]{2,1,0:T(8,128)(2,1)S(1)} %pad_maximum_fusion.7.refs_0_), channel_id=1, source_target_pairs={{0,8},{1,9},{2,10},{3,11},{4,12},{5,13},{6,14},{7,15},{8,0},{9,1},... | collective-permute-start | bytes 2359304 | tf_op jit(solution)/shard_map/ppermute | solution.py:218
  168.9 105.6 %collective-permute-start.38 = (bf16[4,32,1024]{2,1,0:T(8,128)(2,1)}, bf16[4,32,1024]{2,1,0:T(8,128)(2,1)S(1)}, u32[]{:S(2)}, u32[]{:S(2)}) collective-permute-start(bf16[4,32,1024]{2,1,0:T(8,128)(2,1)} %collective-permute-done.34.refs_2_), channel_id=1, source_target_pairs={{0,8},{1,9},{2,10},{3,11},{4,12},{5,13},{6,14},{7,15},{8,0},{9,1},... | collective-permute-start | bytes 786440 | tf_op jit(solution)/shard_map/ppermute | solution.py:218
  169.4 119.8 %collective-permute-start.43 = (bf16[4,48,4096]{2,1,0:T(8,128)(2,1)S(1)}, bf16[4,48,4096]{2,1,0:T(8,128)(2,1)}, u32[]{:S(2)}, u32[]{:S(2)}) collective-permute-start(bf16[4,48,4096]{2,1,0:T(8,128)(2,1)S(1)} %pad_maximum_fusion.1.refs_0_), channel_id=1, source_target_pairs={{0,1},{1,0},{2,3},{3,2},{4,5},{5,4},{6,7},{7,6},{8,9},{9,8},{10,11... | collective-permute-start | bytes 4718600 | tf_op jit(solution)/shard_map/ppermute | solution.py:218
  170.6 114.3 %collective-permute-start.44 = (bf16[4,16,4096]{2,1,0:T(8,128)(2,1)}, bf16[4,16,4096]{2,1,0:T(8,128)(2,1)}, u32[]{:S(2)}, u32[]{:S(2)}) collective-permute-start(bf16[4,16,4096]{2,1,0:T(8,128)(2,1)} %slice.448), channel_id=1, source_target_pairs={{0,16},{1,17},{2,18},{3,19},{4,20},{5,21},{6,22},{7,23},{8,24},{9,... | collective-permute-start | bytes 1572872 | tf_op jit(solution)/shard_map/ppermute | solution.py:218
  171.5 117.7 %collective-permute-start.53 = (bf16[4,96,1024]{2,1,0:T(8,128)(2,1)S(1)}, bf16[4,96,1024]{2,1,0:T(8,128)(2,1)}, u32[]{:S(2)}, u32[]{:S(2)}) collective-permute-start(bf16[4,96,1024]{2,1,0:T(8,128)(2,1)S(1)} %pad_maximum_fusion.8.refs_0_), channel_id=1, source_target_pairs={{0,1},{1,0},{2,3},{3,2},{4,5},{5,4},{6,7},{7,6},{8,9},{9,8},{10,11... | collective-permute-start | bytes 2359304 | tf_op jit(solution)/shard_map/ppermute | solution.py:218
  284.9 41.4 %collective-permute-start.46 = (bf16[4,48,4096]{2,1,0:T(8,128)(2,1)S(1)}, bf16[4,48,4096]{2,1,0:T(8,128)(2,1)}, u32[]{:S(2)}, u32[]{:S(2)}) collective-permute-start(bf16[4,48,4096]{2,1,0:T(8,128)(2,1)S(1)} %pad_maximum_fusion.1.refs_0_), channel_id=1, source_target_pairs={{0,8},{1,9},{2,10},{3,11},{4,12},{5,13},{6,14},{7,15},{8,0},{9,1},... | collective-permute-start | bytes 4718600 | tf_op jit(solution)/shard_map/ppermute | solution.py:218
  289.2 37.1 %collective-permute-start.47 = (bf16[4,48,4096]{2,1,0:T(8,128)(2,1)}, bf16[4,48,4096]{2,1,0:T(8,128)(2,1)}, u32[]{:S(2)}, u32[]{:S(2)}) collective-permute-start(bf16[4,48,4096]{2,1,0:T(8,128)(2,1)} %collective-permute-done.43.refs_1_), channel_id=1, source_target_pairs={{0,8},{1,9},{2,10},{3,11},{4,12},{5,13},{6,14},{7,15},{8,0},{9,1},... | collective-permute-start | bytes 4718600 | tf_op jit(solution)/shard_map/ppermute | solution.py:218
  369.1 57.2 %collective-permute-start.62 = (bf16[4,2,64,4096]{3,2,1,0:T(8,128)(2,1)}, bf16[4,2,64,4096]{3,2,1,0:T(8,128)(2,1)}, u32[]{:S(2)}, u32[]{:S(2)}) collective-permute-start(bf16[4,2,64,4096]{3,2,1,0:T(8,128)(2,1)} %dynamic-slice_bitcast_fusion.refs_2_), channel_id=1, source_target_pairs={{0,8},{1,9},{2,10},{3,11},{4,12},{5,13},{6,14},{7,15},{8,0},{9,1},... | collective-permute-start | bytes 12582920 | tf_op jit(solution)/shard_map/ppermute | solution.py:218
  431.2 32.6 %collective-permute-start.64 = (bf16[4,2,16,4096]{3,2,1,0:T(8,128)(2,1)}, bf16[4,2,16,4096]{3,2,1,0:T(8,128)(2,1)}, u32[]{:S(2)}, u32[]{:S(2)}) collective-permute-start(bf16[4,2,16,4096]{3,2,1,0:T(8,128)(2,1)} %constant_dynamic-slice_fusion.4.refs_2_), channel_id=1, source_target_pairs={{0,16},{1,17},{2,18},{3,19},{4,20},{5,21},{6,22},{7,23},{8,24},{9,... | collective-permute-start | bytes 3145736 | tf_op jit(solution)/shard_map/ppermute | solution.py:218
  455.0 148.6 %collective-permute-start.71 = (bf16[4,2,64,1536]{3,2,1,0:T(8,128)(2,1)}, bf16[4,2,64,1536]{3,2,1,0:T(8,128)(2,1)}, u32[]{:S(2)}, u32[]{:S(2)}) collective-permute-start(bf16[4,2,64,1536]{3,2,1,0:T(8,128)(2,1)} %dynamic-slice_bitcast_fusion.3.refs_6_), channel_id=1, source_target_pairs={{0,8},{1,9},{2,10},{3,11},{4,12},{5,13},{6,14},{7,15},{8,0},{9,1},... | collective-permute-start | bytes 4718600 | tf_op jit(solution)/shard_map/ppermute | solution.py:218
  460.4 86.7 %collective-permute-start.95 = (bf16[4,96,1024]{2,1,0:T(8,128)(2,1)}, bf16[4,96,1024]{2,1,0:T(8,128)(2,1)}, u32[]{:S(2)}, u32[]{:S(2)}) collective-permute-start(bf16[4,96,1024]{2,1,0:T(8,128)(2,1)} %pad_maximum_fusion.10.refs_5_), channel_id=1, source_target_pairs={{0,1},{1,0},{2,3},{3,2},{4,5},{5,4},{6,7},{7,6},{8,9},{9,8},{10,11... | collective-permute-start | bytes 2359304 | tf_op jit(solution)/shard_map/ppermute | solution.py:218
  467.9 151.9 %collective-permute-start.69 = (bf16[4,48,4096]{2,1,0:T(8,128)(2,1)}, bf16[4,48,4096]{2,1,0:T(8,128)(2,1)}, u32[]{:S(2)}, u32[]{:S(2)}) collective-permute-start(bf16[4,48,4096]{2,1,0:T(8,128)(2,1)} %pad_maximum_fusion.2.refs_4_), channel_id=1, source_target_pairs={{0,1},{1,0},{2,3},{3,2},{4,5},{5,4},{6,7},{7,6},{8,9},{9,8},{10,11... | collective-permute-start | bytes 4718600 | tf_op jit(solution)/shard_map/ppermute | solution.py:218
  618.1 46.6 %collective-permute-start.81 = (bf16[4,48,1536]{2,1,0:T(8,128)(2,1)}, bf16[4,48,1536]{2,1,0:T(8,128)(2,1)}, u32[]{:S(2)}, u32[]{:S(2)}) collective-permute-start(bf16[4,48,1536]{2,1,0:T(8,128)(2,1)} %pad_maximum_fusion.14), channel_id=1, source_target_pairs={{0,1},{1,0},{2,3},{3,2},{4,5},{5,4},{6,7},{7,6},{8,9},{9,8},{10,11... | collective-permute-start | bytes 1769480 | tf_op jit(solution)/shard_map/ppermute | solution.py:218
  643.5 50.6 %collective-permute-start.103 = (bf16[48,4096]{1,0:T(8,128)(2,1)}, bf16[48,4096]{1,0:T(8,128)(2,1)}, u32[]{:S(2)}, u32[]{:S(2)}) collective-permute-start(bf16[48,4096]{1,0:T(8,128)(2,1)} %get-tuple-element.130.refs_4_), channel_id=1, source_target_pairs={{0,6},{1,7},{2,0},{3,1},{4,2},{5,3},{6,4},{7,5},{8,14},{9,15},{10,... | collective-permute-start | bytes 1179656 | tf_op jit(solution)/shard_map/ppermute | solution.py:218
  646.7 48.4 %collective-permute-start.102 = (bf16[48,4096]{1,0:T(8,128)(2,1)S(1)}, bf16[48,4096]{1,0:T(8,128)(2,1)}, u32[]{:S(2)}, u32[]{:S(2)}) collective-permute-start(bf16[48,4096]{1,0:T(8,128)(2,1)S(1)} %copy-done.107), channel_id=1, source_target_pairs={{0,4},{1,5},{2,6},{3,7},{4,0},{5,1},{6,2},{7,3},{8,12},{9,13},{10,... | collective-permute-start | bytes 1179656 | tf_op jit(solution)/shard_map/ppermute | solution.py:218
  (314 other events, 2780.0 us)

commit v4 on v3

--- a/solution.py
+++ b/solution.py
@@ -1,9 +1,11 @@
+import functools
+
 import jax
 import jax.numpy as jnp
 from jax import lax
 from jax.experimental import pallas as pl
 from jax.experimental.pallas import tpu as pltpu
-from jax.sharding import PartitionSpec as P
+from jax.sharding import Mesh, PartitionSpec as P
 
 D = 1024
 FF = 2048
@@ -130,12 +132,8 @@
     return low(context.reshape(span_length, QUERY_HEADS * HEAD_SIZE))
 
 
-def state_space(projected, kernel, head_params, segment, low, low_back):
-    span_length = projected.shape[0]
-    conv_in = projected[:, :CONV]
-    step_raw = projected[:, CONV : CONV + MH]
-    slots = jnp.arange(span_length, dtype=jnp.int32)
-    allowed = (segment[:, None] == segment[None, :]) & (slots[None, :] <= slots[:, None])
+def convolution(conv_in, kernel, segment, low):
+    span_length = conv_in.shape[0]
     summed = jnp.zeros_like(conv_in) + kernel[KC][None, :]
     for lag in range(KC):
         shifted = jnp.concatenate(
@@ -146,10 +144,16 @@
         )
         keep = earlier == segment
         summed = summed + kernel[KC - 1 - lag][None, :] * jnp.where(keep[:, None], shifted, 0.0)
-    conv_out = jax.nn.silu(summed)
-    scan_x = low(conv_out[:, : MH * MP]).reshape(span_length, MH, MP)
-    scan_b = low(conv_out[:, MH * MP : MH * MP + NS])
-    scan_c = low(conv_out[:, MH * MP + NS :])
+    return low(jax.nn.silu(summed))
+
+
+def scan(conv_out, step_raw, head_params, segment, low, low_back):
+    span_length = conv_out.shape[0]
+    slots = jnp.arange(span_length, dtype=jnp.int32)
+    allowed = (segment[:, None] == segment[None, :]) & (slots[None, :] <= slots[:, None])
+    scan_x = conv_out[:, : MH * MP].reshape(span_length, MH, MP)
+    scan_b = conv_out[:, MH * MP : MH * MP + NS]
+    scan_c = conv_out[:, MH * MP + NS :]
     step_size = jax.nn.softplus(step_raw + head_params[0][None, :])
     cumulative = jnp.cumsum(-step_size * jnp.exp(head_params[1])[None, :], axis=0)
     intersection = low_back(jnp.dot(scan_c, scan_b.T, precision=None))
@@ -185,25 +189,24 @@
 GATE = MH * MP
 CONV = MH * MP + 2 * NS
 STEP_LANES = 128
-BOTH = ("shard", "rep")
-ALL = ("rep", "shard")
-
-
-def general_gather(own):
-    copies = lax.axis_size("rep")
-    rows = own.shape[0] // copies
-    part = lax.dynamic_slice_in_dim(own, lax.axis_index("rep") * rows, rows, 0)
-    return lax.all_gather(part, BOTH, axis=0, tiled=True)
-
-
-def general_reduce(grad):
-    piece = lax.psum_scatter(grad, BOTH, scatter_dimension=0, tiled=True)
-    return lax.all_gather(piece, "rep", axis=0, tiled=True)
+
+
+def general_gather(own, rep, shard):
+    part = own
+    if rep:
+        copies = lax.axis_size(rep)
+        rows = own.shape[0] // copies
+        part = lax.dynamic_slice_in_dim(own, lax.axis_index(rep) * rows, rows, 0)
+    return lax.all_gather(part, shard + rep, axis=0, tiled=True)
+
+
+def general_reduce(grad, rep, shard):
+    piece = lax.psum_scatter(grad, shard + rep, scatter_dimension=0, tiled=True)
+    return lax.all_gather(piece, rep, axis=0, tiled=True)
 
 
 def place():
-    rep, shard = lax.axis_index("rep"), lax.axis_index("shard")
-    return (rep // 2, rep % 2, shard // 2, shard % 2)
+    return tuple(lax.axis_index(name) for name in ("x", "core", "z", "y"))
 
 
 def send(values, dx=0, dcore=0, dz=0, dy=0):
@@ -215,7 +218,7 @@
                     start = (x * 2 + core) * 8 + z * 2 + y
                     end = ((x ^ dx) * 2 + (core ^ dcore)) * 8 + ((z + dz) % 4) * 2 + (y ^ dy)
                     pairs.append((start, end))
-    return lax.ppermute(values, ALL, pairs)
+    return lax.ppermute(values, ("x", "core", "z", "y"), pairs)
 
 
 def pick(values, index, axis):
@@ -242,8 +245,7 @@
 
     def kernel(*refs):
         sources, target, sems = refs[:8], refs[8], refs[9]
-        rep, shard = lax.axis_index("rep"), lax.axis_index("shard")
-        x, core, z, y = rep // 2, rep % 2, shard // 2, shard % 2
+        x, core, z, y = place()
         copies = []
         for other_core in range(2):
             half = core if other_core == 0 else 1 - core
@@ -345,54 +347,82 @@
     )
 
 
-def general_stages(grad):
-    yield []
-    return general_reduce(grad)
+def paired_reduce(grad):
+    rows, columns = grad.shape[0] // 8, grad.shape[1]
+    x, core, z, y = place()
+    parts = grad.reshape(8, 2, rows // 2, columns)
+    far = pick(parts, 1 - core, 1)
+    yield [far]
+    half = add_low(pick(parts, core, 1), send(far, dcore=1)).reshape(4 * rows, columns)
+    yield [half]
+    own = lax.psum_scatter(half, ("z", "y", "x"), scatter_dimension=0, tiled=True)
+    yield None
+    across = send(own, dx=1)
+    owned = jnp.concatenate(
+        [jnp.where(x == 0, own, across), jnp.where(x == 0, across, own)], axis=0
+    )
+    yield None
+    beside = send(owned, dcore=1)
+    return jnp.concatenate(
+        [jnp.where(core == 0, owned, beside), jnp.where(core == 0, beside, owned)], axis=0
+    )
+
+
+def general_stages(grad, rep, shard):
+    yield None
+    return general_reduce(grad, rep, shard)
 
 
 class Reductions:
 
-    def __init__(self):
-        self.tuned = tuned()
-        self.running, self.results = {}, {}
-
-    def add(self, name, grad):
+    def __init__(self, axes):
+        self.axes = axes
+        self.running, self.results, self.waiting = {}, {}, {}
+
+    def add(self, name, grad, paired=False):
         grad = grad.astype(jnp.bfloat16)
-        self.running[name] = tuned_reduce(grad) if self.tuned else general_stages(grad)
+        if not tuned(self.axes):
+            self.running[name] = general_stages(grad, *self.axes)
+        elif paired:
+            self.running[name] = paired_reduce(grad)
+        else:
+            self.running[name] = tuned_reduce(grad)
 
     def step(self, values):
         after = []
         for name in list(self.running):
-            try:
-                after += next(self.running[name])
-            except StopIteration as stop:
-                self.results[name] = stop.value
-                del self.running[name]
-        if not after:
-            return values
-        return fence(values, after)
+            if self.waiting.get(name):
+                continue
+            ready = self.advance(name)
+            if ready is None:
+                self.waiting[name] = True
+            else:
+                after += ready
+        return fence(values, after) if after else values
+
+    def advance(self, name):
+        try:
+            return next(self.running[name])
+        except StopIteration as stop:
+            self.results[name] = stop.value
+            del self.running[name]
+            return []
 
     def finish(self):
         while self.running:
-            self.step_free()
+            for name in list(self.running):
+                self.advance(name)
         return self.results
 
-    def step_free(self):
-        for name in list(self.running):
-            try:
-                next(self.running[name])
-            except StopIteration as stop:
-                self.results[name] = stop.value
-                del self.running[name]
-
-
-def tuned():
-    return lax.axis_size("rep") == 4 and lax.axis_size("shard") == 8
-
-
-def gather_weights(mixer_in, mixer_out, swiglu_in, swiglu_out, gains, conv_kernel):
+
+def tuned(axes):
+    return axes == (("x", "core"), ("z", "y"))
+
+
+def gather_weights(axes, mixer_in, mixer_out, swiglu_in, swiglu_out, gains, conv_kernel):
     rows = mixer_in.shape[0]
-    owners = lax.axis_size("shard")
+    rep, shard = axes
+    owners = lax.axis_size(shard)
     width = conv_kernel.shape[1]
     count = gains.shape[0] + conv_kernel.size
     lanes = -(-count // rows)
@@ -404,18 +434,13 @@
         [low_in[:, QKV + GATE :], vector.astype(jnp.bfloat16), jnp.zeros((rows, tail), jnp.bfloat16)],
         axis=1,
     )
-    pieces = [
-        conv_piece,
-        low_in[:, :QKV],
-        low_in[:, QKV : QKV + GATE],
-        mixer_out.astype(jnp.bfloat16),
-        swiglu_in.astype(jnp.bfloat16),
-        swiglu_out.astype(jnp.bfloat16),
-    ]
-    if tuned():
+    pieces = [conv_piece, low_in[:, : QKV + GATE]]
+    if tuned(axes):
         pieces = tuned_gather(pieces)
     else:
-        pieces = [general_gather(piece) for piece in pieces]
+        pieces = [general_gather(piece, rep, shard) for piece in pieces]
+    for master in (mixer_out, swiglu_in, swiglu_out):
+        pieces.append(general_gather(master.astype(jnp.bfloat16), rep, shard))
     every = pieces[0][:, CONV + MH : CONV + MH + lanes].reshape(owners, rows * lanes)
     gains_all = every[:, : gains.shape[0]].reshape(-1)
     taps = every[:, gains.shape[0] : count].reshape(owners, KC + 1, width)
@@ -423,8 +448,7 @@
     return pieces + [gains_all.astype(jnp.float32), taps.astype(jnp.float32)]
 
 
-def with_vectors(conv_g, gains_g, taps_g, head_grad):
-    owners = lax.axis_size("shard")
+def with_vectors(conv_g, gains_g, taps_g, head_grad, owners):
     rows = conv_g.shape[0] // owners
     width = taps_g.shape[1] // owners
     vector = jnp.concatenate(
@@ -438,7 +462,6 @@
     count = vector.shape[1]
     lanes = -(-count // rows)
     vector = jnp.pad(vector, ((0, 0), (0, lanes * rows - count))).reshape(owners * rows, lanes)
-    used = CONV + MH
     vector = jnp.pad(vector, ((0, 0), (MH, STEP_LANES - MH - lanes)))
     return jnp.concatenate([conv_g[:, :CONV], conv_g[:, CONV:] + vector], axis=1)
 
@@ -457,25 +480,31 @@
     )
 
 
-def forward_backward(tokens, cotangent, seq_row, weights, head_params):
+def forward_backward(axes, tokens, cotangent, seq_row, weights, head_params):
     low, low_back = make_rounders()
-    w_conv, w_qkv, w_gate, w_out, w_up, w_down, gain_all, taps = weights
+    w_conv, w_side, w_out, w_up, w_down, gain_all, taps = weights
     segment, token_position, valid = layout(seq_row, tokens.shape[0])
     values = tokens.astype(jnp.float32)
+    context_width = QUERY_HEADS * HEAD_SIZE
 
     normed, pull_norm = jax.vjp(lambda v, g: low(normalize(v, g)), values, gain_all[:D])
     normed_low = rows_of(normed)
+    projected = dot(normed_low, w_conv)
+    conv_out, pull_conv = jax.vjp(
+        lambda p, k: convolution(p, k, segment, low), projected[:, :CONV], taps
+    )
     scan_out, pull_scan = jax.vjp(
-        lambda p, k, h: state_space(p, k, h, segment, low, low_back),
-        dot(normed_low, w_conv),
-        taps,
+        lambda c, r, h: scan(c, r, h, segment, low, low_back),
+        conv_out,
+        projected[:, CONV : CONV + MH],
         head_params,
     )
+    beside = dot(normed_low, w_side)
     context, pull_context = jax.vjp(
-        lambda p: attention(p, segment, token_position, low, low_back), dot(normed_low, w_qkv)
+        lambda p: attention(p, segment, token_position, low, low_back), beside[:, :QKV]
     )
     mamba_out, pull_gating = jax.vjp(
-        lambda s, z, g: gating(s, z, g, low), scan_out, dot(normed_low, w_gate), gain_all[2 * D :]
+        lambda s, z, g: gating(s, z, g, low), scan_out, beside[:, QKV:], gain_all[2 * D :]
     )
     joined = jnp.concatenate([rows_of(context), rows_of(mamba_out)], axis=1)
     hidden = values + dot(joined, w_out)
@@ -485,42 +514,47 @@
     activated_low = rows_of(activated)
     output = (hidden + dot(activated_low, w_down)).astype(jnp.bfloat16)
 
-    moving = Reductions()
+    moving = Reductions(axes)
     cot = jnp.where(valid[:, None], cotangent, jnp.zeros_like(cotangent))
     (up_cot,) = pull_active(dot_right(cot, w_down))
     up_cot = rows_of(up_cot)
-    moving.add("down", dot_left(activated_low, cot))
+    moving.add("down", dot_left(activated_low, cot), paired=True)
     (up_cot,) = moving.step([up_cot])
-    moving.add("up", dot_left(normed_ff_low, up_cot))
+    moving.add("up", dot_left(normed_ff_low, up_cot), paired=True)
     (ff_cot,) = moving.step([dot_right(up_cot, w_up)])
     hidden_part, gain_ff = pull_ff(ff_cot)
     hidden_cot = cot.astype(jnp.float32) + hidden_part
     hidden_low = rows_of(hidden_cot)
-    moving.add("out", dot_left(joined, hidden_low))
+    moving.add("out", dot_left(joined, hidden_low), paired=True)
     (joined_cot,) = moving.step([dot_right(hidden_low, w_out)])
-    scan_cot, gate_cot, gain_scan = pull_gating(joined_cot[:, QUERY_HEADS * HEAD_SIZE :])
-    gate_cot = rows_of(gate_cot)
-    moving.add("gate", dot_left(normed_low, gate_cot))
+    scan_cot, gate_cot, gain_scan = pull_gating(joined_cot[:, context_width:])
+    (qkv_cot,) = pull_context(joined_cot[:, :context_width])
+    side_cot = jnp.concatenate([rows_of(qkv_cot), rows_of(gate_cot)], axis=1)
+    moving.add("side", dot_left(normed_low, side_cot))
     (scan_cot,) = moving.step([scan_cot])
-    conv_cot, taps_grad, head_grad = pull_scan(scan_cot)
-    conv_cot = rows_of(conv_cot)
-    (context_cot,) = moving.step([fence([joined_cot[:, : QUERY_HEADS * HEAD_SIZE]], [conv_cot])[0]])
-    (qkv_cot,) = pull_context(context_cot)
-    qkv_cot = rows_of(qkv_cot)
-    normed_cot = (
-        dot_right(qkv_cot, w_qkv) + dot_right(gate_cot, w_gate) + dot_right(conv_cot, w_conv)
-    )
+    conv_out_cot, step_cot, head_grad = pull_scan(scan_cot)
+    (conv_out_cot,) = moving.step([conv_out_cot])
+    conv_cot, taps_grad = pull_conv(conv_out_cot)
+    conv_cot = rows_of(
+        jnp.concatenate(
+            [conv_cot, step_cot, jnp.zeros((tokens.shape[0], STEP_LANES - MH), jnp.float32)], axis=1
+        )
+    )
+    (conv_cot,) = moving.step([conv_cot])
+    normed_cot = dot_right(side_cot, w_side) + dot_right(conv_cot, w_conv)
     tokens_part, gain_in = pull_norm(normed_cot)
     token_grad = hidden_cot + tokens_part
     gains_grad = jnp.concatenate([gain_in, gain_ff, gain_scan])
+    owners = lax.axis_size(axes[1])
     moving.add(
-        "conv", with_vectors(dot_left(normed_low, conv_cot), gains_grad, taps_grad, head_grad)
-    )
-    moving.add("qkv", dot_left(normed_low, qkv_cot))
+        "conv",
+        with_vectors(dot_left(normed_low, conv_cot), gains_grad, taps_grad, head_grad, owners),
+    )
     return output, token_grad, moving.finish()
 
 
 def on_device(
+    axes,
     tokens,
     cotangent,
     seq_lengths,
@@ -546,14 +580,14 @@
     head_params_mean,
     head_params_square,
 ):
-    weights = gather_weights(mixer_in, mixer_out, swiglu_in, swiglu_out, gains, conv_kernel)
+    weights = gather_weights(axes, mixer_in, mixer_out, swiglu_in, swiglu_out, gains, conv_kernel)
     output, token_grad, sums = forward_backward(
-        tokens, cotangent, seq_lengths[0], weights, head_params
+        axes, tokens, cotangent, seq_lengths[0], weights, head_params
     )
     own_gains, own_taps, head_grad = split_vectors(
         sums["conv"], gains.shape[0], conv_kernel.shape[1], head_params.shape
     )
-    matrix = jnp.concatenate([sums["qkv"], sums["gate"], sums["conv"][:, : CONV + MH]], axis=1)
+    matrix = jnp.concatenate([sums["side"], sums["conv"][:, : CONV + MH]], axis=1)
     owned = (
         matrix.astype(jnp.float32),
         sums["out"].astype(jnp.float32),
@@ -613,59 +647,16 @@
 
 
 def solution(mesh):
+    rep, shard = ("rep",), ("shard",)
+    if mesh.shape["rep"] == 4 and mesh.shape["shard"] == 8:
+        rep, shard = ("x", "core"), ("z", "y")
+        mesh = Mesh(mesh.devices.reshape(2, 2, 4, 2), rep + shard)
+    rows, owned, across, copied = P(rep + shard, None), P(shard, None), P(None, shard), P()
+    optimizer = (owned,) * 12 + (P(shard),) * 3 + (across,) * 3 + (copied,) * 3
     return jax.shard_map(
-        on_device,
+        functools.partial(on_device, (rep, shard)),
         mesh=mesh,
-        in_specs=(
-            P(("rep", "shard"), None),
-            P(("rep", "shard"), None),
-            P(("rep", "shard"), None),
-            P("shard", None),
-            P("shard", None),
-            P("shard", None),
-            P("shard", None),
-            P("shard", None),
-            P("shard", None),
-            P("shard", None),
-            P("shard", None),
-            P("shard", None),
-            P("shard", None),
-            P("shard", None),
-            P("shard", None),
-            P("shard"),
-            P("shard"),
-            P("shard"),
-            P(None, "shard"),
-            P(None, "shard"),
-            P(None, "shard"),
-            P(),
-            P(),
-            P(),
-        ),
-        out_specs=(
-            P(("rep", "shard"), None),
-            P(("rep", "shard"), None),
-            P("shard", None),
-            P("shard", None),
-            P("shard", None),
-            P("shard", None),
-            P("shard", None),
-            P("shard", None),
-            P("shard", None),
-            P("shard", None),
-            P("shard", None),
-            P("shard", None),
-            P("shard", None),
-            P("shard", None),
-            P("shard"),
-            P("shard"),
-            P("shard"),
-            P(None, "shard"),
-            P(None, "shard"),
-            P(None, "shard"),
-            P(),
-            P(),
-            P(),
-        ),
+        in_specs=(rows, rows, rows) + optimizer,
+        out_specs=(rows, rows) + optimizer,
         check_vma=False,
     )

time: 797 us -> 652 us (0.82)
  starting transfers between devices: 130 us -> 47.2 us
  local copies, waits for them, and re-layouts: 157 us -> 118 us
  waiting for transfers between devices: 163 us -> 148 us
  Pallas kernels: 22.8 us -> 9.97 us
  between operations: 4.15 us -> 16.4 us
  other arithmetic: 170 us -> 159 us
    ppermute x108 -> x45, starting transfers between devices: 130 us -> 47 us  [send(): return lax.ppermute(values, ('x', 'core', 'z', 'y'), pairs)]
    unnamed x464 -> x317, local copies, waits for them, and re-layouts: 60.4 us -> 40.8 us
    ppermute x108 -> x45, waiting for transfers between devices: 163 us -> 148 us  [send(): return lax.ppermute(values, ('x', 'core', 'z', 'y'), pairs)]
    pallas_call x6 -> x2, Pallas kernels: 22.8 us -> 9.97 us  [assemble(): pl.pallas_call(kernel, out_shape=jax.ShapeDtypeStruct((8 * rows, columns)...]
    convert_element_type x5 -> x6, other arithmetic: 19.6 us -> 28.1 us  [round_value(): values.astype(jnp.bfloat16)]
    dot_general x6 -> x5, matrix products: 28.5 us -> 33.1 us  [dot_right(): lax.dot_general(left, right, (((1,), (1,)), ((), ())), preferred_element_...]
    convert_element_type x24 -> x11, other arithmetic: 19.5 us -> 23 us  [add_low(): (left.astype(jnp.float32) + right.astype(jnp.float32)).astype(jnp.bfloat16)]
    dot_general x6 -> x5, matrix products: 21.6 us -> 18.7 us  [dot_left(): lax.dot_general(left, right, (((0,), (0,)), ((), ())), preferred_element_...]
  transfers between devices with their start and end apart: 108 -> 51, of which waited for: 31 -> 17; matrix products, arithmetic and copies ran while one was open for 48% -> 58% of each run, Pallas kernels for 2% -> 2%
where the time goes in v4:
time: 652 us; the launch traced here: 646 us
  other arithmetic  159 us (24%)
  waiting for transfers between devices  148 us (23%)
  matrix products  147 us (23%)
  local copies, waits for them, and re-layouts  118 us (18%)
  starting transfers between devices  47.2 us (7%)
  between operations  16.4 us (3%)
  Pallas kernels  9.97 us (2%)
    ppermute x45, waiting for transfers between devices, send(): return lax.ppermute(values, ('x', 'core', 'z', 'y'), pairs)  148 us
    ppermute x45, starting transfers between devices, send(): return lax.ppermute(values, ('x', 'core', 'z', 'y'), pairs)  47 us
    unnamed x317, local copies, waits for them, and re-layouts  40.8 us
    dot_general x3, matrix products, scan(): jnp.einsum('hts,shp->thp', mixing, scan_x, precision=None)  39.1 us
    dot_general x5, matrix products, dot_right(): lax.dot_general(left, right, (((1,), (1,)), ((), ())), preferred_element_...  33.1 us
    dot_general x5, matrix products, dot(): return jnp.dot(left, right, preferred_element_type=jnp.float32)  31.6 us
    convert_element_type x6, other arithmetic, round_value(): values.astype(jnp.bfloat16)  28.1 us
    convert_element_type x11, other arithmetic, add_low(): (left.astype(jnp.float32) + right.astype(jnp.float32)).astype(jnp.bfloat16)  23 us
  transfers between devices with their start and end apart: 51, of which 17 were waited for; matrix products, arithmetic and copies ran while one was open for 58% of the time, Pallas kernels for 2%

profile of v4, /device:TPU:1, one launch (start us, length us, event | category | flops | bytes accessed | tf_op | source)
XLA Modules:
  0.0 645.9 jit_solution(7330355938371559150)
XLA Ops:
  30.1 12.1 %collective-permute-done.1.refs_2_ = bf16[48,1920]{1,0:T(8,128)(2,1)S(1)} collective-permute-done((bf16[48,1920]{1,0:T(8,128)(2,1)}, bf16[48,1920]{1,0:T(8,128)(2,1)S(1)}, u32[]{:S(2)}, u32[]{:S(2)}) %collective-permute-start.1) | collective-permute-done | bytes 184352 | tf_op jit(solution)/shard_map/ppermute | solution.py:221
  48.9 6.2 collective-permute-done.12
  55.1 14.3 %collective-permute-done.11 = bf16[48,2304]{1,0:T(8,128)(2,1)S(1)} collective-permute-done((bf16[48,2304]{1,0:T(8,128)(2,1)}, bf16[48,2304]{1,0:T(8,128)(2,1)S(1)}, u32[]{:S(2)}, u32[]{:S(2)}) %collective-permute-start.11) | collective-permute-done | bytes 221216 | tf_op jit(solution)/shard_map/ppermute | solution.py:221
  78.2 7.0 %collective-permute-done.4.refs_2_ = bf16[4,16,1920]{2,1,0:T(8,128)(2,1)S(1)} collective-permute-done((bf16[4,16,1920]{2,1,0:T(8,128)(2,1)S(1)}, bf16[4,16,1920]{2,1,0:T(8,128)(2,1)S(1)}, u32[]{:S(2)}, u32[]{:S(2)}) %collective-permute-start.4) | collective-permute-done | bytes 245792 | tf_op jit(solution)/shard_map/ppermute | solution.py:221
  136.6 9.0 %multiply_convert_fusion.2 = (bf16[512,1792]{1,0:T(8,128)(2,1)S(1)}, f32[512,1792]{1,0:T(8,128)}) fusion(f32[509,1792]{1,0:T(8,128)} %slice.313, pred[512]{0:T(512)(128)(4,1)S(1)} %copy-done.134, f32[1792]{0:T(1024)S(1)} %mul.828, f32[510,1792]{1,0:T(8,128)} %slice.311, pred[512]{0:T(512)(128)(4,1)S(1)} %copy-done.131, f32[1792]{0:T(1024)S(1)} %mul.825, ...), kind=kLoop, calls=%fused_computation.72 | loop fusion | flops 14680064 | bytes 20179456 | tf_op jit(solution)/shard_map/jvp()/convert_element_type | solution.py:35
  161.5 8.3 %multiply_convert_fusion = bf16[24,512,512]{2,1,0:T(8,128)(2,1)} fusion(f32[24,512]{1,0:T(8,128)S(1)} %copy.174, f32[24,512]{1,0:T(8,128)S(1)} %copy_bitcast_fusion.2, f32[512,512]{1,0:T(8,128)S(1)} %fusion.95, pred[512,512]{1,0:T(8,128)(4,1)S(1)} %copy-done.63), kind=kLoop, calls=%fused_computation.4 | loop fusion | flops 31457280 | bytes 13991936 | tf_op jit(solution)/shard_map/jvp()/convert_element_type | solution.py:35
  169.8 10.4 %bitcast_add_fusion.1 = f32[512,24,64]{0,2,1:T(8,128)} fusion(f32[512,24,64]{0,2,1:T(8,128)S(1)} %bitcast.284, bf16[512,24,64]{0,2,1:T(8,128)(2,1)S(1)} %bitcast.288, bf16[24,512,512]{2,1,0:T(8,128)(2,1)} %multiply_convert_fusion, f32[24]{0:T(128)S(1)} %get-tuple-element.223), kind=kOutput, calls=%fused_computation.85 | convolution fusion | flops 806879232 | bytes 20447328 | tf_op jit(solution)/shard_map/jvp(hts,shp->thp)/dot_general | solution.py:164
  203.3 7.5 %fusion.140 = (f32[2,4,512]{2,1,0:T(4,128)S(1)}, f32[2,4,512,512]{2,3,1,0:T(8,128)}) fusion(pred[512,512]{0,1:T(8,128)(4,1)} %fusion.58, bf16[512,2,4,64]{0,3,2,1:T(8,128)(2,1)} %bitcast.313, bf16[512,2,64]{0,2,1:T(8,128)(2,1)S(1)} %pad_maximum_fusion.24), kind=kOutput, calls=%fused_computation.354 | convolution fusion | flops 276824576 | bytes 9322496 | tf_op jit(solution)/shard_map/jvp()/sub | solution.py:130
  210.8 6.7 %divide_convert_fusion = bf16[2,4,512,512]{2,3,1,0:T(8,128)(2,1)} fusion(f32[2,4,512,512]{2,3,1,0:T(8,128)} %get-tuple-element.230, f32[2,4,512]{2,1,0:T(4,128)S(1)} %get-tuple-element.229), kind=kLoop, calls=%fused_computation.20 | loop fusion | flops 4194304 | bytes 12599296 | tf_op jit(solution)/shard_map/jvp()/convert_element_type | solution.py:35
  231.5 11.9 %fusion.147 = f32[512,4096]{1,0:T(8,128)} fusion(bf16[512,1024]{1,0:T(8,128)(2,1)} %multiply_convert_fusion.4, bf16[1024,4096]{1,0:T(8,128)(2,1)} %all-gather.6.cloned.1.call-done), kind=kOutput, calls=%fused_computation.357 | convolution fusion | flops 4294967296 | bytes 17825792 | tf_op jit(solution)/shard_map/dot_general | solution.py:97
  243.4 8.7 %fusion.69 = (f32[512,2048]{1,0:T(8,128)S(1)}, f32[512,2048]{1,0:T(8,128)S(1)}, bf16[512,2048]{1,0:T(8,128)(2,1)S(1)}) fusion(f32[512,4096]{1,0:T(8,128)} %fusion.147, bf16[2048,1024]{1,0:T(8,128)(2,1)} %all-gather.8.cloned.1.call-done, bf16[512,1024]{1,0:T(8,128)(2,1)} %param.25, pred[512]{0:T(512)(128)(4,1)S(1)} %copy-done.145), kind=kOutput, calls=%fused_computation.190 | convolution fusion | flops 2162688000 | bytes 24117760 | tf_op jit(solution)/shard_map/dot_general | solution.py:105
  260.7 7.5 %convolution_convert_fusion = bf16[1024,4096]{1,0:T(8,128)(2,1)S(1)} fusion(bf16[512,1024]{1,0:T(8,128)(2,1)} %multiply_convert_fusion.4, bf16[512,4096]{1,0:T(8,128)(2,1)} %fence.8), kind=kOutput, calls=%fused_computation.22 | convolution fusion | flops 4299161600 | bytes 13631488 | tf_op jit(solution)/shard_map/dot_general | solution.py:101
  278.3 10.5 %fusion.148.refs_0_ = f32[512,1024]{1,0:T(8,128)} fusion(bf16[512,4096]{1,0:T(8,128)(2,1)} %fence.8, bf16[1024,4096]{1,0:T(8,128)(2,1)} %all-gather.6.cloned.1.call-done), kind=kOutput, calls=%fused_computation.358 | convolution fusion | flops 4294967296 | bytes 14680064 | tf_op jit(solution)/shard_map/dot_general | solution.py:105
  308.4 6.9 %add_convert_fusion.2 = bf16[512,1024]{1,0:T(8,128)(2,1)} fusion(f32[512,1024]{1,0:T(8,128)} %copy-done.16, bf16[512,2048]{1,0:T(8,128)(2,1)} %copy-done.148, bf16[2048,1024]{1,0:T(8,128)(2,1)} %all-gather.8.cloned.1.call-done), kind=kOutput, calls=%fused_computation.120 | convolution fusion | flops 2148532224 | bytes 9437184 | tf_op jit(solution)/shard_map/dot_general | solution.py:97
  323.7 7.2 %fusion.4 = bf16[8,64,4096]{2,1,0:T(8,128)(2,1)} fusion(bf16[8,64,4096]{2,1,0:T(8,128)(2,1)} %collective-permute-done.21, bf16[8,2,64,4096]{3,2,1,0:T(8,128)(2,1)} %bitcast.287, s32[]{:T(128)S(6)} %select_n.308), kind=kLoop, calls=%fused_computation.10 | loop fusion | flops 8388608 | bytes 12582916 | tf_op jit(solution)/shard_map/convert_element_type | solution.py:307
  371.2 9.1 %bitcast_add_fusion = f32[512,24,64]{0,2,1:T(8,128)} fusion(f32[512,24,64]{0,2,1:T(8,128)S(1)} %bitcast.273, bf16[24,512,512]{2,1,0:T(8,128)(2,1)} %multiply_convert_fusion, bf16[512,24,64]{0,2,1:T(8,128)(2,1)S(1)} %convert_element_type.368, f32[24]{0:T(128)S(1)} %copy-done.111), kind=kOutput, calls=%fused_computation.84 | convolution fusion | flops 806879232 | bytes 20447328 | tf_op jit(solution)/shard_map/transpose(jvp(hts,shp->thp))/dot_general | solution.py:164
  384.1 19.6 %fusion.3 = (f32[24,512]{1,0:T(8,128)S(1)}, f32[24,512]{1,0:T(8,128)S(1)}, f32[24,512]{1,0:T(8,128)S(1)}, bf16[512,512]{1,0:T(8,128)(2,1)}) fusion(f32[24,512]{1,0:T(8,128)S(1)} %copy-done.86, f32[24,512]{1,0:T(8,128)S(1)} %copy-done.83, f32[512,512]{1,0:T(8,128)} %copy-done.44, pred[512,512]{1,0:T(8,128)(4,1)S(1)} %copy-done.64, ...), kind=kOutput, calls=%fused_computation.8 | convolution fusion | flops 886796288 | bytes 5226496 | tf_op jit(solution)/shard_map/transpose(jvp(hts,shp->thp))/dot_general | solution.py:164
  433.8 9.9 %multiply_reduce_fusion.6 = (f32[1792]{0:T(1024)S(1)}, f32[1792]{0:T(1024)S(1)}, f32[1792]{0:T(1024)S(1)}, f32[1792]{0:T(1024)S(1)}, f32[1792]{0:T(1024)S(1)}, /*index=5*/f32[512,1792]{1,0:T(8,128)S(1)}) fusion(f32[509,1792]{1,0:T(8,128)} %slice.313, pred[512]{0:T(512)(128)(4,1)S(1)} %copy-done.136, f32[512,1920]{1,0:T(8,128)} %copy-done.7, ...), kind=kLoop, calls=%fused_computation.69 | loop fusion | flops 19258624 | bytes 25684480 | tf_op jit(solution)/shard_map/transpose(jvp())/reduce_sum | solution.py:146
  452.3 7.4 %add_convert_fusion.1 = bf16[512,1792]{1,0:T(8,128)(2,1)} fusion(f32[512,1792]{1,0:T(8,128)} %copy-done.6, f32[511,1792]{1,0:T(8,128)} %fusion.24, f32[510,1792]{1,0:T(8,128)} %fusion.25, f32[509,1792]{1,0:T(8,128)} %fusion.26, f32[1792]{0:T(1024)S(1)} %copy-done.94), kind=kLoop, calls=%fused_computation.70 | loop fusion | flops 4587520 | bytes 16479232 | tf_op jit(solution)/shard_map/convert.17
  491.0 27.1 %collective-permute-done.25 = bf16[4,48,2304]{2,1,0:T(8,128)(2,1)} collective-permute-done((bf16[4,48,2304]{2,1,0:T(8,128)(2,1)}, bf16[4,48,2304]{2,1,0:T(8,128)(2,1)}, u32[]{:S(2)}, u32[]{:S(2)}) %collective-permute-start.25) | collective-permute-done | bytes 884768 | tf_op jit(solution)/shard_map/ppermute | solution.py:221
  529.5 15.0 %collective-permute-done.27 = bf16[48,2304]{1,0:T(8,128)(2,1)S(1)} collective-permute-done((bf16[48,2304]{1,0:T(8,128)(2,1)S(1)}, bf16[48,2304]{1,0:T(8,128)(2,1)S(1)}, u32[]{:S(2)}, u32[]{:S(2)}) %collective-permute-start.27) | collective-permute-done | bytes 221216 | tf_op jit(solution)/shard_map/ppermute | solution.py:221
  550.9 13.1 %collective-permute-done.32 = bf16[4,2,16,1920]{3,2,0,1:T(8,128)(2,1)S(1)} collective-permute-done((bf16[4,2,16,1920]{3,2,0,1:T(8,128)(2,1)S(1)}, bf16[4,2,16,1920]{3,2,0,1:T(8,128)(2,1)S(1)}, u32[]{:S(2)}, u32[]{:S(2)}) %collective-permute-start.32) | collective-permute-done | bytes 491552 | tf_op jit(solution)/shard_map/ppermute | solution.py:221
  566.8 13.6 %collective-permute-done.33 = bf16[4,48,1920]{2,1,0:T(8,128)(2,1)S(1)} collective-permute-done((bf16[4,48,1920]{2,1,0:T(8,128)(2,1)S(1)}, bf16[4,48,1920]{2,1,0:T(8,128)(2,1)S(1)}, u32[]{:S(2)}, u32[]{:S(2)}) %collective-permute-start.33) | collective-permute-done | bytes 737312 | tf_op jit(solution)/shard_map/ppermute | solution.py:221
  587.7 11.8 %collective-permute-done.35 = bf16[48,1920]{1,0:T(8,128)(2,1)S(1)} collective-permute-done((bf16[48,1920]{1,0:T(8,128)(2,1)S(1)}, bf16[48,1920]{1,0:T(8,128)(2,1)S(1)}, u32[]{:S(2)}, u32[]{:S(2)}) %collective-permute-start.35) | collective-permute-done | bytes 184352 | tf_op jit(solution)/shard_map/ppermute | solution.py:221
  (658 shorter events, 368.7 us)
Async XLA Ops:
  7.2 216.3 %all-gather.4.cloned.1.call-start = ((), (), s32[]{:S(2)}) async-start(), calls=%async_computation.3 | async-start | bytes 4325376 | tf_op jit(solution)/shard_map/all_gather | solution.py:200
  8.9 222.6 %all-gather.6.cloned.1.call-start = ((), (), s32[]{:S(2)}) async-start(), calls=%async_computation.4 | async-start | bytes 8650752 | tf_op jit(solution)/shard_map/all_gather | solution.py:200
  10.8 232.6 %all-gather.8.cloned.1.call-start = ((), (), s32[]{:S(2)}) async-start(), calls=%async_computation.5 | async-start | bytes 4325376 | tf_op jit(solution)/shard_map/all_gather | solution.py:200
  26.2 392.6 %reduce-scatter.8.cloned.1.call-start = ((), (), s32[]{:S(2)}) async-start(), calls=%async_computation.8 | async-start | bytes 2228224 | tf_op jit(solution)/shard_map/reduce_scatter | solution.py:358
  43.5 25.9 %collective-permute-start.11 = (bf16[48,2304]{1,0:T(8,128)(2,1)}, bf16[48,2304]{1,0:T(8,128)(2,1)S(1)}, u32[]{:S(2)}, u32[]{:S(2)}) collective-permute-start(bf16[48,2304]{1,0:T(8,128)(2,1)} %fence.7), channel_id=1, source_target_pairs={{0,4},{1,5},{2,6},{3,7},{4,0},{5,1},{6,2},{7,3},{8,12},{9,13},{10,... | collective-permute-start | bytes 663560 | tf_op jit(solution)/shard_map/ppermute | solution.py:221
  44.8 24.6 %collective-permute-start.10 = (bf16[48,2304]{1,0:T(8,128)(2,1)}, bf16[48,2304]{1,0:T(8,128)(2,1)S(1)}, u32[]{:S(2)}, u32[]{:S(2)}) collective-permute-start(bf16[48,2304]{1,0:T(8,128)(2,1)} %fence.7), channel_id=1, source_target_pairs={{0,2},{1,3},{2,4},{3,5},{4,6},{5,7},{6,0},{7,1},{8,10},{9,11},{10,... | collective-permute-start | bytes 663560 | tf_op jit(solution)/shard_map/ppermute | solution.py:221
  47.5 29.3 %collective-permute-start.3 = (bf16[4,48,1920]{2,1,0:T(8,128)(2,1)S(1)}, bf16[4,48,1920]{2,1,0:T(8,128)(2,1)S(1)}, u32[]{:S(2)}, u32[]{:S(2)}) collective-permute-start(bf16[4,48,1920]{2,1,0:T(8,128)(2,1)S(1)} %pad_maximum_fusion.12.refs_0_), channel_id=1, source_target_pairs={{0,1},{1,0},{2,3},{3,2},{4,5},{5,4},{6,7},{7,6},{8,9},{9,8},{10,11... | collective-permute-start | bytes 2211848 | tf_op jit(solution)/shard_map/ppermute | solution.py:221
  70.4 28.1 %collective-permute-start.13 = (bf16[4,48,2304]{2,1,0:T(8,128)(2,1)S(1)}, bf16[4,48,2304]{2,1,0:T(8,128)(2,1)S(1)}, u32[]{:S(2)}, u32[]{:S(2)}) collective-permute-start(bf16[4,48,2304]{2,1,0:T(8,128)(2,1)S(1)} %pad_maximum_fusion.10.refs_0_), channel_id=1, source_target_pairs={{0,1},{1,0},{2,3},{3,2},{4,5},{5,4},{6,7},{7,6},{8,9},{9,8},{10,11... | collective-permute-start | bytes 2654216 | tf_op jit(solution)/shard_map/ppermute | solution.py:221
  74.5 33.5 %collective-permute-start.6 = (bf16[4,48,1920]{2,1,0:T(8,128)(2,1)S(1)}, bf16[4,48,1920]{2,1,0:T(8,128)(2,1)}, u32[]{:S(2)}, u32[]{:S(2)}) collective-permute-start(bf16[4,48,1920]{2,1,0:T(8,128)(2,1)S(1)} %pad_maximum_fusion.12.refs_0_), channel_id=1, source_target_pairs={{0,8},{1,9},{2,10},{3,11},{4,12},{5,13},{6,14},{7,15},{8,0},{9,1},... | collective-permute-start | bytes 2211848 | tf_op jit(solution)/shard_map/ppermute | solution.py:221
  76.8 35.3 %collective-permute-start.7 = (bf16[4,48,1920]{2,1,0:T(8,128)(2,1)S(1)}, bf16[4,48,1920]{2,1,0:T(8,128)(2,1)}, u32[]{:S(2)}, u32[]{:S(2)}) collective-permute-start(bf16[4,48,1920]{2,1,0:T(8,128)(2,1)S(1)} %collective-permute-done.3.refs_1_), channel_id=1, source_target_pairs={{0,8},{1,9},{2,10},{3,11},{4,12},{5,13},{6,14},{7,15},{8,0},{9,1},... | collective-permute-start | bytes 2211848 | tf_op jit(solution)/shard_map/ppermute | solution.py:221
  107.8 76.0 %collective-permute-start.16 = (bf16[4,48,2304]{2,1,0:T(8,128)(2,1)S(1)}, bf16[4,48,2304]{2,1,0:T(8,128)(2,1)}, u32[]{:S(2)}, u32[]{:S(2)}) collective-permute-start(bf16[4,48,2304]{2,1,0:T(8,128)(2,1)S(1)} %pad_maximum_fusion.10.refs_0_), channel_id=1, source_target_pairs={{0,8},{1,9},{2,10},{3,11},{4,12},{5,13},{6,14},{7,15},{8,0},{9,1},... | collective-permute-start | bytes 2654216 | tf_op jit(solution)/shard_map/ppermute | solution.py:221
  108.1 75.7 %collective-permute-start.18 = (bf16[4,16,2304]{2,1,0:T(8,128)(2,1)S(1)}, bf16[4,16,2304]{2,1,0:T(8,128)(2,1)}, u32[]{:S(2)}, u32[]{:S(2)}) collective-permute-start(bf16[4,16,2304]{2,1,0:T(8,128)(2,1)S(1)} %collective-permute-done.14.refs_2_), channel_id=1, source_target_pairs={{0,8},{1,9},{2,10},{3,11},{4,12},{5,13},{6,14},{7,15},{8,0},{9,1},... | collective-permute-start | bytes 884744 | tf_op jit(solution)/shard_map/ppermute | solution.py:221
  108.3 75.5 %collective-permute-start.17 = (bf16[4,48,2304]{2,1,0:T(8,128)(2,1)S(1)}, bf16[4,48,2304]{2,1,0:T(8,128)(2,1)}, u32[]{:S(2)}, u32[]{:S(2)}) collective-permute-start(bf16[4,48,2304]{2,1,0:T(8,128)(2,1)S(1)} %collective-permute-done.13.refs_1_), channel_id=1, source_target_pairs={{0,8},{1,9},{2,10},{3,11},{4,12},{5,13},{6,14},{7,15},{8,0},{9,1},... | collective-permute-start | bytes 2654216 | tf_op jit(solution)/shard_map/ppermute | solution.py:221
  110.5 73.3 %collective-permute-start.19 = (bf16[4,16,2304]{2,1,0:T(8,128)(2,1)}, bf16[4,16,2304]{2,1,0:T(8,128)(2,1)}, u32[]{:S(2)}, u32[]{:S(2)}) collective-permute-start(bf16[4,16,2304]{2,1,0:T(8,128)(2,1)} %collective-permute-done.15.refs_3_), channel_id=1, source_target_pairs={{0,8},{1,9},{2,10},{3,11},{4,12},{5,13},{6,14},{7,15},{8,0},{9,1},... | collective-permute-start | bytes 884744 | tf_op jit(solution)/shard_map/ppermute | solution.py:221
  273.8 49.9 %collective-permute-start.21 = (bf16[8,64,4096]{2,1,0:T(8,128)(2,1)}, bf16[8,64,4096]{2,1,0:T(8,128)(2,1)}, u32[]{:S(2)}, u32[]{:S(2)}) collective-permute-start(bf16[8,64,4096]{2,1,0:T(8,128)(2,1)} %dynamic-slice_bitcast_fusion.refs_2_), channel_id=1, source_target_pairs={{0,8},{1,9},{2,10},{3,11},{4,12},{5,13},{6,14},{7,15},{8,0},{9,1},... | collective-permute-start | bytes 12582920 | tf_op jit(solution)/shard_map/ppermute | solution.py:221
  278.2 266.6 %reduce-scatter.4.cloned.1.call-start = ((), (), s32[]{:S(2)}) async-start(), calls=%async_computation.6 | async-start | bytes 2228224 | tf_op jit(solution)/shard_map/reduce_scatter | solution.py:358
  323.7 288.9 %reduce-scatter.6.cloned.1.call-start = ((), (), s32[]{:S(2)}) async-start(), calls=%async_computation.7 | async-start | bytes 4456448 | tf_op jit(solution)/shard_map/reduce_scatter | solution.py:358
  367.6 60.7 %collective-permute-start.23 = (bf16[4,2,64,2304]{3,2,1,0:T(8,128)(2,1)}, bf16[4,2,64,2304]{3,2,1,0:T(8,128)(2,1)}, u32[]{:S(2)}, u32[]{:S(2)}) collective-permute-start(bf16[4,2,64,2304]{3,2,1,0:T(8,128)(2,1)} %dynamic-slice_bitcast_fusion.1.refs_2_), channel_id=1, source_target_pairs={{0,8},{1,9},{2,10},{3,11},{4,12},{5,13},{6,14},{7,15},{8,0},{9,1},... | collective-permute-start | bytes 7077896 | tf_op jit(solution)/shard_map/ppermute | solution.py:221
  427.5 37.9 %collective-permute-start.44 = (bf16[128,1024]{1,0:T(8,128)(2,1)}, bf16[128,1024]{1,0:T(8,128)(2,1)}, u32[]{:S(2)}, u32[]{:S(2)}) collective-permute-start(bf16[128,1024]{1,0:T(8,128)(2,1)} %pad_maximum_fusion.20), channel_id=1, source_target_pairs={{0,8},{1,9},{2,10},{3,11},{4,12},{5,13},{6,14},{7,15},{8,0},{9,1},... | collective-permute-start | bytes 786440 | tf_op jit(solution)/shard_map/ppermute | solution.py:221
  432.2 35.3 %collective-permute-start.24 = (bf16[4,2,16,2304]{3,2,1,0:T(8,128)(2,1)}, bf16[4,2,16,2304]{3,2,1,0:T(8,128)(2,1)}, u32[]{:S(2)}, u32[]{:S(2)}) collective-permute-start(bf16[4,2,16,2304]{3,2,1,0:T(8,128)(2,1)} %constant_dynamic-slice_fusion.1.refs_1_), channel_id=1, source_target_pairs={{0,16},{1,17},{2,18},{3,19},{4,20},{5,21},{6,22},{7,23},{8,24},{9,... | collective-permute-start | bytes 1769480 | tf_op jit(solution)/shard_map/ppermute | solution.py:221
  478.1 40.0 %collective-permute-start.25 = (bf16[4,48,2304]{2,1,0:T(8,128)(2,1)}, bf16[4,48,2304]{2,1,0:T(8,128)(2,1)}, u32[]{:S(2)}, u32[]{:S(2)}) collective-permute-start(bf16[4,48,2304]{2,1,0:T(8,128)(2,1)} %pad_maximum_fusion.11.refs_1_), channel_id=1, source_target_pairs={{0,1},{1,0},{2,3},{3,2},{4,5},{5,4},{6,7},{7,6},{8,9},{9,8},{10,11... | collective-permute-start | bytes 2654216 | tf_op jit(solution)/shard_map/ppermute | solution.py:221
  490.6 55.6 %collective-permute-start.31 = (bf16[4,2,64,1920]{3,2,0,1:T(8,128)(2,1)}, bf16[4,2,64,1920]{3,2,0,1:T(8,128)(2,1)}, u32[]{:S(2)}, u32[]{:S(2)}) collective-permute-start(bf16[4,2,64,1920]{3,2,0,1:T(8,128)(2,1)} %bitcast.264), channel_id=1, source_target_pairs={{0,8},{1,9},{2,10},{3,11},{4,12},{5,13},{6,14},{7,15},{8,0},{9,1},... | collective-permute-start | bytes 5898248 | tf_op jit(solution)/shard_map/ppermute | solution.py:221
  520.0 24.5 %collective-permute-start.27 = (bf16[48,2304]{1,0:T(8,128)(2,1)S(1)}, bf16[48,2304]{1,0:T(8,128)(2,1)S(1)}, u32[]{:S(2)}, u32[]{:S(2)}) collective-permute-start(bf16[48,2304]{1,0:T(8,128)(2,1)S(1)} %get-tuple-element.187), channel_id=1, source_target_pairs={{0,4},{1,5},{2,6},{3,7},{4,0},{5,1},{6,2},{7,3},{8,12},{9,13},{10,... | collective-permute-start | bytes 663560 | tf_op jit(solution)/shard_map/ppermute | solution.py:221
  566.7 33.8 %collective-permute-start.40 = (bf16[128,1024]{1,0:T(8,128)(2,1)S(1)}, bf16[128,1024]{1,0:T(8,128)(2,1)S(1)}, u32[]{:S(2)}, u32[]{:S(2)}) collective-permute-start(bf16[128,1024]{1,0:T(8,128)(2,1)S(1)} %pad_maximum_fusion.19), channel_id=1, source_target_pairs={{0,8},{1,9},{2,10},{3,11},{4,12},{5,13},{6,14},{7,15},{8,0},{9,1},... | collective-permute-start | bytes 786440 | tf_op jit(solution)/shard_map/ppermute | solution.py:221
  (184 other events, 1738.5 us)
Sparse Core Ops, SparseCore 0:
  11.5 85.6 all-gather.3
  100.6 76.5 all-gather.5
  180.6 60.6 all-gather.7
  278.3 68.7 reduce-scatter.7
  349.8 77.5 reduce-scatter.3
  429.6 105.3 reduce-scatter.5

commit v5 on v4

--- a/solution.py
+++ b/solution.py
@@ -239,32 +239,25 @@
     )(*values, *after)
 
 
-def assemble(held, rows):
-    quarter = rows // 8
-    columns = held[0].shape[-1]
-
-    def kernel(*refs):
-        sources, target, sems = refs[:8], refs[8], refs[9]
-        x, core, z, y = place()
+def assemble(mine, beside, widths):
+    half = mine.shape[0] // 8
+    columns = [sum(widths[:index]) for index in range(len(widths))]
+
+    def kernel(mine_ref, beside_ref, *refs):
+        targets, sems = refs[:-1], refs[-1]
+        core = lax.axis_index("core")
         copies = []
-        for other_core in range(2):
-            half = core if other_core == 0 else 1 - core
-            for other_y in range(2):
-                row = y if other_y == 0 else 1 - y
-                for turn in range(4):
-                    owner = ((z + 4 - turn) % 4) * 2 + row
-                    base = owner * rows + half * (rows // 2)
-                    main = sources[other_core * 4 + other_y].at[turn]
-                    cross = sources[other_core * 4 + 2 + other_y].at[turn]
-                    for piece, start, count in (
-                        (main.at[pl.ds(0, quarter)], base + x * quarter, quarter),
-                        (main.at[pl.ds(quarter, 2 * quarter)], base + 2 * quarter, 2 * quarter),
-                        (cross, base + (1 - x) * quarter, quarter),
-                    ):
-                        place_at = pl.ds(pl.multiple_of(start, 16), count)
-                        copies.append(
-                            pltpu.make_async_copy(piece, target.at[place_at], sems.at[len(copies)])
+        for source, which in ((mine_ref, core), (beside_ref, 1 - core)):
+            for owner in range(8):
+                start = pl.multiple_of(owner * 2 * half + which * half, 16)
+                for target, column, width in zip(targets, columns, widths):
+                    copies.append(
+                        pltpu.make_async_copy(
+                            source.at[pl.ds(owner * half, half), pl.ds(column, width)],
+                            target.at[pl.ds(start, half)],
+                            sems.at[len(copies)],
                         )
+                    )
         for copy in copies:
             copy.start()
         for copy in copies:
@@ -272,35 +265,21 @@
 
     return pl.pallas_call(
         kernel,
-        out_shape=jax.ShapeDtypeStruct((8 * rows, columns), jnp.bfloat16),
-        in_specs=[pl.BlockSpec(memory_space=pl.ANY)] * 8,
-        out_specs=pl.BlockSpec(memory_space=pltpu.VMEM),
-        scratch_shapes=[pltpu.SemaphoreType.DMA((48,))],
+        out_shape=[jax.ShapeDtypeStruct((16 * half, width), jnp.bfloat16) for width in widths],
+        in_specs=[pl.BlockSpec(memory_space=pl.ANY)] * 2,
+        out_specs=[pl.BlockSpec(memory_space=pltpu.VMEM)] * len(widths),
+        scratch_shapes=[pltpu.SemaphoreType.DMA((16 * len(widths),))],
         compiler_params=pltpu.CompilerParams(vmem_limit_bytes=24 * 1024 * 1024),
         name="assemble",
-    )(*held)
-
-
-def tuned_gather(pieces):
+    )(mine, beside)
+
+
+def paired_gather(own, widths):
+    rows = own.shape[0]
     x, core, z, y = place()
-    results, after = [], None
-    for own in pieces:
-        rows = own.shape[0]
-        quarter = rows // 8
-        half = lax.dynamic_slice_in_dim(own, core * (rows // 2), rows // 2, 0)
-        mine = jnp.concatenate(
-            [lax.dynamic_slice_in_dim(half, x * quarter, quarter, 0), half[2 * quarter :]], axis=0
-        )
-        if after is not None:
-            mine = fence([mine], after)[0]
-        after = [send(mine, dz=turn) for turn in range(1, 4)]
-        along_z = jnp.stack([mine] + after)
-        across_y = send(along_z, dy=1)
-        held = [along_z, across_y]
-        held += [send(group[:, :quarter], dx=1) for group in held]
-        held += [send(group, dcore=1) for group in held]
-        results.append(assemble(held, rows))
-    return results
+    part = lax.dynamic_slice_in_dim(own, (core * 2 + x) * (rows // 4), rows // 4, 0)
+    mine = lax.all_gather(part.astype(jnp.bfloat16), ("z", "y", "x"), axis=0, tiled=True)
+    return assemble(mine, send(mine, dcore=1), widths)
 
 
 def add_low(left, right):
@@ -353,9 +332,13 @@
     parts = grad.reshape(8, 2, rows // 2, columns)
     far = pick(parts, 1 - core, 1)
     yield [far]
-    half = add_low(pick(parts, core, 1), send(far, dcore=1)).reshape(4 * rows, columns)
-    yield [half]
-    own = lax.psum_scatter(half, ("z", "y", "x"), scatter_dimension=0, tiled=True)
+    half = add_low(pick(parts, core, 1), send(far, dcore=1))
+    parts = half.reshape(8, 2, rows // 4, columns)
+    far = pick(parts, 1 - x, 1)
+    yield [far]
+    near = add_low(pick(parts, x, 1), send(far, dx=1)).reshape(2 * rows, columns)
+    yield [near]
+    own = lax.psum_scatter(near, ("z", "y"), scatter_dimension=0, tiled=True)
     yield None
     across = send(own, dx=1)
     owned = jnp.concatenate(
@@ -428,19 +411,21 @@
     lanes = -(-count // rows)
     vector = jnp.concatenate([gains, conv_kernel.reshape(-1)])
     vector = jnp.pad(vector, (0, lanes * rows - count)).reshape(rows, lanes)
-    low_in = mixer_in.astype(jnp.bfloat16)
     tail = STEP_LANES - MH - lanes
-    conv_piece = jnp.concatenate(
-        [low_in[:, QKV + GATE :], vector.astype(jnp.bfloat16), jnp.zeros((rows, tail), jnp.bfloat16)],
+    piece_in = jnp.concatenate(
+        [mixer_in[:, QKV + GATE :], vector, jnp.zeros((rows, tail)), mixer_in[:, : QKV + GATE]],
         axis=1,
     )
-    pieces = [conv_piece, low_in[:, : QKV + GATE]]
-    if tuned(axes):
-        pieces = tuned_gather(pieces)
-    else:
-        pieces = [general_gather(piece, rep, shard) for piece in pieces]
-    for master in (mixer_out, swiglu_in, swiglu_out):
-        pieces.append(general_gather(master.astype(jnp.bfloat16), rep, shard))
+    pieces = []
+    for master in (piece_in, mixer_out, swiglu_in, swiglu_out):
+        widths = (master.shape[1],)
+        if master is piece_in:
+            widths = (CONV + STEP_LANES, QKV + GATE)
+        if tuned(axes):
+            pieces += paired_gather(master, widths)
+        else:
+            every = general_gather(master.astype(jnp.bfloat16), rep, shard)
+            pieces += jnp.split(every, widths[:1], axis=1)[: len(widths)]
     every = pieces[0][:, CONV + MH : CONV + MH + lanes].reshape(owners, rows * lanes)
     gains_all = every[:, : gains.shape[0]].reshape(-1)
     taps = every[:, gains.shape[0] : count].reshape(owners, KC + 1, width)
@@ -530,7 +515,7 @@
     scan_cot, gate_cot, gain_scan = pull_gating(joined_cot[:, context_width:])
     (qkv_cot,) = pull_context(joined_cot[:, :context_width])
     side_cot = jnp.concatenate([rows_of(qkv_cot), rows_of(gate_cot)], axis=1)
-    moving.add("side", dot_left(normed_low, side_cot))
+    moving.add("side", dot_left(normed_low, side_cot), paired=True)
     (scan_cot,) = moving.step([scan_cot])
     conv_out_cot, step_cot, head_grad = pull_scan(scan_cot)
     (conv_out_cot,) = moving.step([conv_out_cot])

time: 652 us -> 923 us (1.42)
  waiting for transfers between devices: 148 us -> 414 us
  local copies, waits for them, and re-layouts: 118 us -> 142 us
  starting transfers between devices: 47.2 us -> 31.6 us
    all_gather x3 -> x4, waiting for transfers between devices: 0.01 us -> 271 us  [paired_gather(): lax.all_gather(part.astype(jnp.bfloat16), ('z', 'y', 'x'), axis=0, tiled=...]
    ppermute x45 -> x28, waiting for transfers between devices: 148 us -> 44.9 us  [send(): return lax.ppermute(values, ('x', 'core', 'z', 'y'), pairs)]
    reduce_scatter x3 -> x4, waiting for transfers between devices: 0.04 us -> 97.7 us  [paired_reduce(): own = lax.psum_scatter(near, ('z', 'y'), scatter_dimension=0, tiled=True)]
    unnamed x317 -> x305, local copies, waits for them, and re-layouts: 40.8 us -> 58.6 us
    ppermute x45 -> x28, starting transfers between devices: 47 us -> 31.1 us  [send(): return lax.ppermute(values, ('x', 'core', 'z', 'y'), pairs)]
    convert_element_type x11 -> x12, other arithmetic: 23 us -> 29.6 us  [add_low(): (left.astype(jnp.float32) + right.astype(jnp.float32)).astype(jnp.bfloat16)]
    another operation x16 -> x11, other arithmetic: 20.5 us -> 14.2 us
  transfers between devices with their start and end apart: 51 -> 36, of which waited for: 17 -> 15; matrix products, arithmetic and copies ran while one was open for 58% -> 28% of each run, Pallas kernels for 2% -> 1%
where the time goes in v5:
time: 923 us; the launch traced here: 917 us
  waiting for transfers between devices  414 us (45%)
  other arithmetic  160 us (17%)
  matrix products  145 us (16%)
  local copies, waits for them, and re-layouts  142 us (15%)
  starting transfers between devices  31.6 us (3%)
  between operations  16.3 us (2%)
    all_gather x4, waiting for transfers between devices, paired_gather(): lax.all_gather(part.astype(jnp.bfloat16), ('z', 'y', 'x'), axis=0, tiled=...  271 us
    reduce_scatter x4, waiting for transfers between devices, paired_reduce(): own = lax.psum_scatter(near, ('z', 'y'), scatter_dimension=0, tiled=True)  97.7 us
    unnamed x305, local copies, waits for them, and re-layouts  58.6 us
    ppermute x28, waiting for transfers between devices, send(): return lax.ppermute(values, ('x', 'core', 'z', 'y'), pairs)  44.9 us
    dot_general x3, matrix products, scan(): jnp.einsum('hts,shp->thp', mixing, scan_x, precision=None)  36.8 us
    dot_general x5, matrix products, dot_right(): lax.dot_general(left, right, (((1,), (1,)), ((), ())), preferred_element_...  35.8 us
    ppermute x28, starting transfers between devices, send(): return lax.ppermute(values, ('x', 'core', 'z', 'y'), pairs)  31.1 us
    convert_element_type x12, other arithmetic, add_low(): (left.astype(jnp.float32) + right.astype(jnp.float32)).astype(jnp.bfloat16)  29.6 us
  transfers between devices with their start and end apart: 36, of which 15 were waited for; matrix products, arithmetic and copies ran while one was open for 28% of the time, Pallas kernels for 1%

profile of v5, /device:TPU:1, one launch (start us, length us, event | category | flops | bytes accessed | tf_op | source)
XLA Modules:
  0.0 917.1 jit_solution(16358826413958275390)
XLA Ops:
  21.9 72.8 %all-gather.5.cloned.1.call-done.mine_ref = bf16[512,4224]{1,0:T(8,128)(2,1)} async-done(((bf16[32,4224]{1,0:T(8,128)(2,1)}), bf16[512,4224]{1,0:T(8,128)(2,1)}) %all-gather.5.cloned.1.call-update) | async-done | bytes 4325392 | tf_op jit(solution)/shard_map/all_gather | solution.py:281
  96.5 76.2 %all-gather.9.cloned.1.call-done.mine_ref = bf16[512,4096]{1,0:T(8,128)(2,1)} async-done(((bf16[32,4096]{1,0:T(8,128)(2,1)}), bf16[512,4096]{1,0:T(8,128)(2,1)}) %all-gather.9.cloned.1.call-update) | async-done | bytes 4194320 | tf_op jit(solution)/shard_map/all_gather | solution.py:281
  175.5 60.7 %all-gather.7.cloned.1.call-done.mine_ref = bf16[1024,1024]{1,0:T(8,128)(2,1)} async-done(((bf16[64,1024]{1,0:T(8,128)(2,1)}), bf16[1024,1024]{1,0:T(8,128)(2,1)}) %all-gather.7.cloned.1.call-update) | async-done | bytes 2097168 | tf_op jit(solution)/shard_map/all_gather | solution.py:281
  237.3 61.5 %all-gather.11.cloned.1.call-done.mine_ref = bf16[1024,1024]{1,0:T(8,128)(2,1)} async-done(((bf16[64,1024]{1,0:T(8,128)(2,1)}), bf16[1024,1024]{1,0:T(8,128)(2,1)}) %all-gather.11.cloned.1.call-update) | async-done | bytes 2097168 | tf_op jit(solution)/shard_map/all_gather | solution.py:281
  341.8 9.1 multiply_convert_fusion.2
  374.8 10.1 %multiply_convert_fusion = bf16[24,512,512]{2,1,0:T(8,128)(2,1)} fusion(f32[24,512]{1,0:T(8,128)} %copy.185, f32[24,512]{1,0:T(8,128)S(1)} %copy_bitcast_fusion.2, f32[512,512]{1,0:T(8,128)} %fusion.96, pred[512,512]{1,0:T(8,128)(4,1)S(1)} %copy-done.66), kind=kLoop, calls=%fused_computation.4 | loop fusion | flops 31457280 | bytes 13991936 | tf_op jit(solution)/shard_map/jvp()/convert_element_type | solution.py:35
  385.0 10.1 %bitcast_add_fusion.1 = f32[512,24,64]{0,2,1:T(8,128)} fusion(f32[512,24,64]{0,2,1:T(8,128)S(1)} %bitcast.289, bf16[512,24,64]{0,2,1:T(8,128)(2,1)S(1)} %bitcast.305, bf16[24,512,512]{2,1,0:T(8,128)(2,1)} %multiply_convert_fusion, f32[24]{0:T(128)S(1)} %get-tuple-element.218), kind=kOutput, calls=%fused_computation.87 | convolution fusion | flops 806879232 | bytes 20447328 | tf_op jit(solution)/shard_map/jvp(hts,shp->thp)/dot_general | solution.py:164
  411.1 7.4 fusion.137
  418.5 6.6 divide_convert_fusion
  439.2 10.8 %fusion.144 = f32[512,4096]{1,0:T(8,128)} fusion(bf16[512,1024]{1,0:T(8,128)(2,1)S(1)} %multiply_convert_fusion.4, bf16[1024,4096]{1,0:T(8,128)(2,1)} %copy-done), kind=kOutput, calls=%fused_computation.343 | convolution fusion | flops 4294967296 | bytes 17825792 | tf_op jit(solution)/shard_map/dot_general | solution.py:97
  450.0 6.6 fusion.73
  465.2 7.1 convolution_convert_fusion
  478.4 8.7 fusion.145.refs_0_
  512.6 7.4 fusion.71.refs_0_
  519.9 8.4 collective-permute-done.5
  582.6 9.7 %reduce-scatter.11.cloned.1.call-done = bf16[64,1024]{1,0:T(8,128)(2,1)} async-done(((bf16[512,1024]{1,0:T(8,128)(2,1)}), bf16[64,1024]{1,0:T(8,128)(2,1)}) %reduce-scatter.11.cloned.1.call-update) | async-done | bytes 131088 | tf_op jit(solution)/shard_map/reduce_scatter | solution.py:341
  596.2 10.7 %collective-permute-done.26 = bf16[64,1024]{1,0:T(8,128)(2,1)S(1)} collective-permute-done((bf16[64,1024]{1,0:T(8,128)(2,1)}, bf16[64,1024]{1,0:T(8,128)(2,1)S(1)}, u32[]{:S(2)}, u32[]{:S(2)}) %collective-permute-start.26) | collective-permute-done | bytes 131104 | tf_op jit(solution)/shard_map/ppermute | solution.py:221
  619.4 18.2 %fusion.3 = (f32[24,512]{1,0:T(8,128)S(1)}, f32[24,512]{1,0:T(8,128)S(1)}, f32[24,512]{1,0:T(8,128)S(1)}, bf16[512,512]{1,0:T(8,128)(2,1)}) fusion(f32[24,512]{1,0:T(8,128)S(1)} %copy-done.80, f32[24,512]{1,0:T(8,128)S(1)} %copy-done.78, f32[512,512]{1,0:T(8,128)S(1)} %copy-done.44, pred[512,512]{1,0:T(8,128)(4,1)S(1)} %copy-done.67, ...), kind=kOutput, calls=%fused_computation.8 | convolution fusion | flops 886796288 | bytes 5226496 | tf_op jit(solution)/shard_map/transpose(jvp(hts,shp->thp))/dot_general | solution.py:164
  637.6 8.5 bitcast_add_fusion
  672.4 10.0 %multiply_reduce_fusion.6 = (f32[1792]{0:T(1024)S(1)}, f32[1792]{0:T(1024)S(1)}, f32[1792]{0:T(1024)S(1)}, f32[1792]{0:T(1024)S(1)}, f32[1792]{0:T(1024)S(1)}, /*index=5*/f32[512,1792]{1,0:T(8,128)S(1)}) fusion(f32[509,1792]{1,0:T(8,128)} %slice.264, pred[512]{0:T(512)(128)(4,1)S(1)} %copy-done.129, f32[512,1920]{1,0:T(8,128)} %copy-done.10, ...), kind=kLoop, calls=%fused_computation.71 | loop fusion | flops 19258624 | bytes 25684480 | tf_op jit(solution)/shard_map/transpose(jvp())/reduce_sum | solution.py:146
  746.8 6.9 multiply_subtract_fusion.2
  760.4 20.2 %reduce-scatter.5.cloned.1.call-done = bf16[32,2304]{1,0:T(8,128)(2,1)} async-done(((bf16[256,2304]{1,0:T(8,128)(2,1)}), bf16[32,2304]{1,0:T(8,128)(2,1)}) %reduce-scatter.5.cloned.1.call-update) | async-done | bytes 147472 | tf_op jit(solution)/shard_map/reduce_scatter | solution.py:341
  784.9 67.8 %reduce-scatter.9.cloned.1.call-done = bf16[32,4096]{1,0:T(8,128)(2,1)} async-done(((bf16[256,4096]{1,0:T(8,128)(2,1)}), bf16[32,4096]{1,0:T(8,128)(2,1)}) %reduce-scatter.9.cloned.1.call-update) | async-done | bytes 262160 | tf_op jit(solution)/shard_map/reduce_scatter | solution.py:341
  869.4 11.6 %collective-permute-done.18 = bf16[48,1920]{1,0:T(8,128)(2,1)S(1)} collective-permute-done((bf16[48,1920]{1,0:T(8,128)(2,1)S(1)}, bf16[48,1920]{1,0:T(8,128)(2,1)S(1)}, u32[]{:S(2)}, u32[]{:S(2)}) %collective-permute-start.18) | collective-permute-done | bytes 184352 | tf_op jit(solution)/shard_map/ppermute | solution.py:221
  (602 shorter events, 373.7 us)
Async XLA Ops:
  7.2 87.5 %all-gather.5.cloned.1.call-start = ((), (), s32[]{:S(2)}) async-start(), calls=%async_computation.4 | async-start | bytes 4595712 | tf_op jit(solution)/shard_map/all_gather | solution.py:281
  16.6 156.2 %all-gather.9.cloned.1.call-start = ((), (), s32[]{:S(2)}) async-start(), calls=%async_computation.6 | async-start | bytes 4456448 | tf_op jit(solution)/shard_map/all_gather | solution.py:281
  18.4 217.7 %all-gather.7.cloned.1.call-start = ((), (), s32[]{:S(2)}) async-start(), calls=%async_computation.5 | async-start | bytes 2228224 | tf_op jit(solution)/shard_map/all_gather | solution.py:281
  20.1 278.6 %all-gather.11.cloned.1.call-start = ((), (), s32[]{:S(2)}) async-start(), calls=%async_computation.7 | async-start | bytes 2228224 | tf_op jit(solution)/shard_map/all_gather | solution.py:281
  21.8 570.5 %reduce-scatter.11.cloned.1.call-start = ((), (), s32[]{:S(2)}) async-start(), calls=%async_computation.11 | async-start | bytes 1179648 | tf_op jit(solution)/shard_map/reduce_scatter | solution.py:341
  94.7 226.1 %collective-permute-start = (bf16[512,4224]{1,0:T(8,128)(2,1)}, bf16[512,4224]{1,0:T(8,128)(2,1)}, u32[]{:S(2)}, u32[]{:S(2)}) collective-permute-start(bf16[512,4224]{1,0:T(8,128)(2,1)} %all-gather.5.cloned.1.call-done.mine_ref), channel_id=1, source_target_pairs={{0,8},{1,9},{2,10},{3,11},{4,12},{5,13},{6,14},{7,15},{8,0},{9,1},... | collective-permute-start | bytes 12976136 | tf_op jit(solution)/shard_map/ppermute | solution.py:221
  172.7 141.9 %collective-permute-start.2 = (bf16[512,4096]{1,0:T(8,128)(2,1)}, bf16[512,4096]{1,0:T(8,128)(2,1)}, u32[]{:S(2)}, u32[]{:S(2)}) collective-permute-start(bf16[512,4096]{1,0:T(8,128)(2,1)} %all-gather.9.cloned.1.call-done.mine_ref), channel_id=1, source_target_pairs={{0,8},{1,9},{2,10},{3,11},{4,12},{5,13},{6,14},{7,15},{8,0},{9,1},... | collective-permute-start | bytes 12582920 | tf_op jit(solution)/shard_map/ppermute | solution.py:221
  236.2 70.1 %collective-permute-start.1 = (bf16[1024,1024]{1,0:T(8,128)(2,1)}, bf16[1024,1024]{1,0:T(8,128)(2,1)S(1)}, u32[]{:S(2)}, u32[]{:S(2)}) collective-permute-start(bf16[1024,1024]{1,0:T(8,128)(2,1)} %all-gather.7.cloned.1.call-done.mine_ref), channel_id=1, source_target_pairs={{0,8},{1,9},{2,10},{3,11},{4,12},{5,13},{6,14},{7,15},{8,0},{9,1},... | collective-permute-start | bytes 6291464 | tf_op jit(solution)/shard_map/ppermute | solution.py:221
  462.6 24.5 %collective-permute-start.4 = (bf16[8,128,1024]{2,1,0:T(8,128)(2,1)}, bf16[8,128,1024]{2,1,0:T(8,128)(2,1)}, u32[]{:S(2)}, u32[]{:S(2)}) collective-permute-start(bf16[8,128,1024]{2,1,0:T(8,128)(2,1)} %dynamic-slice_bitcast_fusion.4.refs_1_), channel_id=1, source_target_pairs={{0,8},{1,9},{2,10},{3,11},{4,12},{5,13},{6,14},{7,15},{8,0},{9,1},... | collective-permute-start | bytes 6291464 | tf_op jit(solution)/shard_map/ppermute | solution.py:221
  477.9 58.6 %collective-permute-start.6 = (bf16[8,64,4096]{2,1,0:T(8,128)(2,1)}, bf16[8,64,4096]{2,1,0:T(8,128)(2,1)}, u32[]{:S(2)}, u32[]{:S(2)}) collective-permute-start(bf16[8,64,4096]{2,1,0:T(8,128)(2,1)} %dynamic-slice_bitcast_fusion.refs_2_), channel_id=1, source_target_pairs={{0,8},{1,9},{2,10},{3,11},{4,12},{5,13},{6,14},{7,15},{8,0},{9,1},... | collective-permute-start | bytes 12582920 | tf_op jit(solution)/shard_map/ppermute | solution.py:221
  503.8 27.2 %collective-permute-start.8 = (bf16[8,128,1024]{2,1,0:T(8,128)(2,1)}, bf16[8,128,1024]{2,1,0:T(8,128)(2,1)}, u32[]{:S(2)}, u32[]{:S(2)}) collective-permute-start(bf16[8,128,1024]{2,1,0:T(8,128)(2,1)} %dynamic-slice_bitcast_fusion.2.refs_3_), channel_id=1, source_target_pairs={{0,8},{1,9},{2,10},{3,11},{4,12},{5,13},{6,14},{7,15},{8,0},{9,1},... | collective-permute-start | bytes 6291464 | tf_op jit(solution)/shard_map/ppermute | solution.py:221
  503.8 24.5 %collective-permute-start.5 = (bf16[8,64,1024]{2,1,0:T(8,128)(2,1)}, bf16[8,64,1024]{2,1,0:T(8,128)(2,1)}, u32[]{:S(2)}, u32[]{:S(2)}) collective-permute-start(bf16[8,64,1024]{2,1,0:T(8,128)(2,1)} %dynamic-slice_bitcast_fusion.7.refs_1_), channel_id=1, source_target_pairs={{0,16},{1,17},{2,18},{3,19},{4,20},{5,21},{6,22},{7,23},{8,24},{9,... | collective-permute-start | bytes 3145736 | tf_op jit(solution)/shard_map/ppermute | solution.py:221
  530.9 157.5 %reduce-scatter.7.cloned.1.call-start = ((), (), s32[]{:S(2)}) async-start(), calls=%async_computation.9 | async-start | bytes 1179648 | tf_op jit(solution)/shard_map/reduce_scatter | solution.py:341
  535.5 58.0 %collective-permute-start.9 = (bf16[8,64,1024]{2,1,0:T(8,128)(2,1)}, bf16[8,64,1024]{2,1,0:T(8,128)(2,1)}, u32[]{:S(2)}, u32[]{:S(2)}) collective-permute-start(bf16[8,64,1024]{2,1,0:T(8,128)(2,1)} %dynamic-slice_bitcast_fusion.6.refs_2_), channel_id=1, source_target_pairs={{0,16},{1,17},{2,18},{3,19},{4,20},{5,21},{6,22},{7,23},{8,24},{9,... | collective-permute-start | bytes 3145736 | tf_op jit(solution)/shard_map/ppermute | solution.py:221
  545.1 65.4 %collective-permute-start.7 = (bf16[8,32,4096]{2,1,0:T(8,128)(2,1)}, bf16[8,32,4096]{2,1,0:T(8,128)(2,1)}, u32[]{:S(2)}, u32[]{:S(2)}) collective-permute-start(bf16[8,32,4096]{2,1,0:T(8,128)(2,1)} %dynamic-slice_bitcast_fusion.3.refs_2_), channel_id=1, source_target_pairs={{0,16},{1,17},{2,18},{3,19},{4,20},{5,21},{6,22},{7,23},{8,24},{9,... | collective-permute-start | bytes 6291464 | tf_op jit(solution)/shard_map/ppermute | solution.py:221
  580.8 87.4 %collective-permute-start.10 = (bf16[8,64,2304]{2,1,0:T(8,128)(2,1)}, bf16[8,64,2304]{2,1,0:T(8,128)(2,1)}, u32[]{:S(2)}, u32[]{:S(2)}) collective-permute-start(bf16[8,64,2304]{2,1,0:T(8,128)(2,1)} %dynamic-slice_bitcast_fusion.1.refs_3_), channel_id=1, source_target_pairs={{0,8},{1,9},{2,10},{3,11},{4,12},{5,13},{6,14},{7,15},{8,0},{9,1},... | collective-permute-start | bytes 7077896 | tf_op jit(solution)/shard_map/ppermute | solution.py:221
  596.1 184.5 %reduce-scatter.5.cloned.1.call-start = ((), (), s32[]{:S(2)}) async-start(), calls=%async_computation.8 | async-start | bytes 1327104 | tf_op jit(solution)/shard_map/reduce_scatter | solution.py:341
  608.3 135.5 %collective-permute-start.27 = (bf16[128,1024]{1,0:T(8,128)(2,1)}, bf16[128,1024]{1,0:T(8,128)(2,1)}, u32[]{:S(2)}, u32[]{:S(2)}) collective-permute-start(bf16[128,1024]{1,0:T(8,128)(2,1)} %pad_maximum_fusion.17), channel_id=1, source_target_pairs={{0,8},{1,9},{2,10},{3,11},{4,12},{5,13},{6,14},{7,15},{8,0},{9,1},... | collective-permute-start | bytes 786440 | tf_op jit(solution)/shard_map/ppermute | solution.py:221
  671.3 33.7 %collective-permute-start.11 = (bf16[8,32,2304]{2,1,0:T(8,128)(2,1)S(1)}, bf16[8,32,2304]{2,1,0:T(8,128)(2,1)}, u32[]{:S(2)}, u32[]{:S(2)}) collective-permute-start(bf16[8,32,2304]{2,1,0:T(8,128)(2,1)S(1)} %dynamic-slice_bitcast_fusion.5.refs_2_), channel_id=1, source_target_pairs={{0,16},{1,17},{2,18},{3,19},{4,20},{5,21},{6,22},{7,23},{8,24},{9,... | collective-permute-start | bytes 3538952 | tf_op jit(solution)/shard_map/ppermute | solution.py:221
  704.1 41.5 %collective-permute-start.23 = (bf16[128,1024]{1,0:T(8,128)(2,1)}, bf16[128,1024]{1,0:T(8,128)(2,1)}, u32[]{:S(2)}, u32[]{:S(2)}) collective-permute-start(bf16[128,1024]{1,0:T(8,128)(2,1)} %pad_maximum_fusion.16), channel_id=1, source_target_pairs={{0,8},{1,9},{2,10},{3,11},{4,12},{5,13},{6,14},{7,15},{8,0},{9,1},... | collective-permute-start | bytes 786440 | tf_op jit(solution)/shard_map/ppermute | solution.py:221
  719.8 132.9 %reduce-scatter.9.cloned.1.call-start = ((), (), s32[]{:S(2)}) async-start(), calls=%async_computation.10 | async-start | bytes 2359296 | tf_op jit(solution)/shard_map/reduce_scatter | solution.py:341
  757.3 24.5 %collective-permute-start.15 = (bf16[4,2,16,1920]{3,2,0,1:T(8,128)(2,1)S(1)}, bf16[4,2,16,1920]{3,2,0,1:T(8,128)(2,1)}, u32[]{:S(2)}, u32[]{:S(2)}) collective-permute-start(bf16[4,2,16,1920]{3,2,0,1:T(8,128)(2,1)S(1)} %constant_dynamic-slice_fusion), channel_id=1, source_target_pairs={{0,16},{1,17},{2,18},{3,19},{4,20},{5,21},{6,22},{7,23},{8,24},{9,... | collective-permute-start | bytes 1474568 | tf_op jit(solution)/shard_map/ppermute | solution.py:221
  783.1 79.6 %collective-permute-start.16 = (bf16[4,48,1920]{2,1,0:T(8,128)(2,1)S(1)}, bf16[4,48,1920]{2,1,0:T(8,128)(2,1)S(1)}, u32[]{:S(2)}, u32[]{:S(2)}) collective-permute-start(bf16[4,48,1920]{2,1,0:T(8,128)(2,1)S(1)} %pad_maximum_fusion.10), channel_id=1, source_target_pairs={{0,1},{1,0},{2,3},{3,2},{4,5},{5,4},{6,7},{7,6},{8,9},{9,8},{10,11... | collective-permute-start | bytes 2211848 | tf_op jit(solution)/shard_map/ppermute | solution.py:221
  860.0 22.4 %collective-permute-start.25 = (bf16[64,4096]{1,0:T(8,128)(2,1)S(1)}, bf16[64,4096]{1,0:T(8,128)(2,1)S(1)}, u32[]{:S(2)}, u32[]{:S(2)}) collective-permute-start(bf16[64,4096]{1,0:T(8,128)(2,1)S(1)} %pad_maximum_fusion.13), channel_id=1, source_target_pairs={{0,8},{1,9},{2,10},{3,11},{4,12},{5,13},{6,14},{7,15},{8,0},{9,1},... | collective-permute-start | bytes 1572872 | tf_op jit(solution)/shard_map/ppermute | solution.py:221
  (162 other events, 1953.7 us)
Sparse Core Ops, SparseCore 0:
  16.7 77.9 all-gather.4
  98.1 74.6 all-gather.8
  176.1 60.0 all-gather.6
  239.4 59.3 all-gather.10
  531.1 61.1 reduce-scatter.10
  596.5 62.3 reduce-scatter.6
  719.9 60.7 reduce-scatter.4
  784.8 67.8 reduce-scatter.8

commit v6 on v4

--- a/solution.py
+++ b/solution.py
@@ -1,4 +1,5 @@
 import functools
+import math
 
 import jax
 import jax.numpy as jnp
@@ -189,6 +190,7 @@
 GATE = MH * MP
 CONV = MH * MP + 2 * NS
 STEP_LANES = 128
+MERGED = (("down", "up"), ("out", "side"))
 
 
 def general_gather(own, rep, shard):
@@ -283,7 +285,7 @@
 
 def tuned_gather(pieces):
     x, core, z, y = place()
-    results, after = [], None
+    results, after, held = [], None, None
     for own in pieces:
         rows = own.shape[0]
         quarter = rows // 8
@@ -300,7 +302,63 @@
         held += [send(group[:, :quarter], dx=1) for group in held]
         held += [send(group, dcore=1) for group in held]
         results.append(assemble(held, rows))
-    return results
+    return results, held
+
+
+def slabs(matrix, width=D):
+    blocks = [matrix[..., start : start + width] for start in range(0, matrix.shape[-1], width)]
+    return jnp.concatenate(blocks, axis=-2)
+
+
+def merged_gather(masters):
+    x, core, z, y = place()
+    parts = []
+    for master in masters:
+        rows = master.shape[0] // 4
+        part = lax.dynamic_slice_in_dim(master, (core * 2 + x) * rows, rows, 0)
+        parts.append(slabs(part.astype(jnp.bfloat16)))
+    own = jnp.concatenate(parts, axis=0)
+    return lax.all_gather(own, ("z", "y", "x"), axis=0, tiled=True)
+
+
+def merged_place(mine, shapes):
+    beside = send(mine, dcore=1)
+    total = mine.shape[0] // 16
+
+    def kernel(mine_ref, beside_ref, *refs):
+        targets, sems = refs[:-1], refs[-1]
+        core = lax.axis_index("core")
+        copies = []
+        for source, which in ((mine_ref, core), (beside_ref, 1 - core)):
+            start = 0
+            for target, (rows, columns) in zip(targets, shapes):
+                for column in range(0, columns, D):
+                    copies.append(
+                        pltpu.make_async_copy(
+                            source.at[:, :, pl.ds(start, rows)],
+                            target.at[:, which, :, :, pl.ds(column, D)],
+                            sems.at[len(copies)],
+                        )
+                    )
+                    start += rows
+        for copy in copies:
+            copy.start()
+        for copy in copies:
+            copy.wait()
+
+    count = 2 * sum(columns // D for _, columns in shapes)
+    placed = pl.pallas_call(
+        kernel,
+        out_shape=[
+            jax.ShapeDtypeStruct((8, 2, 2, rows, columns), jnp.bfloat16) for rows, columns in shapes
+        ],
+        in_specs=[pl.BlockSpec(memory_space=pl.ANY)] * 2,
+        out_specs=[pl.BlockSpec(memory_space=pltpu.VMEM)] * len(shapes),
+        scratch_shapes=[pltpu.SemaphoreType.DMA((count,))],
+        compiler_params=pltpu.CompilerParams(vmem_limit_bytes=40 * 1024 * 1024),
+        name="merged_place",
+    )(mine.reshape(8, 2, total, D), beside.reshape(8, 2, total, D))
+    return [array.reshape(-1, array.shape[-1]) for array in placed]
 
 
 def add_low(left, right):
@@ -347,25 +405,50 @@
     )
 
 
-def paired_reduce(grad):
+def swap_parts(own, late):
+    x, core, z, y = place()
+    (own,) = fence([own], late)
+    across = send(own, dx=1)
+    owned = jnp.concatenate(
+        [jnp.where(x == 0, own, across), jnp.where(x == 0, across, own)], axis=0
+    )
+    beside = send(owned, dcore=1)
+    return jnp.concatenate(
+        [jnp.where(core == 0, owned, beside), jnp.where(core == 0, beside, owned)], axis=0
+    )
+
+
+def quarter_sum(grad):
     rows, columns = grad.shape[0] // 8, grad.shape[1]
     x, core, z, y = place()
     parts = grad.reshape(8, 2, rows // 2, columns)
     far = pick(parts, 1 - core, 1)
     yield [far]
-    half = add_low(pick(parts, core, 1), send(far, dcore=1)).reshape(4 * rows, columns)
-    yield [half]
-    own = lax.psum_scatter(half, ("z", "y", "x"), scatter_dimension=0, tiled=True)
+    half = add_low(pick(parts, core, 1), send(far, dcore=1))
+    parts = half.reshape(8, 2, rows // 4, columns)
+    far = pick(parts, 1 - x, 1)
+    yield [far]
+    return add_low(pick(parts, x, 1), send(far, dx=1))
+
+
+def merged_reduce(nears, late):
+    width = math.gcd(*(near.shape[-1] for near in nears))
+    every = jnp.concatenate([slabs(near, width) for near in nears], axis=1)
+    yield [every]
+    own = lax.psum_scatter(every.reshape(-1, width), ("z", "y"), scatter_dimension=0, tiled=True)
+    yield []
+    yield [own]
     yield None
-    across = send(own, dx=1)
-    owned = jnp.concatenate(
-        [jnp.where(x == 0, own, across), jnp.where(x == 0, across, own)], axis=0
-    )
-    yield None
-    beside = send(owned, dcore=1)
-    return jnp.concatenate(
-        [jnp.where(core == 0, owned, beside), jnp.where(core == 0, beside, owned)], axis=0
-    )
+    (own,) = fence([own], late)
+    results, start = [], 0
+    for near in nears:
+        rows, columns = near.shape[1:]
+        blocks = []
+        for _ in range(0, columns, width):
+            blocks.append(own[start : start + rows])
+            start += rows
+        results.append(swap_parts(jnp.concatenate(blocks, axis=1), late))
+    return results
 
 
 def general_stages(grad, rep, shard):
@@ -377,27 +460,26 @@
 
     def __init__(self, axes):
         self.axes = axes
-        self.running, self.results, self.waiting = {}, {}, {}
-
-    def add(self, name, grad, paired=False):
+        self.running, self.results, self.waiting, self.late = {}, {}, {}, []
+
+    def add(self, name, grad, how="chain"):
         grad = grad.astype(jnp.bfloat16)
         if not tuned(self.axes):
             self.running[name] = general_stages(grad, *self.axes)
-        elif paired:
-            self.running[name] = paired_reduce(grad)
+        elif how == "chain":
+            self.running[name] = tuned_reduce(grad)
         else:
-            self.running[name] = tuned_reduce(grad)
+            self.running[name] = quarter_sum(grad)
 
     def step(self, values):
         after = []
         for name in list(self.running):
-            if self.waiting.get(name):
-                continue
-            ready = self.advance(name)
-            if ready is None:
-                self.waiting[name] = True
-            else:
-                after += ready
+            if not self.waiting.get(name):
+                ready = self.advance(name)
+                if ready is None:
+                    self.waiting[name] = True
+                else:
+                    after += ready
         return fence(values, after) if after else values
 
     def advance(self, name):
@@ -406,12 +488,21 @@
         except StopIteration as stop:
             self.results[name] = stop.value
             del self.running[name]
-            return []
-
-    def finish(self):
+        for group in MERGED:
+            if tuned(self.axes) and name in group and all(n in self.results for n in group):
+                nears = [self.results.pop(n) for n in group]
+                self.running[group] = merged_reduce(nears, self.late)
+                return self.advance(group)
+        return []
+
+    def finish(self, late):
+        self.late += late
         while self.running:
             for name in list(self.running):
                 self.advance(name)
+        for group in MERGED:
+            if group in self.results:
+                self.results.update(zip(group, self.results[group]))
         return self.results
 
 
@@ -436,16 +527,19 @@
     )
     pieces = [conv_piece, low_in[:, : QKV + GATE]]
     if tuned(axes):
-        pieces = tuned_gather(pieces)
+        pieces, held = tuned_gather(pieces)
     else:
         pieces = [general_gather(piece, rep, shard) for piece in pieces]
-    for master in (mixer_out, swiglu_in, swiglu_out):
-        pieces.append(general_gather(master.astype(jnp.bfloat16), rep, shard))
+    masters = (mixer_out, swiglu_in, swiglu_out)
+    if tuned(axes):
+        others = [merged_gather(masters), [(m.shape[0] // 4, m.shape[1]) for m in masters], held]
+    else:
+        others = [general_gather(master.astype(jnp.bfloat16), rep, shard) for master in masters]
     every = pieces[0][:, CONV + MH : CONV + MH + lanes].reshape(owners, rows * lanes)
     gains_all = every[:, : gains.shape[0]].reshape(-1)
     taps = every[:, gains.shape[0] : count].reshape(owners, KC + 1, width)
     taps = jnp.swapaxes(taps, 0, 1).reshape(KC + 1, owners * width)
-    return pieces + [gains_all.astype(jnp.float32), taps.astype(jnp.float32)]
+    return pieces + [gains_all.astype(jnp.float32), taps.astype(jnp.float32), others]
 
 
 def with_vectors(conv_g, gains_g, taps_g, head_grad, owners):
@@ -482,7 +576,7 @@
 
 def forward_backward(axes, tokens, cotangent, seq_row, weights, head_params):
     low, low_back = make_rounders()
-    w_conv, w_side, w_out, w_up, w_down, gain_all, taps = weights
+    w_conv, w_side, gain_all, taps, others = weights
     segment, token_position, valid = layout(seq_row, tokens.shape[0])
     values = tokens.astype(jnp.float32)
     context_width = QUERY_HEADS * HEAD_SIZE
@@ -490,15 +584,21 @@
     normed, pull_norm = jax.vjp(lambda v, g: low(normalize(v, g)), values, gain_all[:D])
     normed_low = rows_of(normed)
     projected = dot(normed_low, w_conv)
+    if tuned(axes):
+        (projected,) = fence([projected], others[2][:1])
     conv_out, pull_conv = jax.vjp(
         lambda p, k: convolution(p, k, segment, low), projected[:, :CONV], taps
     )
+    if tuned(axes):
+        (conv_out,) = fence([conv_out], others[2][1:3])
     scan_out, pull_scan = jax.vjp(
         lambda c, r, h: scan(c, r, h, segment, low, low_back),
         conv_out,
         projected[:, CONV : CONV + MH],
         head_params,
     )
+    if tuned(axes):
+        (scan_out,) = fence([scan_out], others[2][4:])
     beside = dot(normed_low, w_side)
     context, pull_context = jax.vjp(
         lambda p: attention(p, segment, token_position, low, low_back), beside[:, :QKV]
@@ -506,6 +606,10 @@
     mamba_out, pull_gating = jax.vjp(
         lambda s, z, g: gating(s, z, g, low), scan_out, beside[:, QKV:], gain_all[2 * D :]
     )
+    if tuned(axes):
+        (gathered,) = fence([others[0]], [scan_out])
+        others = merged_place(gathered, others[1])
+    w_out, w_up, w_down = others
     joined = jnp.concatenate([rows_of(context), rows_of(mamba_out)], axis=1)
     hidden = values + dot(joined, w_out)
     normed_ff, pull_ff = jax.vjp(lambda v, g: low(normalize(v, g)), hidden, gain_all[D : 2 * D])
@@ -518,19 +622,19 @@
     cot = jnp.where(valid[:, None], cotangent, jnp.zeros_like(cotangent))
     (up_cot,) = pull_active(dot_right(cot, w_down))
     up_cot = rows_of(up_cot)
-    moving.add("down", dot_left(activated_low, cot), paired=True)
+    moving.add("down", dot_left(activated_low, cot), "part")
     (up_cot,) = moving.step([up_cot])
-    moving.add("up", dot_left(normed_ff_low, up_cot), paired=True)
+    moving.add("up", dot_left(normed_ff_low, up_cot), "part")
     (ff_cot,) = moving.step([dot_right(up_cot, w_up)])
     hidden_part, gain_ff = pull_ff(ff_cot)
     hidden_cot = cot.astype(jnp.float32) + hidden_part
     hidden_low = rows_of(hidden_cot)
-    moving.add("out", dot_left(joined, hidden_low), paired=True)
+    moving.add("out", dot_left(joined, hidden_low), "part")
     (joined_cot,) = moving.step([dot_right(hidden_low, w_out)])
     scan_cot, gate_cot, gain_scan = pull_gating(joined_cot[:, context_width:])
     (qkv_cot,) = pull_context(joined_cot[:, :context_width])
     side_cot = jnp.concatenate([rows_of(qkv_cot), rows_of(gate_cot)], axis=1)
-    moving.add("side", dot_left(normed_low, side_cot))
+    moving.add("side", dot_left(normed_low, side_cot), "part")
     (scan_cot,) = moving.step([scan_cot])
     conv_out_cot, step_cot, head_grad = pull_scan(scan_cot)
     (conv_out_cot,) = moving.step([conv_out_cot])
@@ -546,11 +650,11 @@
     token_grad = hidden_cot + tokens_part
     gains_grad = jnp.concatenate([gain_in, gain_ff, gain_scan])
     owners = lax.axis_size(axes[1])
-    moving.add(
-        "conv",
-        with_vectors(dot_left(normed_low, conv_cot), gains_grad, taps_grad, head_grad, owners),
-    )
-    return output, token_grad, moving.finish()
+    conv_grad = rows_of(
+        with_vectors(dot_left(normed_low, conv_cot), gains_grad, taps_grad, head_grad, owners)
+    )
+    moving.add("conv", conv_grad)
+    return output, token_grad, moving.finish([conv_grad])
 
 
 def on_device(

time: 652 us -> 777 us (1.19)
  waiting for transfers between devices: 148 us -> 214 us
  local copies, waits for them, and re-layouts: 118 us -> 160 us
  starting transfers between devices: 47.2 us -> 67.4 us
  matrix products: 147 us -> 133 us
  Pallas kernels: 9.97 us -> 18.8 us
    reduce_scatter x3 -> x2, waiting for transfers between devices: 0.04 us -> 60 us  [merged_reduce(): lax.psum_scatter(every.reshape(-1, width), ('z', 'y'), scatter_dimension=...]
    unnamed x317 -> x386, local copies, waits for them, and re-layouts: 40.8 us -> 76.3 us
    ppermute x45, starting transfers between devices: 47 us -> 67.3 us  [send(): return lax.ppermute(values, ('x', 'core', 'z', 'y'), pairs)]
    dot_general x5, matrix products: 31.6 us -> 21.6 us  [dot(): return jnp.dot(left, right, preferred_element_type=jnp.float32)]
    pallas_call x0 -> x1, Pallas kernels: none -> 9.43 us  [merged_place(): pl.pallas_call(kernel, out_shape=[jax.ShapeDtypeStruct((8, 2, 2, rows, co...]
    sub x6 -> x7, other arithmetic: 17.8 us -> 16.4 us  [adamw(): return (weight - rate * (corrected + DECAY * weight), mean_new, square_new)]
  transfers between devices with their start and end apart: 51 -> 48, of which waited for: 17 -> 18; matrix products, arithmetic and copies ran while one was open for 58% -> 47% of each run, Pallas kernels for 2% -> 1%
where the time goes in v6:
time: 777 us; the launch traced here: 771 us
  waiting for transfers between devices  214 us (28%)
  other arithmetic  161 us (21%)
  local copies, waits for them, and re-layouts  160 us (21%)
  matrix products  133 us (17%)
  starting transfers between devices  67.4 us (9%)
  Pallas kernels  18.8 us (2%)
  between operations  16.3 us (2%)
    ppermute x45, waiting for transfers between devices, send(): return lax.ppermute(values, ('x', 'core', 'z', 'y'), pairs)  154 us
    unnamed x386, local copies, waits for them, and re-layouts  76.3 us
    ppermute x45, starting transfers between devices, send(): return lax.ppermute(values, ('x', 'core', 'z', 'y'), pairs)  67.3 us
    reduce_scatter x2, waiting for transfers between devices, merged_reduce(): lax.psum_scatter(every.reshape(-1, width), ('z', 'y'), scatter_dimension=...  60 us
    dot_general x3, matrix products, scan(): jnp.einsum('hts,shp->thp', mixing, scan_x, precision=None)  40 us
    convert_element_type x6, other arithmetic, round_value(): values.astype(jnp.bfloat16)  26.9 us
    dot_general x5, matrix products, dot_right(): lax.dot_general(left, right, (((1,), (1,)), ((), ())), preferred_element_...  26.4 us
    dot_general x5, matrix products, dot(): return jnp.dot(left, right, preferred_element_type=jnp.float32)  21.6 us
  transfers between devices with their start and end apart: 48, of which 18 were waited for; matrix products, arithmetic and copies ran while one was open for 47% of the time, Pallas kernels for 1%

profile of v6, /device:TPU:1, one launch (start us, length us, event | category | flops | bytes accessed | tf_op | source)
XLA Modules:
  0.0 770.7 jit_solution(8729695456609532453)
XLA Ops:
  31.3 15.9 %collective-permute-done.1.refs_2_ = bf16[48,1920]{1,0:T(8,128)(2,1)S(1)} collective-permute-done((bf16[48,1920]{1,0:T(8,128)(2,1)S(1)}, bf16[48,1920]{1,0:T(8,128)(2,1)S(1)}, u32[]{:S(2)}, u32[]{:S(2)}) %collective-permute-start.1) | collective-permute-done | bytes 184352 | tf_op jit(solution)/shard_map/ppermute | solution.py:223
  49.1 7.3 collective-permute-start.11
  60.4 34.8 %collective-permute-done.11 = bf16[48,2304]{1,0:T(8,128)(2,1)S(1)} collective-permute-done((bf16[48,2304]{1,0:T(8,128)(2,1)}, bf16[48,2304]{1,0:T(8,128)(2,1)S(1)}, u32[]{:S(2)}, u32[]{:S(2)}) %collective-permute-start.11) | collective-permute-done | bytes 221216 | tf_op jit(solution)/shard_map/ppermute | solution.py:223
  115.0 9.6 %collective-permute-done.5.refs_3_ = bf16[4,16,1920]{2,1,0:T(8,128)(2,1)} collective-permute-done((bf16[4,16,1920]{2,1,0:T(8,128)(2,1)S(1)}, bf16[4,16,1920]{2,1,0:T(8,128)(2,1)}, u32[]{:S(2)}, u32[]{:S(2)}) %collective-permute-start.5) | collective-permute-done | bytes 245792 | tf_op jit(solution)/shard_map/ppermute | solution.py:223
  126.1 7.7 %collective-permute-start.9 = (bf16[4,16,1920]{2,1,0:T(8,128)(2,1)}, bf16[4,16,1920]{2,1,0:T(8,128)(2,1)}, u32[]{:S(2)}, u32[]{:S(2)}) collective-permute-start(bf16[4,16,1920]{2,1,0:T(8,128)(2,1)} %collective-permute-done.5.refs_3_), channel_id=1, source_target_pairs={{0,8},{1,9},{2,10},{3,11},{4,12},{5,13},{6,14},{7,15},{8,0},{9,1},... | collective-permute-start | bytes 737288 | tf_op jit(solution)/shard_map/ppermute | solution.py:223
  142.3 10.2 %collective-permute-done.15.refs_3_ = bf16[4,16,2304]{2,1,0:T(8,128)(2,1)} collective-permute-done((bf16[4,16,2304]{2,1,0:T(8,128)(2,1)}, bf16[4,16,2304]{2,1,0:T(8,128)(2,1)}, u32[]{:S(2)}, u32[]{:S(2)}) %collective-permute-start.15) | collective-permute-done | bytes 294944 | tf_op jit(solution)/shard_map/ppermute | solution.py:223
  181.1 8.9 %multiply_convert_fusion.2 = (bf16[512,1792]{1,0:T(8,128)(2,1)S(1)}, f32[512,1792]{1,0:T(8,128)}) fusion(f32[509,1792]{1,0:T(8,128)} %slice.444, pred[512]{0:T(512)(128)(4,1)S(1)} %get-tuple-element.231, f32[1792]{0:T(1024)S(1)} %mul.826, f32[510,1792]{1,0:T(8,128)} %slice.442, pred[512]{0:T(512)(128)(4,1)S(1)} %get-tuple-element.230, f32[1792]{0:T(1024)S(1)} %mul.823, ...), kind=kLoop, calls=%fused_computation.75 | loop fusion | flops 14680064 | bytes 20179456 | tf_op jit(solution)/shard_map/jvp()/convert_element_type | solution.py:36
  196.3 8.2 %multiply_convert_fusion = bf16[24,512,512]{2,1,0:T(8,128)(2,1)} fusion(f32[24,512]{1,0:T(8,128)S(1)} %copy.182, f32[24,512]{1,0:T(8,128)S(1)} %copy_bitcast_fusion, f32[512,512]{1,0:T(8,128)S(1)} %fusion.89, pred[512,512]{1,0:T(8,128)(4,1)S(1)} %copy-done.76), kind=kLoop, calls=%fused_computation.4 | loop fusion | flops 31457280 | bytes 13991936 | tf_op jit(solution)/shard_map/jvp()/convert_element_type | solution.py:36
  210.3 11.9 %bitcast_add_fusion.1 = f32[512,24,64]{0,2,1:T(8,128)} fusion(f32[512,24,64]{0,2,1:T(8,128)} %bitcast.304, bf16[24,512,512]{2,1,0:T(8,128)(2,1)} %multiply_convert_fusion, f32[24]{0:T(128)S(1)} %get-tuple-element.226), kind=kOutput, calls=%fused_computation.88 | convolution fusion | flops 806879232 | bytes 18874464 | tf_op jit(solution)/shard_map/jvp(hts,shp->thp)/dot_general | solution.py:165
  257.7 7.5 fusion.147
  277.8 9.4 %merged_place.1 = (bf16[8,2,2,64,1024]{4,3,2,1,0:T(8,128)(2,1)S(1)}, bf16[8,2,2,32,4096]{4,3,2,1,0:T(8,128)(2,1)}, bf16[8,2,2,64,1024]{4,3,2,1,0:T(8,128)(2,1)S(1)}) custom-call(bf16[8,2,256,1024]{3,2,1,0:T(8,128)(2,1)} %bitcast.297, bf16[8,2,256,1024]{3,2,1,0:T(8,128)(2,1)} %bitcast.35.beside_ref), custom_call_target="tpu_custom_call" | custom-call | tf_op jit(solution)/shard_map/merged_place/pallas_call | solution.py:350
  294.7 6.9 fusion.154
  317.1 7.1 convolution_convert_fusion
  335.8 8.8 %fusion.155.refs_0_ = f32[512,1024]{1,0:T(8,128)} fusion(bf16[512,4096]{1,0:T(8,128)(2,1)S(1)} %copy-done.33, bf16[1024,4096]{1,0:T(8,128)(2,1)} %bitcast.354), kind=kOutput, calls=%fused_computation.390 | convolution fusion | flops 4294967296 | bytes 14680064 | tf_op jit(solution)/shard_map/dot_general | solution.py:106
  368.0 6.9 collective-permute-done.23
  431.9 22.1 %collective-permute-done.27 = bf16[8,64,1024]{2,1,0:T(8,128)(2,1)} collective-permute-done((bf16[8,64,1024]{2,1,0:T(8,128)(2,1)S(1)}, bf16[8,64,1024]{2,1,0:T(8,128)(2,1)}, u32[]{:S(2)}, u32[]{:S(2)}) %collective-permute-start.27) | collective-permute-done | bytes 1048608 | tf_op jit(solution)/shard_map/ppermute | solution.py:223
  469.4 19.6 %fusion.3 = (f32[24,512]{1,0:T(8,128)S(1)}, f32[24,512]{1,0:T(8,128)S(1)}, f32[24,512]{1,0:T(8,128)S(1)}, bf16[512,512]{1,0:T(8,128)(2,1)}) fusion(f32[24,512]{1,0:T(8,128)S(1)} %copy-done.105, f32[24,512]{1,0:T(8,128)S(1)} %copy-done.101, f32[512,512]{1,0:T(8,128)S(1)} %copy-done.57, pred[512,512]{1,0:T(8,128)(4,1)S(1)} %copy-done.77, ...), kind=kOutput, calls=%fused_computation.8 | convolution fusion | flops 886796288 | bytes 6799360 | tf_op jit(solution)/shard_map/transpose(jvp(hts,shp->thp))/dot_general | solution.py:165
  489.0 8.4 %bitcast_add_fusion = f32[512,24,64]{0,2,1:T(8,128)} fusion(f32[512,24,64]{0,2,1:T(8,128)S(1)} %bitcast.296, bf16[24,512,512]{2,1,0:T(8,128)(2,1)} %multiply_convert_fusion, bf16[512,24,64]{0,2,1:T(8,128)(2,1)S(1)} %convert_element_type.381, f32[24]{0:T(128)S(1)} %copy-done.129), kind=kOutput, calls=%fused_computation.87 | convolution fusion | flops 806879232 | bytes 20447328 | tf_op jit(solution)/shard_map/transpose(jvp(hts,shp->thp))/dot_general | solution.py:165
  524.5 11.6 %multiply_reduce_fusion.6 = (f32[1792]{0:T(1024)S(1)}, f32[1792]{0:T(1024)S(1)}, f32[1792]{0:T(1024)S(1)}, f32[1792]{0:T(1024)S(1)}, f32[1792]{0:T(1024)S(1)}, /*index=5*/f32[512,1792]{1,0:T(8,128)}) fusion(f32[509,1792]{1,0:T(8,128)} %slice.444, pred[512]{0:T(512)(128)(4,1)} %copy-done.154, f32[512,1920]{1,0:T(8,128)} %fence.18, f32[511,1792]{1,0:T(8,128)} %slice.440, ...), kind=kLoop, calls=%fused_computation.72 | loop fusion | flops 19258624 | bytes 25684480 | tf_op jit(solution)/shard_map/transpose(jvp())/reduce_sum | solution.py:147
  565.7 13.8 %reduce-scatter.3.cloned.1.call-done.refs_2_.refs_0_ = bf16[192,1024]{1,0:T(8,128)(2,1)} async-done(((bf16[1536,1024]{1,0:T(8,128)(2,1)}), bf16[192,1024]{1,0:T(8,128)(2,1)}) %reduce-scatter.3.cloned.1.call-update) | async-done | bytes 393232 | tf_op jit(solution)/shard_map/reduce_scatter | solution.py:438
  603.9 46.2 %reduce-scatter.5.cloned.1.call-done.refs_0_ = bf16[544,256]{1,0:T(8,128)(2,1)} async-done(((bf16[4352,256]{1,0:T(8,128)(2,1)}), bf16[544,256]{1,0:T(8,128)(2,1)}) %reduce-scatter.5.cloned.1.call-update) | async-done | bytes 278544 | tf_op jit(solution)/shard_map/reduce_scatter | solution.py:438
  688.3 11.3 %collective-permute-done.32 = bf16[4,2,16,1920]{3,2,1,0:T(8,128)(2,1)S(1)} collective-permute-done((bf16[4,2,16,1920]{3,2,1,0:T(8,128)(2,1)S(1)}, bf16[4,2,16,1920]{3,2,1,0:T(8,128)(2,1)S(1)}, u32[]{:S(2)}, u32[]{:S(2)}) %collective-permute-start.32) | collective-permute-done | bytes 491552 | tf_op jit(solution)/shard_map/ppermute | solution.py:223
  705.6 11.5 %collective-permute-done.33 = bf16[4,48,1920]{2,1,0:T(8,128)(2,1)S(1)} collective-permute-done((bf16[4,48,1920]{2,1,0:T(8,128)(2,1)S(1)}, bf16[4,48,1920]{2,1,0:T(8,128)(2,1)S(1)}, u32[]{:S(2)}, u32[]{:S(2)}) %collective-permute-start.33) | collective-permute-done | bytes 737312 | tf_op jit(solution)/shard_map/ppermute | solution.py:223
  721.8 12.6 %collective-permute-done.35 = bf16[48,1920]{1,0:T(8,128)(2,1)S(1)} collective-permute-done((bf16[48,1920]{1,0:T(8,128)(2,1)S(1)}, bf16[48,1920]{1,0:T(8,128)(2,1)S(1)}, u32[]{:S(2)}, u32[]{:S(2)}) %collective-permute-start.35) | collective-permute-done | bytes 184352 | tf_op jit(solution)/shard_map/ppermute | solution.py:223
  (736 shorter events, 436.0 us)
Async XLA Ops:
  7.2 219.5 %all-gather.2.cloned.1.call-start = ((), (), s32[]{:S(2)}) async-start(), calls=%async_computation.2 | async-start | bytes 8912896 | tf_op jit(solution)/shard_map/all_gather | solution.py:321
  11.2 568.3 %reduce-scatter.3.cloned.1.call-start = ((), (), s32[]{:S(2)}) async-start(), calls=%async_computation.3 | async-start | bytes 3538944 | tf_op jit(solution)/shard_map/reduce_scatter | solution.py:438
  49.1 46.2 %collective-permute-start.11 = (bf16[48,2304]{1,0:T(8,128)(2,1)}, bf16[48,2304]{1,0:T(8,128)(2,1)S(1)}, u32[]{:S(2)}, u32[]{:S(2)}) collective-permute-start(bf16[48,2304]{1,0:T(8,128)(2,1)} %fence.17), channel_id=1, source_target_pairs={{0,4},{1,5},{2,6},{3,7},{4,0},{5,1},{6,2},{7,3},{8,12},{9,13},{10,... | collective-permute-start | bytes 663560 | tf_op jit(solution)/shard_map/ppermute | solution.py:223
  56.4 38.9 %collective-permute-start.10 = (bf16[48,2304]{1,0:T(8,128)(2,1)}, bf16[48,2304]{1,0:T(8,128)(2,1)S(1)}, u32[]{:S(2)}, u32[]{:S(2)}) collective-permute-start(bf16[48,2304]{1,0:T(8,128)(2,1)} %fence.17), channel_id=1, source_target_pairs={{0,2},{1,3},{2,4},{3,5},{4,6},{5,7},{6,0},{7,1},{8,10},{9,11},{10,... | collective-permute-start | bytes 663560 | tf_op jit(solution)/shard_map/ppermute | solution.py:223
  59.0 50.6 %collective-permute-start.3 = (bf16[4,48,1920]{2,1,0:T(8,128)(2,1)S(1)}, bf16[4,48,1920]{2,1,0:T(8,128)(2,1)}, u32[]{:S(2)}, u32[]{:S(2)}) collective-permute-start(bf16[4,48,1920]{2,1,0:T(8,128)(2,1)S(1)} %pad_maximum_fusion.12.refs_0_), channel_id=1, source_target_pairs={{0,1},{1,0},{2,3},{3,2},{4,5},{5,4},{6,7},{7,6},{8,9},{9,8},{10,11... | collective-permute-start | bytes 2211848 | tf_op jit(solution)/shard_map/ppermute | solution.py:223
  96.3 29.8 %collective-permute-start.13 = (bf16[4,48,2304]{2,1,0:T(8,128)(2,1)S(1)}, bf16[4,48,2304]{2,1,0:T(8,128)(2,1)S(1)}, u32[]{:S(2)}, u32[]{:S(2)}) collective-permute-start(bf16[4,48,2304]{2,1,0:T(8,128)(2,1)S(1)} %pad_maximum_fusion.11.refs_0_.refs_1_), channel_id=1, source_target_pairs={{0,1},{1,0},{2,3},{3,2},{4,5},{5,4},{6,7},{7,6},{8,9},{9,8},{10,11... | collective-permute-start | bytes 2654216 | tf_op jit(solution)/shard_map/ppermute | solution.py:223
  100.6 41.3 %collective-permute-start.6 = (bf16[4,48,1920]{2,1,0:T(8,128)(2,1)S(1)}, bf16[4,48,1920]{2,1,0:T(8,128)(2,1)}, u32[]{:S(2)}, u32[]{:S(2)}) collective-permute-start(bf16[4,48,1920]{2,1,0:T(8,128)(2,1)S(1)} %pad_maximum_fusion.12.refs_0_), channel_id=1, source_target_pairs={{0,8},{1,9},{2,10},{3,11},{4,12},{5,13},{6,14},{7,15},{8,0},{9,1},... | collective-permute-start | bytes 2211848 | tf_op jit(solution)/shard_map/ppermute | solution.py:223
  103.4 31.1 %collective-permute-start.8 = (bf16[4,16,1920]{2,1,0:T(8,128)(2,1)S(1)}, bf16[4,16,1920]{2,1,0:T(8,128)(2,1)S(1)}, u32[]{:S(2)}, u32[]{:S(2)}) collective-permute-start(bf16[4,16,1920]{2,1,0:T(8,128)(2,1)S(1)} %collective-permute-done.4.refs_2_), channel_id=1, source_target_pairs={{0,8},{1,9},{2,10},{3,11},{4,12},{5,13},{6,14},{7,15},{8,0},{9,1},... | collective-permute-start | bytes 737288 | tf_op jit(solution)/shard_map/ppermute | solution.py:223
  112.9 41.2 %collective-permute-start.7 = (bf16[4,48,1920]{2,1,0:T(8,128)(2,1)}, bf16[4,48,1920]{2,1,0:T(8,128)(2,1)}, u32[]{:S(2)}, u32[]{:S(2)}) collective-permute-start(bf16[4,48,1920]{2,1,0:T(8,128)(2,1)} %collective-permute-done.3.refs_1_), channel_id=1, source_target_pairs={{0,8},{1,9},{2,10},{3,11},{4,12},{5,13},{6,14},{7,15},{8,0},{9,1},... | collective-permute-start | bytes 2211848 | tf_op jit(solution)/shard_map/ppermute | solution.py:223
  139.9 85.9 %collective-permute-start.16 = (bf16[4,48,2304]{2,1,0:T(8,128)(2,1)S(1)}, bf16[4,48,2304]{2,1,0:T(8,128)(2,1)S(1)}, u32[]{:S(2)}, u32[]{:S(2)}) collective-permute-start(bf16[4,48,2304]{2,1,0:T(8,128)(2,1)S(1)} %pad_maximum_fusion.11.refs_0_.refs_1_), channel_id=1, source_target_pairs={{0,8},{1,9},{2,10},{3,11},{4,12},{5,13},{6,14},{7,15},{8,0},{9,1},... | collective-permute-start | bytes 2654216 | tf_op jit(solution)/shard_map/ppermute | solution.py:223
  141.8 84.0 %collective-permute-start.18 = (bf16[4,16,2304]{2,1,0:T(8,128)(2,1)}, bf16[4,16,2304]{2,1,0:T(8,128)(2,1)}, u32[]{:S(2)}, u32[]{:S(2)}) collective-permute-start(bf16[4,16,2304]{2,1,0:T(8,128)(2,1)} %collective-permute-done.14.refs_2_), channel_id=1, source_target_pairs={{0,8},{1,9},{2,10},{3,11},{4,12},{5,13},{6,14},{7,15},{8,0},{9,1},... | collective-permute-start | bytes 884744 | tf_op jit(solution)/shard_map/ppermute | solution.py:223
  141.8 84.0 %collective-permute-start.17 = (bf16[4,48,2304]{2,1,0:T(8,128)(2,1)S(1)}, bf16[4,48,2304]{2,1,0:T(8,128)(2,1)}, u32[]{:S(2)}, u32[]{:S(2)}) collective-permute-start(bf16[4,48,2304]{2,1,0:T(8,128)(2,1)S(1)} %collective-permute-done.13.refs_1_), channel_id=1, source_target_pairs={{0,8},{1,9},{2,10},{3,11},{4,12},{5,13},{6,14},{7,15},{8,0},{9,1},... | collective-permute-start | bytes 2654216 | tf_op jit(solution)/shard_map/ppermute | solution.py:223
  152.6 73.2 %collective-permute-start.19 = (bf16[4,16,2304]{2,1,0:T(8,128)(2,1)}, bf16[4,16,2304]{2,1,0:T(8,128)(2,1)}, u32[]{:S(2)}, u32[]{:S(2)}) collective-permute-start(bf16[4,16,2304]{2,1,0:T(8,128)(2,1)} %collective-permute-done.15.refs_3_), channel_id=1, source_target_pairs={{0,8},{1,9},{2,10},{3,11},{4,12},{5,13},{6,14},{7,15},{8,0},{9,1},... | collective-permute-start | bytes 884744 | tf_op jit(solution)/shard_map/ppermute | solution.py:223
  226.7 51.0 %collective-permute-start.20 = (bf16[4096,1024]{1,0:T(8,128)(2,1)}, bf16[4096,1024]{1,0:T(8,128)(2,1)}, u32[]{:S(2)}, u32[]{:S(2)}) collective-permute-start(bf16[4096,1024]{1,0:T(8,128)(2,1)} %fence.21), channel_id=1, source_target_pairs={{0,8},{1,9},{2,10},{3,11},{4,12},{5,13},{6,14},{7,15},{8,0},{9,1},... | collective-permute-start | bytes 25165832 | tf_op jit(solution)/shard_map/ppermute | solution.py:223
  314.1 30.5 %collective-permute-start.21 = (bf16[8,128,1024]{2,1,0:T(8,128)(2,1)}, bf16[8,128,1024]{2,1,0:T(8,128)(2,1)}, u32[]{:S(2)}, u32[]{:S(2)}) collective-permute-start(bf16[8,128,1024]{2,1,0:T(8,128)(2,1)} %dynamic-slice_bitcast_fusion.4.refs_1_), channel_id=1, source_target_pairs={{0,8},{1,9},{2,10},{3,11},{4,12},{5,13},{6,14},{7,15},{8,0},{9,1},... | collective-permute-start | bytes 6291464 | tf_op jit(solution)/shard_map/ppermute | solution.py:223
  329.9 47.7 %collective-permute-start.22 = (bf16[8,64,4096]{2,1,0:T(8,128)(2,1)}, bf16[8,64,4096]{2,1,0:T(8,128)(2,1)}, u32[]{:S(2)}, u32[]{:S(2)}) collective-permute-start(bf16[8,64,4096]{2,1,0:T(8,128)(2,1)} %dynamic-slice_bitcast_fusion.refs_2_), channel_id=1, source_target_pairs={{0,8},{1,9},{2,10},{3,11},{4,12},{5,13},{6,14},{7,15},{8,0},{9,1},... | collective-permute-start | bytes 12582920 | tf_op jit(solution)/shard_map/ppermute | solution.py:223
  360.8 52.8 %collective-permute-start.25 = (bf16[8,128,1024]{2,1,0:T(8,128)(2,1)}, bf16[8,128,1024]{2,1,0:T(8,128)(2,1)}, u32[]{:S(2)}, u32[]{:S(2)}) collective-permute-start(bf16[8,128,1024]{2,1,0:T(8,128)(2,1)} %dynamic-slice_bitcast_fusion.2.refs_2_), channel_id=1, source_target_pairs={{0,8},{1,9},{2,10},{3,11},{4,12},{5,13},{6,14},{7,15},{8,0},{9,1},... | collective-permute-start | bytes 6291464 | tf_op jit(solution)/shard_map/ppermute | solution.py:223
  384.7 73.9 %collective-permute-start.24 = (bf16[8,32,4096]{2,1,0:T(8,128)(2,1)}, bf16[8,32,4096]{2,1,0:T(8,128)(2,1)}, u32[]{:S(2)}, u32[]{:S(2)}) collective-permute-start(bf16[8,32,4096]{2,1,0:T(8,128)(2,1)} %dynamic-slice_bitcast_fusion.3.refs_1_), channel_id=1, source_target_pairs={{0,16},{1,17},{2,18},{3,19},{4,20},{5,21},{6,22},{7,23},{8,24},{9,... | collective-permute-start | bytes 6291464 | tf_op jit(solution)/shard_map/ppermute | solution.py:223
  416.3 37.7 %collective-permute-start.27 = (bf16[8,64,1024]{2,1,0:T(8,128)(2,1)S(1)}, bf16[8,64,1024]{2,1,0:T(8,128)(2,1)}, u32[]{:S(2)}, u32[]{:S(2)}) collective-permute-start(bf16[8,64,1024]{2,1,0:T(8,128)(2,1)S(1)} %dynamic-slice_bitcast_fusion.6.refs_2_), channel_id=1, source_target_pairs={{0,16},{1,17},{2,18},{3,19},{4,20},{5,21},{6,22},{7,23},{8,24},{9,... | collective-permute-start | bytes 3145736 | tf_op jit(solution)/shard_map/ppermute | solution.py:223
  430.9 89.3 %collective-permute-start.26 = (bf16[8,64,2304]{2,1,0:T(8,128)(2,1)}, bf16[8,64,2304]{2,1,0:T(8,128)(2,1)}, u32[]{:S(2)}, u32[]{:S(2)}) collective-permute-start(bf16[8,64,2304]{2,1,0:T(8,128)(2,1)} %dynamic-slice_bitcast_fusion.1.refs_3_), channel_id=1, source_target_pairs={{0,8},{1,9},{2,10},{3,11},{4,12},{5,13},{6,14},{7,15},{8,0},{9,1},... | collective-permute-start | bytes 7077896 | tf_op jit(solution)/shard_map/ppermute | solution.py:223
  507.3 142.8 %reduce-scatter.5.cloned.1.call-start = ((), (), s32[]{:S(2)}) async-start(), calls=%async_computation.4 | async-start | bytes 2506752 | tf_op jit(solution)/shard_map/reduce_scatter | solution.py:438
  523.3 26.3 %collective-permute-start.28 = (bf16[8,32,2304]{2,1,0:T(8,128)(2,1)S(1)}, bf16[8,32,2304]{2,1,0:T(8,128)(2,1)}, u32[]{:S(2)}, u32[]{:S(2)}) collective-permute-start(bf16[8,32,2304]{2,1,0:T(8,128)(2,1)S(1)} %dynamic-slice_bitcast_fusion.5.refs_1_), channel_id=1, source_target_pairs={{0,16},{1,17},{2,18},{3,19},{4,20},{5,21},{6,22},{7,23},{8,24},{9,... | collective-permute-start | bytes 3538952 | tf_op jit(solution)/shard_map/ppermute | solution.py:223
  681.3 38.5 %collective-permute-start.30 = (bf16[64,2304]{1,0:T(8,128)(2,1)S(1)}, bf16[64,2304]{1,0:T(8,128)(2,1)S(1)}, u32[]{:S(2)}, u32[]{:S(2)}) collective-permute-start(bf16[64,2304]{1,0:T(8,128)(2,1)S(1)} %pad_maximum_fusion.18), channel_id=1, source_target_pairs={{0,8},{1,9},{2,10},{3,11},{4,12},{5,13},{6,14},{7,15},{8,0},{9,1},... | collective-permute-start | bytes 884744 | tf_op jit(solution)/shard_map/ppermute | solution.py:223
  683.7 52.0 %collective-permute-start.42 = (bf16[64,4096]{1,0:T(8,128)(2,1)S(1)}, bf16[64,4096]{1,0:T(8,128)(2,1)S(1)}, u32[]{:S(2)}, u32[]{:S(2)}) collective-permute-start(bf16[64,4096]{1,0:T(8,128)(2,1)S(1)} %pad_maximum_fusion.16), channel_id=1, source_target_pairs={{0,8},{1,9},{2,10},{3,11},{4,12},{5,13},{6,14},{7,15},{8,0},{9,1},... | collective-permute-start | bytes 1572872 | tf_op jit(solution)/shard_map/ppermute | solution.py:223
  (201 other events, 2262.6 us)
Sparse Core Ops, SparseCore 0:
  11.4 159.4 all-gather.1
  507.4 72.0 reduce-scatter.2
  582.9 67.1 reduce-scatter.4

commit v7 on v4

--- a/solution.py
+++ b/solution.py
@@ -147,23 +147,168 @@
     return low(jax.nn.silu(summed))
 
 
-def scan(conv_out, step_raw, head_params, segment, low, low_back):
-    span_length = conv_out.shape[0]
-    slots = jnp.arange(span_length, dtype=jnp.int32)
-    allowed = (segment[:, None] == segment[None, :]) & (slots[None, :] <= slots[:, None])
-    scan_x = conv_out[:, : MH * MP].reshape(span_length, MH, MP)
-    scan_b = conv_out[:, MH * MP : MH * MP + NS]
-    scan_c = conv_out[:, MH * MP + NS :]
+TILE = 128
+
+
+def mixing_tables(b_ref, c_ref, row_segment, column_segment, table, bias, transposed):
+    left, right = (b_ref, c_ref) if transposed else (c_ref, b_ref)
+    table[...] = dot_right(left[...], right[...])
+    shape = table.shape
+    first = lax.broadcasted_iota(jnp.int32, shape, 0)
+    second = lax.broadcasted_iota(jnp.int32, shape, 1)
+    order = (first <= second) if transposed else (second <= first)
+    allowed = order & (column_segment[...] == row_segment[...])
+    bias[...] = jnp.where(allowed, 0.0, -1e30)
+
+
+def scan_forward_kernel(
+    x_ref, b_ref, c_ref, cum_col, cum_row, step_row, skip, row_segment, column_segment,
+    out_ref, table, bias,
+):
+    @pl.when(pl.program_id(0) == 0)
+    def _():
+        mixing_tables(b_ref, c_ref, row_segment, column_segment, table, bias, False)
+
+    for start in range(0, x_ref.shape[0], TILE):
+        rows, width = pl.ds(start, TILE), start + TILE
+        halves = []
+        for head in range(2):
+            spread = cum_col[0, rows, head : head + 1] - cum_row[0, head : head + 1, :width]
+            decay = jnp.exp(spread + bias[rows, :width])
+            mixing = table[rows, :width] * decay * step_row[0, head : head + 1, :width]
+            halves.append(dot(mixing.astype(jnp.bfloat16), x_ref[:width, :]))
+        first = lax.broadcasted_iota(jnp.int32, (TILE, 2 * MP), 1) < MP
+        out_ref[rows, :] = jnp.where(first, halves[0], halves[1]) + skip[...] * x_ref[
+            rows, :
+        ].astype(jnp.float32)
+
+
+def scan_backward_kernel(
+    cot_ref, out_ref, x_ref, b_ref, c_ref, cum_col, cum_row, step_col, skip,
+    row_segment, column_segment, dx_ref, dcum_ref, dstep_ref, dskip_ref, dtable_ref,
+    table, bias, dtable,
+):
+    @pl.when(pl.program_id(0) == 0)
+    def _():
+        mixing_tables(b_ref, c_ref, row_segment, column_segment, table, bias, True)
+        dtable[...] = jnp.zeros_like(dtable)
+
+    span = x_ref.shape[0]
+    cot = cot_ref[...]
+    cot_low = cot.astype(jnp.bfloat16)
+    dskip_ref[...] = jnp.sum(cot * x_ref[...].astype(jnp.float32), axis=0, keepdims=True)
+    for start in range(0, span, TILE):
+        rows, later = pl.ds(start, TILE), pl.ds(start, span - start)
+        first = lax.broadcasted_iota(jnp.int32, (TILE, 2 * MP), 1) < MP
+        x_tile = x_ref[rows, :]
+        halves = []
+        for head in range(2):
+            spread = cum_row[0, head : head + 1, start:] - cum_col[0, rows, head : head + 1]
+            scaled = jnp.exp(spread + bias[rows, later]) * step_col[0, rows, head : head + 1]
+            mixing = table[rows, later] * scaled
+            mine = first if head == 0 else jnp.logical_not(first)
+            x_head = jnp.where(mine, x_tile, jnp.zeros_like(x_tile))
+            dtable[rows, later] += dot_right(x_head, cot_low[start:, :]) * scaled
+            halves.append(dot(mixing.astype(jnp.bfloat16), cot_low[start:, :]))
+        part = jnp.where(first, halves[0], halves[1])
+        x_wide = x_tile.astype(jnp.float32)
+        dx_ref[rows, :] = part + skip[...] * cot[start : start + TILE, :]
+        into = x_wide * part
+        product = out_ref[rows, :] - skip[...] * x_wide
+        across = cot_low[start : start + TILE, :].astype(jnp.float32) * product - into
+        for head in range(2):
+            mine = first if head == 0 else jnp.logical_not(first)
+            dcum_ref[0, rows, head : head + 1] = jnp.sum(
+                jnp.where(mine, across, 0.0), axis=1, keepdims=True
+            )
+            dstep_ref[0, rows, head : head + 1] = jnp.sum(
+                jnp.where(mine, into, 0.0), axis=1, keepdims=True
+            )
+
+    @pl.when(pl.program_id(0) == pl.num_programs(0) - 1)
+    def _():
+        dtable_ref[...] = dtable[...].astype(jnp.bfloat16)
+
+
+def decay_steps(step_raw, head_params):
     step_size = jax.nn.softplus(step_raw + head_params[0][None, :])
-    cumulative = jnp.cumsum(-step_size * jnp.exp(head_params[1])[None, :], axis=0)
-    intersection = low_back(jnp.dot(scan_c, scan_b.T, precision=None))
-    cum_heads = cumulative.T
-    spread = cum_heads[:, :, None] - cum_heads[:, None, :]
-    decay_matrix = jnp.exp(jnp.where(allowed[None], spread, -10000.0))
-    mixing = low(intersection[None] * decay_matrix * step_size.T[:, None, :])
-    scan_out = low_back(jnp.einsum("hts,shp->thp", mixing, scan_x, precision=None))
-    scan_out = scan_out + head_params[2][None, :, None] * scan_x
-    return scan_out.reshape(span_length, MH * MP)
+    return step_size, jnp.cumsum(-step_size * jnp.exp(head_params[1])[None, :], axis=0)
+
+
+def pair_columns(values):
+    return jnp.swapaxes(values.reshape(values.shape[0], MH // 2, 2), 0, 1)
+
+
+def scan_operands(conv_low, step_size, cumulative, head_params, segment):
+    span = conv_low.shape[0]
+    pair = pl.BlockSpec((span, 2 * MP), lambda i: (0, i))
+    column = pl.BlockSpec((1, span, 2), lambda i: (i, 0, 0))
+    row = pl.BlockSpec((1, 2, span), lambda i: (i, 0, 0))
+    lanes = pl.BlockSpec((1, 2 * MP), lambda i: (0, i))
+    b_spec = pl.BlockSpec((span, NS), lambda i: (0, MH // 2))
+    c_spec = pl.BlockSpec((span, NS), lambda i: (0, MH // 2 + 1))
+    row_segment = pl.BlockSpec((1, span), lambda i: (0, 0))
+    column_segment = pl.BlockSpec((span, 1), lambda i: (0, 0))
+    arrays = {
+        "x": (conv_low, pair),
+        "b": (conv_low, b_spec),
+        "c": (conv_low, c_spec),
+        "cum_col": (pair_columns(cumulative), column),
+        "cum_row": (cumulative.T.reshape(MH // 2, 2, span), row),
+        "step_col": (pair_columns(step_size), column),
+        "step_row": (step_size.T.reshape(MH // 2, 2, span), row),
+        "skip": (jnp.repeat(head_params[2], MP)[None, :], lanes),
+        "row_segment": (segment[None, :], row_segment),
+        "column_segment": (segment[:, None], column_segment),
+    }
+    return arrays, pair, column, lanes
+
+
+def scan_forward(conv_low, step_size, cumulative, head_params, segment):
+    span = conv_low.shape[0]
+    arrays, pair, _, _ = scan_operands(conv_low, step_size, cumulative, head_params, segment)
+    names = "x b c cum_col cum_row step_row skip row_segment column_segment".split()
+    return pl.pallas_call(
+        scan_forward_kernel,
+        grid=(MH // 2,),
+        out_shape=jax.ShapeDtypeStruct((span, MH * MP), jnp.float32),
+        in_specs=[arrays[name][1] for name in names],
+        out_specs=pair,
+        scratch_shapes=[pltpu.VMEM((span, span), jnp.float32)] * 2,
+        compiler_params=pltpu.CompilerParams(vmem_limit_bytes=32 * 1024 * 1024),
+        name="scan_forward",
+    )(*(arrays[name][0] for name in names))
+
+
+def scan_backward(cot, out, conv_low, step_size, cumulative, head_params, segment):
+    span = conv_low.shape[0]
+    arrays, pair, column, lanes = scan_operands(
+        conv_low, step_size, cumulative, head_params, segment
+    )
+    names = "x b c cum_col cum_row step_col skip row_segment column_segment".split()
+    dx, dcum, dstep, dskip, dtable = pl.pallas_call(
+        scan_backward_kernel,
+        grid=(MH // 2,),
+        out_shape=[
+            jax.ShapeDtypeStruct((span, MH * MP), jnp.float32),
+            jax.ShapeDtypeStruct((MH // 2, span, 2), jnp.float32),
+            jax.ShapeDtypeStruct((MH // 2, span, 2), jnp.float32),
+            jax.ShapeDtypeStruct((1, MH * MP), jnp.float32),
+            jax.ShapeDtypeStruct((span, span), jnp.bfloat16),
+        ],
+        in_specs=[pair, pair] + [arrays[name][1] for name in names],
+        out_specs=[pair, column, column, lanes, pl.BlockSpec((span, span), lambda i: (0, 0))],
+        scratch_shapes=[pltpu.VMEM((span, span), jnp.float32)] * 3,
+        compiler_params=pltpu.CompilerParams(vmem_limit_bytes=32 * 1024 * 1024),
+        name="scan_backward",
+    )(cot, out, *(arrays[name][0] for name in names))
+    scan_b = conv_low[:, MH * MP : MH * MP + NS]
+    scan_c = conv_low[:, MH * MP + NS :]
+    conv_cot = jnp.concatenate([dx, dot(dtable, scan_c), dot_left(dtable, scan_b)], axis=1)
+    dcum = jnp.swapaxes(dcum, 0, 1).reshape(span, MH)
+    dstep = jnp.swapaxes(dstep, 0, 1).reshape(span, MH)
+    dstep = jnp.where(step_size > 1e-30, dstep / jnp.maximum(step_size, 1e-30), 0.0)
+    return conv_cot, dstep, dcum, jnp.sum(dskip.reshape(MH, MP), axis=1)
 
 
 def gating(scan_out, gate_z, gain, low):
@@ -493,12 +638,11 @@
     conv_out, pull_conv = jax.vjp(
         lambda p, k: convolution(p, k, segment, low), projected[:, :CONV], taps
     )
-    scan_out, pull_scan = jax.vjp(
-        lambda c, r, h: scan(c, r, h, segment, low, low_back),
-        conv_out,
-        projected[:, CONV : CONV + MH],
-        head_params,
-    )
+    conv_low = rows_of(conv_out)
+    (step_size, cumulative), pull_steps = jax.vjp(
+        decay_steps, projected[:, CONV : CONV + MH], head_params
+    )
+    scan_out = scan_forward(conv_low, step_size, cumulative, head_params, segment)
     beside = dot(normed_low, w_side)
     context, pull_context = jax.vjp(
         lambda p: attention(p, segment, token_position, low, low_back), beside[:, :QKV]
@@ -525,14 +669,18 @@
     hidden_part, gain_ff = pull_ff(ff_cot)
     hidden_cot = cot.astype(jnp.float32) + hidden_part
     hidden_low = rows_of(hidden_cot)
-    moving.add("out", dot_left(joined, hidden_low), paired=True)
+    moving.add("out", dot_left(joined, hidden_low))
     (joined_cot,) = moving.step([dot_right(hidden_low, w_out)])
     scan_cot, gate_cot, gain_scan = pull_gating(joined_cot[:, context_width:])
     (qkv_cot,) = pull_context(joined_cot[:, :context_width])
     side_cot = jnp.concatenate([rows_of(qkv_cot), rows_of(gate_cot)], axis=1)
-    moving.add("side", dot_left(normed_low, side_cot))
+    moving.add("side", dot_left(normed_low, side_cot), paired=True)
     (scan_cot,) = moving.step([scan_cot])
-    conv_out_cot, step_cot, head_grad = pull_scan(scan_cot)
+    conv_out_cot, dstep, dcum, dskip = scan_backward(
+        scan_cot, scan_out, conv_low, step_size, cumulative, head_params, segment
+    )
+    step_cot, head_grad = pull_steps((dstep, dcum))
+    head_grad = head_grad.at[2].add(dskip)
     (conv_out_cot,) = moving.step([conv_out_cot])
     conv_cot, taps_grad = pull_conv(conv_out_cot)
     conv_cot = rows_of(

time: 652 us -> 735 us (1.13)
  waiting for transfers between devices: 148 us -> 245 us
  matrix products: 147 us -> 105 us
  Pallas kernels: 9.97 us -> 35 us
  local copies, waits for them, and re-layouts: 118 us -> 127 us
    reduce_scatter x3, waiting for transfers between devices: 0.04 us -> 87.5 us  [paired_reduce(): lax.psum_scatter(half, ('z', 'y', 'x'), scatter_dimension=0, tiled=True)]
    dot_general x6 -> x0, matrix products: 42.3 us -> none  [the longest x3 39.1 us: scan(): jnp.einsum('hts,shp->thp', mixing, scan_x, precision=None)]
    pallas_call x0 -> x2, Pallas kernels: none -> 26.4 us  [the longest x1 18.7 us: scan_backward(): pl.pallas_call(scan_backward_kernel, grid=(MH // 2,), out_shape=[jax.Shap...]
    all_gather x3, waiting for transfers between devices: 0.01 us -> 25.6 us  [general_gather(): return lax.all_gather(part, shard + rep, axis=0, tiled=True)]
    unnamed x317 -> x305, local copies, waits for them, and re-layouts: 40.8 us -> 62.1 us
    ppermute x45, waiting for transfers between devices: 148 us -> 132 us  [send(): return lax.ppermute(values, ('x', 'core', 'z', 'y'), pairs)]
    convert_element_type x6 -> x5, other arithmetic: 28.1 us -> 19 us  [round_value(): values.astype(jnp.bfloat16)]
    dot_general x5 -> x6, matrix products: 18.7 us -> 20.8 us  [dot_left(): lax.dot_general(left, right, (((0,), (0,)), ((), ())), preferred_element_...]
  transfers between devices with their start and end apart: 51 -> 51, of which waited for: 17 -> 19; matrix products, arithmetic and copies ran while one was open for 58% -> 43% of each run, Pallas kernels for 2% -> 5%
where the time goes in v7:
time: 735 us; the launch traced here: 731 us
  waiting for transfers between devices  245 us (33%)
  other arithmetic  152 us (21%)
  local copies, waits for them, and re-layouts  127 us (17%)
  matrix products  105 us (14%)
  starting transfers between devices  50.7 us (7%)
  Pallas kernels  35 us (5%)
  between operations  16.5 us (2%)
    ppermute x45, waiting for transfers between devices, send(): return lax.ppermute(values, ('x', 'core', 'z', 'y'), pairs)  132 us
    reduce_scatter x3, waiting for transfers between devices, paired_reduce(): lax.psum_scatter(half, ('z', 'y', 'x'), scatter_dimension=0, tiled=True)  87.5 us
    unnamed x305, local copies, waits for them, and re-layouts  62.1 us
    ppermute x45, starting transfers between devices, send(): return lax.ppermute(values, ('x', 'core', 'z', 'y'), pairs)  50.5 us
    dot_general x5, matrix products, dot_right(): lax.dot_general(left, right, (((1,), (1,)), ((), ())), preferred_element_...  31.3 us
    dot_general x6, matrix products, dot(): return jnp.dot(left, right, preferred_element_type=jnp.float32)  29.8 us
    all_gather x3, waiting for transfers between devices, general_gather(): return lax.all_gather(part, shard + rep, axis=0, tiled=True)  25.6 us
    convert_element_type x11, other arithmetic, add_low(): (left.astype(jnp.float32) + right.astype(jnp.float32)).astype(jnp.bfloat16)  23.2 us
  transfers between devices with their start and end apart: 51, of which 19 were waited for; matrix products, arithmetic and copies ran while one was open for 43% of the time, Pallas kernels for 5%

profile of v7, /device:TPU:1, one launch (start us, length us, event | category | flops | bytes accessed | tf_op | source)
XLA Modules:
  0.0 730.6 jit_solution(7525266990199855391)
XLA Ops:
  31.5 10.7 %collective-permute-done.1.refs_2_ = bf16[48,1920]{1,0:T(8,128)(2,1)S(1)} collective-permute-done((bf16[48,1920]{1,0:T(8,128)(2,1)}, bf16[48,1920]{1,0:T(8,128)(2,1)S(1)}, u32[]{:S(2)}, u32[]{:S(2)}) %collective-permute-start.1) | collective-permute-done | bytes 184352 | tf_op jit(solution)/shard_map/ppermute | solution.py:366
  55.1 14.3 %collective-permute-done.11 = bf16[48,2304]{1,0:T(8,128)(2,1)S(1)} collective-permute-done((bf16[48,2304]{1,0:T(8,128)(2,1)}, bf16[48,2304]{1,0:T(8,128)(2,1)S(1)}, u32[]{:S(2)}, u32[]{:S(2)}) %collective-permute-start.11) | collective-permute-done | bytes 221216 | tf_op jit(solution)/shard_map/ppermute | solution.py:366
  76.5 7.8 %collective-permute-done.4.refs_2_ = bf16[4,16,1920]{2,1,0:T(8,128)(2,1)S(1)} collective-permute-done((bf16[4,16,1920]{2,1,0:T(8,128)(2,1)S(1)}, bf16[4,16,1920]{2,1,0:T(8,128)(2,1)S(1)}, u32[]{:S(2)}, u32[]{:S(2)}) %collective-permute-start.4) | collective-permute-done | bytes 245792 | tf_op jit(solution)/shard_map/ppermute | solution.py:366
  135.2 9.1 %multiply_convert_fusion.1 = (bf16[512,1792]{1,0:T(8,128)(2,1)S(1)}, f32[512,1792]{1,0:T(8,128)}) fusion(f32[509,1792]{1,0:T(8,128)} %slice.324, pred[512]{0:T(512)(128)(4,1)S(1)} %get-tuple-element.221, f32[1792]{0:T(1024)S(1)} %mul.775, f32[510,1792]{1,0:T(8,128)} %slice.322, pred[512]{0:T(512)(128)(4,1)S(1)} %get-tuple-element.220, f32[1792]{0:T(1024)S(1)} %mul.772, ...), kind=kLoop, calls=%fused_computation.64 | loop fusion | flops 14680064 | bytes 20179456 | tf_op jit(solution)/shard_map/jvp()/convert_element_type | solution.py:35
  154.1 7.6 %scan_forward.1.out_ref = f32[512,1536]{1,0:T(8,128)S(1)} custom-call(bf16[512,1792]{1,0:T(8,128)(2,1)S(1)} %get-tuple-element.158.x_ref.b_ref.c_ref, bf16[512,1792]{1,0:T(8,128)(2,1)S(1)} %get-tuple-element.158.x_ref.b_ref.c_ref, bf16[512,1792]{1,0:T(8,128)(2,1)S(1)} %get-tuple-element.158.x_ref.b_ref.c_ref, f32[12,512,2]{2,1,0:T(8,128)S(1)} %bitcast.262, ...), custom_call_target="tpu_custom_call" | custom-call | tf_op jit(solution)/shard_map/scan_forward/pallas_call | solution.py:271
  178.0 7.4 %fusion.129 = (f32[2,4,512]{2,1,0:T(4,128)S(1)}, f32[2,4,512,512]{2,3,1,0:T(8,128)}) fusion(pred[512,512]{0,1:T(8,128)(4,1)S(1)} %copy-done.70, bf16[512,2,4,64]{0,3,2,1:T(8,128)(2,1)} %bitcast.308, bf16[512,2,64]{0,2,1:T(8,128)(2,1)S(1)} %pad_maximum_fusion.25), kind=kOutput, calls=%fused_computation.337 | convolution fusion | flops 276824576 | bytes 9322496 | tf_op jit(solution)/shard_map/jvp()/sub | solution.py:130
  185.4 6.7 divide_convert_fusion
  205.2 10.6 %fusion.136 = f32[512,4096]{1,0:T(8,128)} fusion(bf16[512,1024]{1,0:T(8,128)(2,1)S(1)} %multiply_convert_fusion.3, bf16[1024,4096]{1,0:T(8,128)(2,1)} %all-gather.6.cloned.1.call-done), kind=kOutput, calls=%fused_computation.340 | convolution fusion | flops 4294967296 | bytes 17825792 | tf_op jit(solution)/shard_map/dot_general | solution.py:97
  215.8 25.6 %all-gather.8.cloned.1.call-done = bf16[2048,1024]{1,0:T(8,128)(2,1)} async-done(((bf16[64,1024]{1,0:T(8,128)(2,1)}), bf16[2048,1024]{1,0:T(8,128)(2,1)}) %all-gather.8.cloned.1.call-update) | async-done | bytes 4194320 | tf_op jit(solution)/shard_map/all_gather | solution.py:345
  241.4 8.7 %fusion.63 = (f32[512,2048]{1,0:T(8,128)S(1)}, f32[512,2048]{1,0:T(8,128)S(1)}, bf16[512,2048]{1,0:T(8,128)(2,1)S(1)}) fusion(f32[512,4096]{1,0:T(8,128)} %fusion.136, bf16[2048,1024]{1,0:T(8,128)(2,1)} %all-gather.8.cloned.1.call-done, bf16[512,1024]{1,0:T(8,128)(2,1)} %param.27, pred[512]{0:T(512)(128)(4,1)S(1)} %copy-done.138), kind=kOutput, calls=%fused_computation.176 | convolution fusion | flops 2162688000 | bytes 24117760 | tf_op jit(solution)/shard_map/dot_general | solution.py:105
  258.8 7.0 convolution_convert_fusion
  271.7 8.6 %fusion.137.refs_0_ = f32[512,1024]{1,0:T(8,128)} fusion(bf16[512,4096]{1,0:T(8,128)(2,1)S(1)} %copy-done.29, bf16[1024,4096]{1,0:T(8,128)(2,1)} %all-gather.6.cloned.1.call-done), kind=kOutput, calls=%fused_computation.341 | convolution fusion | flops 4294967296 | bytes 14680064 | tf_op jit(solution)/shard_map/dot_general | solution.py:105
  300.7 7.4 %fusion.61.refs_0_ = f32[512,2048]{1,0:T(8,128)} fusion(bf16[2048,1024]{1,0:T(8,128)(2,1)} %all-gather.4.cloned.1.call-done, f32[512,1024]{1,0:T(8,128)} %copy-done.38), kind=kOutput, calls=%fused_computation.167 | convolution fusion | flops 2148007936 | bytes 10485760 | tf_op jit(solution)/shard_map/dot_general | solution.py:105
  314.9 7.2 fusion.1
  371.8 18.7 %scan_backward.1 = (f32[512,1536]{1,0:T(8,128)S(1)}, f32[12,512,2]{2,1,0:T(8,128)S(1)}, f32[12,512,2]{2,1,0:T(8,128)S(1)}, f32[1,1536]{1,0:T(1,128)S(1)}, bf16[512,512]{1,0:T(8,128)(2,1)S(1)}) custom-call(f32[512,1536]{1,0:T(8,128)S(1)} %copy-done.5, f32[512,1536]{1,0:T(8,128)S(1)} %copy-done.2, bf16[512,1792]{1,0:T(8,128)(2,1)S(1)} %get-tuple-element.158.x_ref.b_ref.c_ref, ...), custom_call_target="tpu_custom_call" | custom-call | tf_op jit(solution)/shard_map/scan_backward/pallas_call | solution.py:289
  414.7 15.9 %collective-permute-done.25 = bf16[4,96,1024]{2,1,0:T(8,128)(2,1)S(1)} collective-permute-done((bf16[4,96,1024]{2,1,0:T(8,128)(2,1)S(1)}, bf16[4,96,1024]{2,1,0:T(8,128)(2,1)S(1)}, u32[]{:S(2)}, u32[]{:S(2)}) %collective-permute-start.25) | collective-permute-done | bytes 786464 | tf_op jit(solution)/shard_map/ppermute | solution.py:366
  436.9 9.9 %multiply_reduce_fusion.4 = (f32[1792]{0:T(1024)S(1)}, f32[1792]{0:T(1024)S(1)}, f32[1792]{0:T(1024)S(1)}, f32[1792]{0:T(1024)S(1)}, f32[1792]{0:T(1024)S(1)}, /*index=5*/f32[512,1792]{1,0:T(8,128)S(1)}) fusion(f32[509,1792]{1,0:T(8,128)} %slice.324, pred[512]{0:T(512)(128)(4,1)S(1)} %copy-done.130, f32[512,1920]{1,0:T(8,128)} %copy-done.18, ...), kind=kLoop, calls=%fused_computation.62 | loop fusion | flops 19258624 | bytes 25684480 | tf_op jit(solution)/shard_map/transpose(jvp())/reduce_sum | solution.py:146
  454.4 6.2 add_convert_fusion.1
  499.3 14.5 %collective-permute-done.37 = bf16[96,1024]{1,0:T(8,128)(2,1)} collective-permute-done((bf16[96,1024]{1,0:T(8,128)(2,1)S(1)}, bf16[96,1024]{1,0:T(8,128)(2,1)}, u32[]{:S(2)}, u32[]{:S(2)}) %collective-permute-start.37) | collective-permute-done | bytes 196640 | tf_op jit(solution)/shard_map/ppermute | solution.py:366
  515.9 6.2 add_convert_fusion.2
  530.4 8.7 %collective-permute-done.29 = bf16[4,2,16,1920]{3,2,0,1:T(8,128)(2,1)} collective-permute-done((bf16[4,2,16,1920]{3,2,0,1:T(8,128)(2,1)}, bf16[4,2,16,1920]{3,2,0,1:T(8,128)(2,1)}, u32[]{:S(2)}, u32[]{:S(2)}) %collective-permute-start.29) | collective-permute-done | bytes 491552 | tf_op jit(solution)/shard_map/ppermute | solution.py:366
  546.6 9.9 %collective-permute-done.30 = bf16[4,48,1920]{2,1,0:T(8,128)(2,1)S(1)} collective-permute-done((bf16[4,48,1920]{2,1,0:T(8,128)(2,1)S(1)}, bf16[4,48,1920]{2,1,0:T(8,128)(2,1)S(1)}, u32[]{:S(2)}, u32[]{:S(2)}) %collective-permute-start.30) | collective-permute-done | bytes 737312 | tf_op jit(solution)/shard_map/ppermute | solution.py:366
  563.6 17.0 %collective-permute-done.32 = bf16[48,1920]{1,0:T(8,128)(2,1)S(1)} collective-permute-done((bf16[48,1920]{1,0:T(8,128)(2,1)S(1)}, bf16[48,1920]{1,0:T(8,128)(2,1)S(1)}, u32[]{:S(2)}, u32[]{:S(2)}) %collective-permute-start.32) | collective-permute-done | bytes 184352 | tf_op jit(solution)/shard_map/ppermute | solution.py:366
  604.3 87.4 %reduce-scatter.6.cloned.1.call-done = bf16[32,4096]{1,0:T(8,128)(2,1)} async-done(((bf16[512,4096]{1,0:T(8,128)(2,1)}), bf16[32,4096]{1,0:T(8,128)(2,1)}) %reduce-scatter.6.cloned.1.call-update) | async-done | bytes 262160 | tf_op jit(solution)/shard_map/reduce_scatter | solution.py:503
  (656 shorter events, 381.2 us)
Async XLA Ops:
  7.2 191.1 %all-gather.4.cloned.1.call-start = ((), (), s32[]{:S(2)}) async-start(), calls=%async_computation.3 | async-start | bytes 4325376 | tf_op jit(solution)/shard_map/all_gather | solution.py:345
  8.9 196.3 %all-gather.6.cloned.1.call-start = ((), (), s32[]{:S(2)}) async-start(), calls=%async_computation.4 | async-start | bytes 8650752 | tf_op jit(solution)/shard_map/all_gather | solution.py:345
  10.8 230.6 %all-gather.8.cloned.1.call-start = ((), (), s32[]{:S(2)}) async-start(), calls=%async_computation.5 | async-start | bytes 4325376 | tf_op jit(solution)/shard_map/all_gather | solution.py:345
  26.3 503.1 %reduce-scatter.8.cloned.1.call-start = ((), (), s32[]{:S(2)}) async-start(), calls=%async_computation.8 | async-start | bytes 2228224 | tf_op jit(solution)/shard_map/reduce_scatter | solution.py:503
  43.5 25.9 %collective-permute-start.11 = (bf16[48,2304]{1,0:T(8,128)(2,1)}, bf16[48,2304]{1,0:T(8,128)(2,1)S(1)}, u32[]{:S(2)}, u32[]{:S(2)}) collective-permute-start(bf16[48,2304]{1,0:T(8,128)(2,1)} %fence.7), channel_id=1, source_target_pairs={{0,4},{1,5},{2,6},{3,7},{4,0},{5,1},{6,2},{7,3},{8,12},{9,13},{10,... | collective-permute-start | bytes 663560 | tf_op jit(solution)/shard_map/ppermute | solution.py:366
  44.8 24.6 %collective-permute-start.10 = (bf16[48,2304]{1,0:T(8,128)(2,1)}, bf16[48,2304]{1,0:T(8,128)(2,1)S(1)}, u32[]{:S(2)}, u32[]{:S(2)}) collective-permute-start(bf16[48,2304]{1,0:T(8,128)(2,1)} %fence.7), channel_id=1, source_target_pairs={{0,2},{1,3},{2,4},{3,5},{4,6},{5,7},{6,0},{7,1},{8,10},{9,11},{10,... | collective-permute-start | bytes 663560 | tf_op jit(solution)/shard_map/ppermute | solution.py:366
  48.0 38.8 %collective-permute-start.3 = (bf16[4,48,1920]{2,1,0:T(8,128)(2,1)S(1)}, bf16[4,48,1920]{2,1,0:T(8,128)(2,1)S(1)}, u32[]{:S(2)}, u32[]{:S(2)}) collective-permute-start(bf16[4,48,1920]{2,1,0:T(8,128)(2,1)S(1)} %pad_maximum_fusion.13.refs_0_), channel_id=1, source_target_pairs={{0,1},{1,0},{2,3},{3,2},{4,5},{5,4},{6,7},{7,6},{8,9},{9,8},{10,11... | collective-permute-start | bytes 2211848 | tf_op jit(solution)/shard_map/ppermute | solution.py:366
  70.5 28.2 %collective-permute-start.13 = (bf16[4,48,2304]{2,1,0:T(8,128)(2,1)S(1)}, bf16[4,48,2304]{2,1,0:T(8,128)(2,1)}, u32[]{:S(2)}, u32[]{:S(2)}) collective-permute-start(bf16[4,48,2304]{2,1,0:T(8,128)(2,1)S(1)} %pad_maximum_fusion.11.refs_0_), channel_id=1, source_target_pairs={{0,1},{1,0},{2,3},{3,2},{4,5},{5,4},{6,7},{7,6},{8,9},{9,8},{10,11... | collective-permute-start | bytes 2654216 | tf_op jit(solution)/shard_map/ppermute | solution.py:366
  74.2 33.2 %collective-permute-start.6 = (bf16[4,48,1920]{2,1,0:T(8,128)(2,1)S(1)}, bf16[4,48,1920]{2,1,0:T(8,128)(2,1)}, u32[]{:S(2)}, u32[]{:S(2)}) collective-permute-start(bf16[4,48,1920]{2,1,0:T(8,128)(2,1)S(1)} %pad_maximum_fusion.13.refs_0_), channel_id=1, source_target_pairs={{0,8},{1,9},{2,10},{3,11},{4,12},{5,13},{6,14},{7,15},{8,0},{9,1},... | collective-permute-start | bytes 2211848 | tf_op jit(solution)/shard_map/ppermute | solution.py:366
  87.0 25.7 %collective-permute-start.7 = (bf16[4,48,1920]{2,1,0:T(8,128)(2,1)S(1)}, bf16[4,48,1920]{2,1,0:T(8,128)(2,1)}, u32[]{:S(2)}, u32[]{:S(2)}) collective-permute-start(bf16[4,48,1920]{2,1,0:T(8,128)(2,1)S(1)} %collective-permute-done.3.refs_1_), channel_id=1, source_target_pairs={{0,8},{1,9},{2,10},{3,11},{4,12},{5,13},{6,14},{7,15},{8,0},{9,1},... | collective-permute-start | bytes 2211848 | tf_op jit(solution)/shard_map/ppermute | solution.py:366
  107.1 54.7 %collective-permute-start.16 = (bf16[4,48,2304]{2,1,0:T(8,128)(2,1)S(1)}, bf16[4,48,2304]{2,1,0:T(8,128)(2,1)}, u32[]{:S(2)}, u32[]{:S(2)}) collective-permute-start(bf16[4,48,2304]{2,1,0:T(8,128)(2,1)S(1)} %pad_maximum_fusion.11.refs_0_), channel_id=1, source_target_pairs={{0,8},{1,9},{2,10},{3,11},{4,12},{5,13},{6,14},{7,15},{8,0},{9,1},... | collective-permute-start | bytes 2654216 | tf_op jit(solution)/shard_map/ppermute | solution.py:366
  107.4 54.3 %collective-permute-start.18 = (bf16[4,16,2304]{2,1,0:T(8,128)(2,1)S(1)}, bf16[4,16,2304]{2,1,0:T(8,128)(2,1)}, u32[]{:S(2)}, u32[]{:S(2)}) collective-permute-start(bf16[4,16,2304]{2,1,0:T(8,128)(2,1)S(1)} %collective-permute-done.14.refs_2_), channel_id=1, source_target_pairs={{0,8},{1,9},{2,10},{3,11},{4,12},{5,13},{6,14},{7,15},{8,0},{9,1},... | collective-permute-start | bytes 884744 | tf_op jit(solution)/shard_map/ppermute | solution.py:366
  107.7 54.1 %collective-permute-start.17 = (bf16[4,48,2304]{2,1,0:T(8,128)(2,1)}, bf16[4,48,2304]{2,1,0:T(8,128)(2,1)}, u32[]{:S(2)}, u32[]{:S(2)}) collective-permute-start(bf16[4,48,2304]{2,1,0:T(8,128)(2,1)} %collective-permute-done.13.refs_1_), channel_id=1, source_target_pairs={{0,8},{1,9},{2,10},{3,11},{4,12},{5,13},{6,14},{7,15},{8,0},{9,1},... | collective-permute-start | bytes 2654216 | tf_op jit(solution)/shard_map/ppermute | solution.py:366
  111.2 50.5 %collective-permute-start.19 = (bf16[4,16,2304]{2,1,0:T(8,128)(2,1)}, bf16[4,16,2304]{2,1,0:T(8,128)(2,1)}, u32[]{:S(2)}, u32[]{:S(2)}) collective-permute-start(bf16[4,16,2304]{2,1,0:T(8,128)(2,1)} %collective-permute-done.15.refs_3_), channel_id=1, source_target_pairs={{0,8},{1,9},{2,10},{3,11},{4,12},{5,13},{6,14},{7,15},{8,0},{9,1},... | collective-permute-start | bytes 884744 | tf_op jit(solution)/shard_map/ppermute | solution.py:366
  256.0 24.3 %collective-permute-start.20 = (bf16[8,128,1024]{2,1,0:T(8,128)(2,1)}, bf16[8,128,1024]{2,1,0:T(8,128)(2,1)}, u32[]{:S(2)}, u32[]{:S(2)}) collective-permute-start(bf16[8,128,1024]{2,1,0:T(8,128)(2,1)} %dynamic-slice_bitcast_fusion.3.refs_1_), channel_id=1, source_target_pairs={{0,8},{1,9},{2,10},{3,11},{4,12},{5,13},{6,14},{7,15},{8,0},{9,1},... | collective-permute-start | bytes 6291464 | tf_op jit(solution)/shard_map/ppermute | solution.py:366
  271.4 43.5 %collective-permute-start.21 = (bf16[8,64,4096]{2,1,0:T(8,128)(2,1)}, bf16[8,64,4096]{2,1,0:T(8,128)(2,1)}, u32[]{:S(2)}, u32[]{:S(2)}) collective-permute-start(bf16[8,64,4096]{2,1,0:T(8,128)(2,1)} %dynamic-slice_bitcast_fusion.refs_2_), channel_id=1, source_target_pairs={{0,8},{1,9},{2,10},{3,11},{4,12},{5,13},{6,14},{7,15},{8,0},{9,1},... | collective-permute-start | bytes 12582920 | tf_op jit(solution)/shard_map/ppermute | solution.py:366
  300.7 293.7 %reduce-scatter.4.cloned.1.call-start = ((), (), s32[]{:S(2)}) async-start(), calls=%async_computation.6 | async-start | bytes 2506752 | tf_op jit(solution)/shard_map/reduce_scatter | solution.py:503
  312.8 95.8 %collective-permute-start.23 = (bf16[4,2,32,1024]{3,2,1,0:T(8,128)(2,1)}, bf16[4,2,32,1024]{3,2,1,0:T(8,128)(2,1)}, u32[]{:S(2)}, u32[]{:S(2)}) collective-permute-start(bf16[4,2,32,1024]{3,2,1,0:T(8,128)(2,1)} %constant_dynamic-slice_fusion.1.refs_1_), channel_id=1, source_target_pairs={{0,16},{1,17},{2,18},{3,19},{4,20},{5,21},{6,22},{7,23},{8,24},{9,... | collective-permute-start | bytes 1572872 | tf_op jit(solution)/shard_map/ppermute | solution.py:366
  365.5 67.1 %collective-permute-start.24 = (bf16[8,64,2304]{2,1,0:T(8,128)(2,1)}, bf16[8,64,2304]{2,1,0:T(8,128)(2,1)}, u32[]{:S(2)}, u32[]{:S(2)}) collective-permute-start(bf16[8,64,2304]{2,1,0:T(8,128)(2,1)} %dynamic-slice_bitcast_fusion.1.refs_2_), channel_id=1, source_target_pairs={{0,8},{1,9},{2,10},{3,11},{4,12},{5,13},{6,14},{7,15},{8,0},{9,1},... | collective-permute-start | bytes 7077896 | tf_op jit(solution)/shard_map/ppermute | solution.py:366
  454.3 237.3 %reduce-scatter.6.cloned.1.call-start = ((), (), s32[]{:S(2)}) async-start(), calls=%async_computation.7 | async-start | bytes 4456448 | tf_op jit(solution)/shard_map/reduce_scatter | solution.py:503
  489.6 32.6 %collective-permute-start.28 = (bf16[4,2,64,1920]{3,2,0,1:T(8,128)(2,1)}, bf16[4,2,64,1920]{3,2,0,1:T(8,128)(2,1)}, u32[]{:S(2)}, u32[]{:S(2)}) collective-permute-start(bf16[4,2,64,1920]{3,2,0,1:T(8,128)(2,1)} %bitcast.258), channel_id=1, source_target_pairs={{0,8},{1,9},{2,10},{3,11},{4,12},{5,13},{6,14},{7,15},{8,0},{9,1},... | collective-permute-start | bytes 5898248 | tf_op jit(solution)/shard_map/ppermute | solution.py:366
  543.3 37.4 %collective-permute-start.44 = (bf16[128,1024]{1,0:T(8,128)(2,1)S(1)}, bf16[128,1024]{1,0:T(8,128)(2,1)S(1)}, u32[]{:S(2)}, u32[]{:S(2)}) collective-permute-start(bf16[128,1024]{1,0:T(8,128)(2,1)S(1)} %pad_maximum_fusion.21), channel_id=1, source_target_pairs={{0,8},{1,9},{2,10},{3,11},{4,12},{5,13},{6,14},{7,15},{8,0},{9,1},... | collective-permute-start | bytes 786440 | tf_op jit(solution)/shard_map/ppermute | solution.py:366
  557.0 23.6 %collective-permute-start.32 = (bf16[48,1920]{1,0:T(8,128)(2,1)S(1)}, bf16[48,1920]{1,0:T(8,128)(2,1)S(1)}, u32[]{:S(2)}, u32[]{:S(2)}) collective-permute-start(bf16[48,1920]{1,0:T(8,128)(2,1)S(1)} %get-tuple-element.182), channel_id=1, source_target_pairs={{0,4},{1,5},{2,6},{3,7},{4,0},{5,1},{6,2},{7,3},{8,12},{9,13},{10,... | collective-permute-start | bytes 552968 | tf_op jit(solution)/shard_map/ppermute | solution.py:366
  600.3 91.4 %collective-permute-start.27 = (bf16[64,2304]{1,0:T(8,128)(2,1)}, bf16[64,2304]{1,0:T(8,128)(2,1)}, u32[]{:S(2)}, u32[]{:S(2)}) collective-permute-start(bf16[64,2304]{1,0:T(8,128)(2,1)} %pad_maximum_fusion.19), channel_id=1, source_target_pairs={{0,8},{1,9},{2,10},{3,11},{4,12},{5,13},{6,14},{7,15},{8,0},{9,1},... | collective-permute-start | bytes 884744 | tf_op jit(solution)/shard_map/ppermute | solution.py:366
  (178 other events, 1887.5 us)
Sparse Core Ops, SparseCore 0:
  11.5 85.6 all-gather.3
  100.5 76.5 all-gather.5
  180.6 60.7 all-gather.7
  300.8 72.4 reduce-scatter.7
  454.4 139.9 reduce-scatter.3
  596.7 94.9 reduce-scatter.5

commit v8 on v7

--- a/solution.py
+++ b/solution.py
@@ -343,6 +343,15 @@
         rows = own.shape[0] // copies
         part = lax.dynamic_slice_in_dim(own, lax.axis_index(rep) * rows, rows, 0)
     return lax.all_gather(part, shard + rep, axis=0, tiled=True)
+
+
+def gather_two(first, second, rep, shard):
+    rows = first.shape[0] // lax.axis_size(rep)
+    start = lax.axis_index(rep) * rows
+    parts = [lax.dynamic_slice_in_dim(master, start, rows, 0) for master in (first, second)]
+    own = jnp.stack(parts).astype(jnp.bfloat16)
+    every = lax.all_gather(own, shard + rep, axis=0, tiled=False)
+    return [every[:, index].reshape(-1, first.shape[1]) for index in range(2)]
 
 
 def general_reduce(grad, rep, shard):
@@ -584,8 +593,12 @@
         pieces = tuned_gather(pieces)
     else:
         pieces = [general_gather(piece, rep, shard) for piece in pieces]
-    for master in (mixer_out, swiglu_in, swiglu_out):
-        pieces.append(general_gather(master.astype(jnp.bfloat16), rep, shard))
+    if tuned(axes):
+        w_out, w_down = gather_two(mixer_out, swiglu_out, rep, shard)
+        pieces += [w_out, general_gather(swiglu_in.astype(jnp.bfloat16), rep, shard), w_down]
+    else:
+        for master in (mixer_out, swiglu_in, swiglu_out):
+            pieces.append(general_gather(master.astype(jnp.bfloat16), rep, shard))
     every = pieces[0][:, CONV + MH : CONV + MH + lanes].reshape(owners, rows * lanes)
     gains_all = every[:, : gains.shape[0]].reshape(-1)
     taps = every[:, gains.shape[0] : count].reshape(owners, KC + 1, width)
@@ -669,12 +682,12 @@
     hidden_part, gain_ff = pull_ff(ff_cot)
     hidden_cot = cot.astype(jnp.float32) + hidden_part
     hidden_low = rows_of(hidden_cot)
-    moving.add("out", dot_left(joined, hidden_low))
+    moving.add("out", dot_left(joined, hidden_low), paired=True)
     (joined_cot,) = moving.step([dot_right(hidden_low, w_out)])
     scan_cot, gate_cot, gain_scan = pull_gating(joined_cot[:, context_width:])
     (qkv_cot,) = pull_context(joined_cot[:, :context_width])
     side_cot = jnp.concatenate([rows_of(qkv_cot), rows_of(gate_cot)], axis=1)
-    moving.add("side", dot_left(normed_low, side_cot), paired=True)
+    moving.add("side", dot_left(normed_low, side_cot))
     (scan_cot,) = moving.step([scan_cot])
     conv_out_cot, dstep, dcum, dskip = scan_backward(
         scan_cot, scan_out, conv_low, step_size, cumulative, head_params, segment
@@ -735,7 +748,7 @@
     own_gains, own_taps, head_grad = split_vectors(
         sums["conv"], gains.shape[0], conv_kernel.shape[1], head_params.shape
     )
-    matrix = jnp.concatenate([sums["side"], sums["conv"][:, : CONV + MH]], axis=1)
+    matrix = jnp.concatenate([sums["side"].T, sums["conv"][:, : CONV + MH].T], axis=0)
     owned = (
         matrix.astype(jnp.float32),
         sums["out"].astype(jnp.float32),
@@ -762,9 +775,10 @@
         conv_kernel_square,
     )
     rates = (MATRIX_RATE, MATRIX_RATE, MATRIX_RATE, MATRIX_RATE, VECTOR_RATE, VECTOR_RATE)
-    updated = [
+    turned = adamw(mixer_in.T, mixer_in_mean.T, mixer_in_square.T, owned[0], rates[0])
+    updated = [tuple(array.T for array in turned)] + [
         adamw(masters[index], means[index], squares[index], owned[index], rates[index])
-        for index in range(6)
+        for index in range(1, 6)
     ]
     head_new = adamw(head_params, head_params_mean, head_params_square, head_grad, VECTOR_RATE)
     return (

time: 735 us -> 631 us (0.86)
  waiting for transfers between devices: 245 us -> 142 us
  starting transfers between devices: 50.7 us -> 61.7 us
  matrix products: 105 us -> 97.4 us
    reduce_scatter x3, waiting for transfers between devices: 87.5 us -> 0.01 us  [paired_reduce(): lax.psum_scatter(half, ('z', 'y', 'x'), scatter_dimension=0, tiled=True)]
    all_gather x3 -> x1, waiting for transfers between devices: 25.6 us -> 0.02 us  [general_gather(): return lax.all_gather(part, shard + rep, axis=0, tiled=True)]
    ppermute x45, starting transfers between devices: 50.5 us -> 61 us  [send(): return lax.ppermute(values, ('x', 'core', 'z', 'y'), pairs)]
    ppermute x45, waiting for transfers between devices: 132 us -> 142 us  [send(): return lax.ppermute(values, ('x', 'core', 'z', 'y'), pairs)]
    transpose x0 -> x3, other arithmetic: none -> 7.65 us  [the longest x1 6.79 us: on_device(): updated = [tuple((array.T for array in turned))] + [adamw(masters[index],...]
    unnamed x305 -> x295, local copies, waits for them, and re-layouts: 62.1 us -> 55.4 us
    another operation x14 -> x15, other arithmetic: 15.9 us -> 16.3 us
  transfers between devices with their start and end apart: 51 -> 50, of which waited for: 19 -> 17; matrix products, arithmetic and copies ran while one was open for 43% -> 48% of each run, Pallas kernels for 5% -> 6%
where the time goes in v8:
time: 631 us; the launch traced here: 627 us
  other arithmetic  154 us (24%)
  waiting for transfers between devices  142 us (23%)
  local copies, waits for them, and re-layouts  120 us (19%)
  matrix products  97.4 us (15%)
  starting transfers between devices  61.7 us (10%)
  Pallas kernels  35.2 us (6%)
  between operations  16.1 us (3%)
    ppermute x45, waiting for transfers between devices, send(): return lax.ppermute(values, ('x', 'core', 'z', 'y'), pairs)  142 us
    ppermute x45, starting transfers between devices, send(): return lax.ppermute(values, ('x', 'core', 'z', 'y'), pairs)  61 us
    unnamed x295, local copies, waits for them, and re-layouts  55.4 us
    dot_general x5, matrix products, dot_right(): lax.dot_general(left, right, (((1,), (1,)), ((), ())), preferred_element_...  30.8 us
    dot_general x6, matrix products, dot(): return jnp.dot(left, right, preferred_element_type=jnp.float32)  27.6 us
    convert_element_type x11, other arithmetic, add_low(): (left.astype(jnp.float32) + right.astype(jnp.float32)).astype(jnp.bfloat16)  23.6 us
    convert_element_type x5, other arithmetic, round_value(): values.astype(jnp.bfloat16)  19.3 us
    pallas_call x1, Pallas kernels, scan_backward(): pl.pallas_call(scan_backward_kernel, grid=(MH // 2,), out_shape=[jax.Shap...  18.8 us
  transfers between devices with their start and end apart: 50, of which 17 were waited for; matrix products, arithmetic and copies ran while one was open for 48% of the time, Pallas kernels for 6%

profile of v8, /device:TPU:1, one launch (start us, length us, event | category | flops | bytes accessed | tf_op | source)
XLA Modules:
  0.0 626.5 jit_solution(535863226951815104)
XLA Ops:
  30.4 14.7 %collective-permute-done.1.refs_2_ = bf16[48,1920]{1,0:T(8,128)(2,1)S(1)} collective-permute-done((bf16[48,1920]{1,0:T(8,128)(2,1)}, bf16[48,1920]{1,0:T(8,128)(2,1)S(1)}, u32[]{:S(2)}, u32[]{:S(2)}) %collective-permute-start.1) | collective-permute-done | bytes 184352 | tf_op jit(solution)/shard_map/ppermute | solution.py:375
  58.7 20.3 %collective-permute-done.11 = bf16[48,2304]{1,0:T(8,128)(2,1)S(1)} collective-permute-done((bf16[48,2304]{1,0:T(8,128)(2,1)}, bf16[48,2304]{1,0:T(8,128)(2,1)S(1)}, u32[]{:S(2)}, u32[]{:S(2)}) %collective-permute-start.11) | collective-permute-done | bytes 221216 | tf_op jit(solution)/shard_map/ppermute | solution.py:375
  85.4 8.5 %collective-permute-done.4.refs_2_ = bf16[4,16,1920]{2,1,0:T(8,128)(2,1)S(1)} collective-permute-done((bf16[4,16,1920]{2,1,0:T(8,128)(2,1)S(1)}, bf16[4,16,1920]{2,1,0:T(8,128)(2,1)S(1)}, u32[]{:S(2)}, u32[]{:S(2)}) %collective-permute-start.4) | collective-permute-done | bytes 245792 | tf_op jit(solution)/shard_map/ppermute | solution.py:375
  100.8 8.4 %collective-permute-done.5.refs_3_ = bf16[4,16,1920]{2,1,0:T(8,128)(2,1)} collective-permute-done((bf16[4,16,1920]{2,1,0:T(8,128)(2,1)S(1)}, bf16[4,16,1920]{2,1,0:T(8,128)(2,1)}, u32[]{:S(2)}, u32[]{:S(2)}) %collective-permute-start.5) | collective-permute-done | bytes 245792 | tf_op jit(solution)/shard_map/ppermute | solution.py:375
  109.3 6.5 %collective-permute-done.13.refs_1_ = bf16[4,48,2304]{2,1,0:T(8,128)(2,1)} collective-permute-done((bf16[4,48,2304]{2,1,0:T(8,128)(2,1)S(1)}, bf16[4,48,2304]{2,1,0:T(8,128)(2,1)}, u32[]{:S(2)}, u32[]{:S(2)}) %collective-permute-start.13) | collective-permute-done | bytes 884768 | tf_op jit(solution)/shard_map/ppermute | solution.py:375
  151.1 9.2 %multiply_convert_fusion.1 = (bf16[512,1792]{1,0:T(8,128)(2,1)S(1)}, f32[512,1792]{1,0:T(8,128)}) fusion(f32[509,1792]{1,0:T(8,128)} %slice.332, pred[512]{0:T(512)(128)(4,1)} %get-tuple-element.269, f32[1792]{0:T(1024)S(1)} %mul.775, f32[510,1792]{1,0:T(8,128)} %slice.330, pred[512]{0:T(512)(128)(4,1)S(1)} %copy-done.124, f32[1792]{0:T(1024)S(1)} %mul.772, ...), kind=kLoop, calls=%fused_computation.64 | loop fusion | flops 14680064 | bytes 20179456 | tf_op jit(solution)/shard_map/jvp()/convert_element_type | solution.py:35
  170.2 7.8 %scan_forward.1.out_ref = f32[512,1536]{1,0:T(8,128)S(1)} custom-call(bf16[512,1792]{1,0:T(8,128)(2,1)S(1)} %get-tuple-element.201.x_ref.b_ref.c_ref, bf16[512,1792]{1,0:T(8,128)(2,1)S(1)} %get-tuple-element.201.x_ref.b_ref.c_ref, bf16[512,1792]{1,0:T(8,128)(2,1)S(1)} %get-tuple-element.201.x_ref.b_ref.c_ref, f32[12,512,2]{2,1,0:T(8,128)S(1)} %bitcast.301, ...), custom_call_target="tpu_custom_call" | custom-call | tf_op jit(solution)/shard_map/scan_forward/pallas_call | solution.py:271
  194.2 7.5 %fusion.135 = (f32[2,4,512]{2,1,0:T(4,128)S(1)}, f32[2,4,512,512]{2,3,1,0:T(8,128)}) fusion(pred[512,512]{0,1:T(8,128)(4,1)S(1)} %copy-done.71, bf16[512,2,4,64]{0,3,2,1:T(8,128)(2,1)} %bitcast.347, bf16[512,2,64]{0,2,1:T(8,128)(2,1)S(1)} %pad_maximum_fusion.26), kind=kOutput, calls=%fused_computation.348 | convolution fusion | flops 276824576 | bytes 9322496 | tf_op jit(solution)/shard_map/jvp()/sub | solution.py:130
  201.8 6.9 %divide_convert_fusion = bf16[2,4,512,512]{2,3,1,0:T(8,128)(2,1)} fusion(f32[2,4,512,512]{2,3,1,0:T(8,128)} %get-tuple-element.271, f32[2,4,512]{2,1,0:T(4,128)S(1)} %get-tuple-element.270), kind=kLoop, calls=%fused_computation.12 | loop fusion | flops 4194304 | bytes 12599296 | tf_op jit(solution)/shard_map/jvp()/convert_element_type | solution.py:35
  222.5 10.4 %fusion.142 = f32[512,4096]{1,0:T(8,128)} fusion(bf16[512,1024]{1,0:T(8,128)(2,1)S(1)} %multiply_convert_fusion.3, bf16[1024,4096]{1,0:T(8,128)(2,1)} %all-gather.5.cloned.1.call-done), kind=kOutput, calls=%fused_computation.351 | convolution fusion | flops 4294967296 | bytes 17825792 | tf_op jit(solution)/shard_map/dot_general | solution.py:97
  232.9 6.4 %fusion.68 = (f32[512,2048]{1,0:T(8,128)S(1)}, f32[512,2048]{1,0:T(8,128)S(1)}, bf16[512,2048]{1,0:T(8,128)(2,1)S(1)}) fusion(f32[512,4096]{1,0:T(8,128)} %fusion.142, bf16[2048,1024]{1,0:T(8,128)(2,1)S(1)} %bitcast.334, bf16[512,1024]{1,0:T(8,128)(2,1)S(1)} %copy-done.65, pred[512]{0:T(512)(128)(4,1)S(1)} %copy-done.137), kind=kOutput, calls=%fused_computation.183 | convolution fusion | flops 2162688000 | bytes 24117760 | tf_op jit(solution)/shard_map/dot_general | solution.py:105
  247.9 7.0 %convolution_convert_fusion = bf16[1024,4096]{1,0:T(8,128)(2,1)S(1)} fusion(bf16[512,1024]{1,0:T(8,128)(2,1)S(1)} %multiply_convert_fusion.3, bf16[512,4096]{1,0:T(8,128)(2,1)} %fence.8), kind=kOutput, calls=%fused_computation.14 | convolution fusion | flops 4299161600 | bytes 13631488 | tf_op jit(solution)/shard_map/dot_general | solution.py:101
  265.1 10.5 %fusion.143.refs_0_ = f32[512,1024]{1,0:T(8,128)} fusion(bf16[512,4096]{1,0:T(8,128)(2,1)} %fence.8, bf16[1024,4096]{1,0:T(8,128)(2,1)} %all-gather.5.cloned.1.call-done), kind=kOutput, calls=%fused_computation.352 | convolution fusion | flops 4294967296 | bytes 14680064 | tf_op jit(solution)/shard_map/dot_general | solution.py:105
  298.1 7.0 %add_convert_fusion.2 = bf16[512,1024]{1,0:T(8,128)(2,1)} fusion(f32[512,1024]{1,0:T(8,128)} %copy-done.22, bf16[512,2048]{1,0:T(8,128)(2,1)} %copy-done.139, bf16[2048,1024]{1,0:T(8,128)(2,1)} %bitcast.333), kind=kOutput, calls=%fused_computation.113 | convolution fusion | flops 2148532224 | bytes 9437184 | tf_op jit(solution)/shard_map/dot_general | solution.py:97
  313.1 7.2 %fusion.1 = bf16[8,64,4096]{2,1,0:T(8,128)(2,1)} fusion(bf16[8,64,4096]{2,1,0:T(8,128)(2,1)} %collective-permute-done.21, bf16[8,2,64,4096]{3,2,1,0:T(8,128)(2,1)} %bitcast.318, s32[]{:T(128)S(6)} %select_n.317), kind=kLoop, calls=%fused_computation.2 | loop fusion | flops 8388608 | bytes 12582916 | tf_op jit(solution)/shard_map/convert_element_type | solution.py:461
  365.9 18.8 %scan_backward.1 = (f32[512,1536]{1,0:T(8,128)S(1)}, f32[12,512,2]{2,1,0:T(8,128)S(1)}, f32[12,512,2]{2,1,0:T(8,128)S(1)}, f32[1,1536]{1,0:T(1,128)S(1)}, bf16[512,512]{1,0:T(8,128)(2,1)S(1)}) custom-call(f32[512,1536]{1,0:T(8,128)S(1)} %copy-done.5, f32[512,1536]{1,0:T(8,128)S(1)} %copy-done.2, bf16[512,1792]{1,0:T(8,128)(2,1)S(1)} %get-tuple-element.201.x_ref.b_ref.c_ref, ...), custom_call_target="tpu_custom_call" | custom-call | tf_op jit(solution)/shard_map/scan_backward/pallas_call | solution.py:289
  420.7 9.9 %multiply_reduce_fusion.4 = (f32[1792]{0:T(1024)S(1)}, f32[1792]{0:T(1024)S(1)}, f32[1792]{0:T(1024)S(1)}, f32[1792]{0:T(1024)S(1)}, f32[1792]{0:T(1024)S(1)}, /*index=5*/f32[512,1792]{1,0:T(8,128)S(1)}) fusion(f32[509,1792]{1,0:T(8,128)} %slice.332, pred[512]{0:T(512)(128)(4,1)S(1)} %copy-done.128, f32[512,1920]{1,0:T(8,128)} %copy-done.16, ...), kind=kLoop, calls=%fused_computation.62 | loop fusion | flops 19258624 | bytes 25684480 | tf_op jit(solution)/shard_map/transpose(jvp())/reduce_sum | solution.py:146
  480.2 15.7 %collective-permute-done.25 = bf16[4,48,2304]{2,1,0:T(8,128)(2,1)} collective-permute-done((bf16[4,48,2304]{2,1,0:T(8,128)(2,1)}, bf16[4,48,2304]{2,1,0:T(8,128)(2,1)}, u32[]{:S(2)}, u32[]{:S(2)}) %collective-permute-start.25) | collective-permute-done | bytes 884768 | tf_op jit(solution)/shard_map/ppermute | solution.py:375
  500.3 7.9 %collective-permute-done.28 = bf16[48,2304]{1,0:T(8,128)(2,1)S(1)} collective-permute-done((bf16[48,2304]{1,0:T(8,128)(2,1)S(1)}, bf16[48,2304]{1,0:T(8,128)(2,1)S(1)}, u32[]{:S(2)}, u32[]{:S(2)}) %collective-permute-start.28) | collective-permute-done | bytes 221216 | tf_op jit(solution)/shard_map/ppermute | solution.py:375
  508.2 18.5 %collective-permute-done.27 = bf16[48,2304]{1,0:T(8,128)(2,1)S(1)} collective-permute-done((bf16[48,2304]{1,0:T(8,128)(2,1)S(1)}, bf16[48,2304]{1,0:T(8,128)(2,1)S(1)}, u32[]{:S(2)}, u32[]{:S(2)}) %collective-permute-start.27) | collective-permute-done | bytes 221216 | tf_op jit(solution)/shard_map/ppermute | solution.py:375
  552.7 9.1 %collective-permute-done.33 = bf16[4,48,1920]{2,1,0:T(8,128)(2,1)S(1)} collective-permute-done((bf16[4,48,1920]{2,1,0:T(8,128)(2,1)S(1)}, bf16[4,48,1920]{2,1,0:T(8,128)(2,1)S(1)}, u32[]{:S(2)}, u32[]{:S(2)}) %collective-permute-start.33) | collective-permute-done | bytes 737312 | tf_op jit(solution)/shard_map/ppermute | solution.py:375
  568.4 7.8 %collective-permute-done.35 = bf16[48,1920]{1,0:T(8,128)(2,1)S(1)} collective-permute-done((bf16[48,1920]{1,0:T(8,128)(2,1)S(1)}, bf16[48,1920]{1,0:T(8,128)(2,1)S(1)}, u32[]{:S(2)}, u32[]{:S(2)}) %collective-permute-start.35) | collective-permute-done | bytes 184352 | tf_op jit(solution)/shard_map/ppermute | solution.py:375
  582.0 8.1 %collective-permute-start.38 = (bf16[64,1920]{1,0:T(8,128)(2,1)S(1)}, bf16[64,1920]{1,0:T(8,128)(2,1)S(1)}, u32[]{:S(2)}, u32[]{:S(2)}) collective-permute-start(bf16[64,1920]{1,0:T(8,128)(2,1)S(1)} %pad_maximum_fusion.23), channel_id=1, source_target_pairs={{0,8},{1,9},{2,10},{3,11},{4,12},{5,13},{6,14},{7,15},{8,0},{9,1},... | collective-permute-start | bytes 737288 | tf_op jit(solution)/shard_map/ppermute | solution.py:375
  594.8 6.8 %fusion.52 = (f32[128,4120]{1,0:T(8,128)}, f32[128,4120]{1,0:T(8,128)}, f32[128,4120]{1,0:T(8,128)}) fusion(f32[128,4120]{1,0:T(8,128)} %copy.239, bf16[1816,128]{0,1:T(8,128)(2,1)} %maximum_bitcast_fusion.1, bf16[2304,128]{0,1:T(8,128)(2,1)S(1)} %maximum_bitcast_fusion, f32[128,4120]{1,0:T(8,128)} %copy.234, f32[128,4120]{1,0:T(8,128)S(1)} %copy-done.20), kind=kLoop, calls=%fused_computation.134 | loop fusion | flops 10019840 | bytes 13711360 | tf_op jit(solution)/shard_map/transpose | solution.py:779
  (645 shorter events, 369.4 us)
Async XLA Ops:
  7.2 205.7 %all-gather.3.cloned.1.call-start = ((), (), s32[]{:S(2)}) async-start(), calls=%async_computation.3 | async-start | bytes 8650752 | tf_op jit(solution)/shard_map/all_gather | solution.py:353
  9.1 213.4 %all-gather.5.cloned.1.call-start = ((), (), s32[]{:S(2)}) async-start(), calls=%async_computation.4 | async-start | bytes 8650752 | tf_op jit(solution)/shard_map/all_gather | solution.py:345
  10.9 395.7 %reduce-scatter.8.cloned.1.call-start = ((), (), s32[]{:S(2)}) async-start(), calls=%async_computation.7 | async-start | bytes 2228224 | tf_op jit(solution)/shard_map/reduce_scatter | solution.py:512
  46.4 32.6 %collective-permute-start.11 = (bf16[48,2304]{1,0:T(8,128)(2,1)}, bf16[48,2304]{1,0:T(8,128)(2,1)S(1)}, u32[]{:S(2)}, u32[]{:S(2)}) collective-permute-start(bf16[48,2304]{1,0:T(8,128)(2,1)} %fence.7), channel_id=1, source_target_pairs={{0,4},{1,5},{2,6},{3,7},{4,0},{5,1},{6,2},{7,3},{8,12},{9,13},{10,... | collective-permute-start | bytes 663560 | tf_op jit(solution)/shard_map/ppermute | solution.py:375
  48.2 30.8 %collective-permute-start.10 = (bf16[48,2304]{1,0:T(8,128)(2,1)}, bf16[48,2304]{1,0:T(8,128)(2,1)S(1)}, u32[]{:S(2)}, u32[]{:S(2)}) collective-permute-start(bf16[48,2304]{1,0:T(8,128)(2,1)} %fence.7), channel_id=1, source_target_pairs={{0,2},{1,3},{2,4},{3,5},{4,6},{5,7},{6,0},{7,1},{8,10},{9,11},{10,... | collective-permute-start | bytes 663560 | tf_op jit(solution)/shard_map/ppermute | solution.py:375
  51.4 45.0 %collective-permute-start.3 = (bf16[4,48,1920]{2,1,0:T(8,128)(2,1)S(1)}, bf16[4,48,1920]{2,1,0:T(8,128)(2,1)S(1)}, u32[]{:S(2)}, u32[]{:S(2)}) collective-permute-start(bf16[4,48,1920]{2,1,0:T(8,128)(2,1)S(1)} %pad_maximum_fusion.13.refs_0_), channel_id=1, source_target_pairs={{0,1},{1,0},{2,3},{3,2},{4,5},{5,4},{6,7},{7,6},{8,9},{9,8},{10,11... | collective-permute-start | bytes 2211848 | tf_op jit(solution)/shard_map/ppermute | solution.py:375
  80.1 35.7 %collective-permute-start.13 = (bf16[4,48,2304]{2,1,0:T(8,128)(2,1)S(1)}, bf16[4,48,2304]{2,1,0:T(8,128)(2,1)}, u32[]{:S(2)}, u32[]{:S(2)}) collective-permute-start(bf16[4,48,2304]{2,1,0:T(8,128)(2,1)S(1)} %pad_maximum_fusion.11.refs_0_), channel_id=1, source_target_pairs={{0,1},{1,0},{2,3},{3,2},{4,5},{5,4},{6,7},{7,6},{8,9},{9,8},{10,11... | collective-permute-start | bytes 2654216 | tf_op jit(solution)/shard_map/ppermute | solution.py:375
  83.6 40.7 %collective-permute-start.6 = (bf16[4,48,1920]{2,1,0:T(8,128)(2,1)S(1)}, bf16[4,48,1920]{2,1,0:T(8,128)(2,1)}, u32[]{:S(2)}, u32[]{:S(2)}) collective-permute-start(bf16[4,48,1920]{2,1,0:T(8,128)(2,1)S(1)} %pad_maximum_fusion.13.refs_0_), channel_id=1, source_target_pairs={{0,8},{1,9},{2,10},{3,11},{4,12},{5,13},{6,14},{7,15},{8,0},{9,1},... | collective-permute-start | bytes 2211848 | tf_op jit(solution)/shard_map/ppermute | solution.py:375
  97.6 31.1 %collective-permute-start.7 = (bf16[4,48,1920]{2,1,0:T(8,128)(2,1)S(1)}, bf16[4,48,1920]{2,1,0:T(8,128)(2,1)}, u32[]{:S(2)}, u32[]{:S(2)}) collective-permute-start(bf16[4,48,1920]{2,1,0:T(8,128)(2,1)S(1)} %collective-permute-done.3.refs_1_), channel_id=1, source_target_pairs={{0,8},{1,9},{2,10},{3,11},{4,12},{5,13},{6,14},{7,15},{8,0},{9,1},... | collective-permute-start | bytes 2211848 | tf_op jit(solution)/shard_map/ppermute | solution.py:375
  124.0 54.0 %collective-permute-start.16 = (bf16[4,48,2304]{2,1,0:T(8,128)(2,1)S(1)}, bf16[4,48,2304]{2,1,0:T(8,128)(2,1)}, u32[]{:S(2)}, u32[]{:S(2)}) collective-permute-start(bf16[4,48,2304]{2,1,0:T(8,128)(2,1)S(1)} %pad_maximum_fusion.11.refs_0_), channel_id=1, source_target_pairs={{0,8},{1,9},{2,10},{3,11},{4,12},{5,13},{6,14},{7,15},{8,0},{9,1},... | collective-permute-start | bytes 2654216 | tf_op jit(solution)/shard_map/ppermute | solution.py:375
  124.3 53.6 %collective-permute-start.18 = (bf16[4,16,2304]{2,1,0:T(8,128)(2,1)S(1)}, bf16[4,16,2304]{2,1,0:T(8,128)(2,1)}, u32[]{:S(2)}, u32[]{:S(2)}) collective-permute-start(bf16[4,16,2304]{2,1,0:T(8,128)(2,1)S(1)} %collective-permute-done.14.refs_2_), channel_id=1, source_target_pairs={{0,8},{1,9},{2,10},{3,11},{4,12},{5,13},{6,14},{7,15},{8,0},{9,1},... | collective-permute-start | bytes 884744 | tf_op jit(solution)/shard_map/ppermute | solution.py:375
  124.6 53.4 %collective-permute-start.17 = (bf16[4,48,2304]{2,1,0:T(8,128)(2,1)}, bf16[4,48,2304]{2,1,0:T(8,128)(2,1)}, u32[]{:S(2)}, u32[]{:S(2)}) collective-permute-start(bf16[4,48,2304]{2,1,0:T(8,128)(2,1)} %collective-permute-done.13.refs_1_), channel_id=1, source_target_pairs={{0,8},{1,9},{2,10},{3,11},{4,12},{5,13},{6,14},{7,15},{8,0},{9,1},... | collective-permute-start | bytes 2654216 | tf_op jit(solution)/shard_map/ppermute | solution.py:375
  127.9 50.1 %collective-permute-start.19 = (bf16[4,16,2304]{2,1,0:T(8,128)(2,1)}, bf16[4,16,2304]{2,1,0:T(8,128)(2,1)}, u32[]{:S(2)}, u32[]{:S(2)}) collective-permute-start(bf16[4,16,2304]{2,1,0:T(8,128)(2,1)} %collective-permute-done.15.refs_3_), channel_id=1, source_target_pairs={{0,8},{1,9},{2,10},{3,11},{4,12},{5,13},{6,14},{7,15},{8,0},{9,1},... | collective-permute-start | bytes 884744 | tf_op jit(solution)/shard_map/ppermute | solution.py:375
  260.5 52.7 %collective-permute-start.21 = (bf16[8,64,4096]{2,1,0:T(8,128)(2,1)}, bf16[8,64,4096]{2,1,0:T(8,128)(2,1)}, u32[]{:S(2)}, u32[]{:S(2)}) collective-permute-start(bf16[8,64,4096]{2,1,0:T(8,128)(2,1)} %dynamic-slice_bitcast_fusion.refs_2_), channel_id=1, source_target_pairs={{0,8},{1,9},{2,10},{3,11},{4,12},{5,13},{6,14},{7,15},{8,0},{9,1},... | collective-permute-start | bytes 12582920 | tf_op jit(solution)/shard_map/ppermute | solution.py:375
  264.6 264.2 %reduce-scatter.4.cloned.1.call-start = ((), (), s32[]{:S(2)}) async-start(), calls=%async_computation.5 | async-start | bytes 2228224 | tf_op jit(solution)/shard_map/reduce_scatter | solution.py:512
  313.1 280.1 %reduce-scatter.6.cloned.1.call-start = ((), (), s32[]{:S(2)}) async-start(), calls=%async_computation.6 | async-start | bytes 4456448 | tf_op jit(solution)/shard_map/reduce_scatter | solution.py:512
  359.7 56.4 %collective-permute-start.23 = (bf16[4,2,64,2304]{3,2,1,0:T(8,128)(2,1)}, bf16[4,2,64,2304]{3,2,1,0:T(8,128)(2,1)}, u32[]{:S(2)}, u32[]{:S(2)}) collective-permute-start(bf16[4,2,64,2304]{3,2,1,0:T(8,128)(2,1)} %dynamic-slice_bitcast_fusion.1.refs_2_), channel_id=1, source_target_pairs={{0,8},{1,9},{2,10},{3,11},{4,12},{5,13},{6,14},{7,15},{8,0},{9,1},... | collective-permute-start | bytes 7077896 | tf_op jit(solution)/shard_map/ppermute | solution.py:375
  415.6 33.0 %collective-permute-start.44 = (bf16[128,1024]{1,0:T(8,128)(2,1)}, bf16[128,1024]{1,0:T(8,128)(2,1)}, u32[]{:S(2)}, u32[]{:S(2)}) collective-permute-start(bf16[128,1024]{1,0:T(8,128)(2,1)} %pad_maximum_fusion.22), channel_id=1, source_target_pairs={{0,8},{1,9},{2,10},{3,11},{4,12},{5,13},{6,14},{7,15},{8,0},{9,1},... | collective-permute-start | bytes 786440 | tf_op jit(solution)/shard_map/ppermute | solution.py:375
  420.0 32.3 %collective-permute-start.24 = (bf16[4,2,16,2304]{3,2,1,0:T(8,128)(2,1)}, bf16[4,2,16,2304]{3,2,1,0:T(8,128)(2,1)}, u32[]{:S(2)}, u32[]{:S(2)}) collective-permute-start(bf16[4,2,16,2304]{3,2,1,0:T(8,128)(2,1)} %constant_dynamic-slice_fusion.1.refs_1_), channel_id=1, source_target_pairs={{0,16},{1,17},{2,18},{3,19},{4,20},{5,21},{6,22},{7,23},{8,24},{9,... | collective-permute-start | bytes 1769480 | tf_op jit(solution)/shard_map/ppermute | solution.py:375
  455.3 40.6 %collective-permute-start.25 = (bf16[4,48,2304]{2,1,0:T(8,128)(2,1)}, bf16[4,48,2304]{2,1,0:T(8,128)(2,1)}, u32[]{:S(2)}, u32[]{:S(2)}) collective-permute-start(bf16[4,48,2304]{2,1,0:T(8,128)(2,1)} %pad_maximum_fusion.12.refs_1_), channel_id=1, source_target_pairs={{0,1},{1,0},{2,3},{3,2},{4,5},{5,4},{6,7},{7,6},{8,9},{9,8},{10,11... | collective-permute-start | bytes 2654216 | tf_op jit(solution)/shard_map/ppermute | solution.py:375
  479.9 54.3 %collective-permute-start.31 = (bf16[4,2,64,1920]{3,2,0,1:T(8,128)(2,1)}, bf16[4,2,64,1920]{3,2,0,1:T(8,128)(2,1)}, u32[]{:S(2)}, u32[]{:S(2)}) collective-permute-start(bf16[4,2,64,1920]{3,2,0,1:T(8,128)(2,1)} %bitcast.297), channel_id=1, source_target_pairs={{0,8},{1,9},{2,10},{3,11},{4,12},{5,13},{6,14},{7,15},{8,0},{9,1},... | collective-permute-start | bytes 5898248 | tf_op jit(solution)/shard_map/ppermute | solution.py:375
  497.5 29.3 %collective-permute-start.27 = (bf16[48,2304]{1,0:T(8,128)(2,1)S(1)}, bf16[48,2304]{1,0:T(8,128)(2,1)S(1)}, u32[]{:S(2)}, u32[]{:S(2)}) collective-permute-start(bf16[48,2304]{1,0:T(8,128)(2,1)S(1)} %get-tuple-element.227), channel_id=1, source_target_pairs={{0,4},{1,5},{2,6},{3,7},{4,0},{5,1},{6,2},{7,3},{8,12},{9,13},{10,... | collective-permute-start | bytes 663560 | tf_op jit(solution)/shard_map/ppermute | solution.py:375
  498.9 27.8 %collective-permute-start.26 = (bf16[48,2304]{1,0:T(8,128)(2,1)S(1)}, bf16[48,2304]{1,0:T(8,128)(2,1)S(1)}, u32[]{:S(2)}, u32[]{:S(2)}) collective-permute-start(bf16[48,2304]{1,0:T(8,128)(2,1)S(1)} %get-tuple-element.225), channel_id=1, source_target_pairs={{0,2},{1,3},{2,4},{3,5},{4,6},{5,7},{6,0},{7,1},{8,10},{9,11},{10,... | collective-permute-start | bytes 663560 | tf_op jit(solution)/shard_map/ppermute | solution.py:375
  548.7 30.0 %collective-permute-start.40 = (bf16[128,1024]{1,0:T(8,128)(2,1)S(1)}, bf16[128,1024]{1,0:T(8,128)(2,1)S(1)}, u32[]{:S(2)}, u32[]{:S(2)}) collective-permute-start(bf16[128,1024]{1,0:T(8,128)(2,1)S(1)} %pad_maximum_fusion.21), channel_id=1, source_target_pairs={{0,8},{1,9},{2,10},{3,11},{4,12},{5,13},{6,14},{7,15},{8,0},{9,1},... | collective-permute-start | bytes 786440 | tf_op jit(solution)/shard_map/ppermute | solution.py:375
  (173 other events, 1641.1 us)
Sparse Core Ops, SparseCore 0:
  11.5 117.2 all-gather.2
  132.2 74.5 all-gather.4
  264.8 68.2 reduce-scatter.7
  335.8 77.8 reduce-scatter.3
  415.8 104.3 reduce-scatter.5

commit v9 on v8

--- a/solution.py
+++ b/solution.py
@@ -478,12 +478,12 @@
     yield [there]
     column = add_low(here, send(there, dy=1))
     turns = [pick(column, (z + turn) % 4, 0) for turn in range(1, 4)]
-    yield turns
+    turns = (yield turns) or turns
     total = pick(column, z, 0).astype(jnp.float32)
     for turn in range(1, 4):
         total = total + send(turns[turn - 1], dz=turn).astype(jnp.float32)
     total = total.astype(jnp.bfloat16)
-    yield [total]
+    (total,) = (yield [total]) or (total,)
     across = send(total, dx=1)
     own_x, other_x = total[:quarter], across[:quarter]
     owned = jnp.concatenate(
@@ -494,7 +494,7 @@
         ],
         axis=0,
     )
-    yield [owned]
+    (owned,) = (yield [owned]) or (owned,)
     beside = send(owned, dcore=1)
     return jnp.concatenate(
         [jnp.where(core == 0, owned, beside), jnp.where(core == 0, beside, owned)], axis=0
@@ -561,6 +561,17 @@
             self.results[name] = stop.value
             del self.running[name]
             return []
+
+    def interleave(self, first, second):
+        next(self.running[first])
+        reply = None
+        try:
+            while True:
+                ahead = next(self.running[first])
+                reply = fence(self.running[second].send(reply), ahead)
+        except StopIteration as stop:
+            self.results[second] = stop.value
+            del self.running[second]
 
     def finish(self):
         while self.running:
@@ -711,6 +722,8 @@
         "conv",
         with_vectors(dot_left(normed_low, conv_cot), gains_grad, taps_grad, head_grad, owners),
     )
+    if tuned(axes):
+        moving.interleave("conv", "side")
     return output, token_grad, moving.finish()
 
 

time: 631 us -> 626 us (level)
  starting transfers between devices: 61.7 us -> 46.6 us
  other arithmetic: 154 us -> 162 us
    ppermute x45, starting transfers between devices: 61 us -> 46 us  [send(): return lax.ppermute(values, ('x', 'core', 'z', 'y'), pairs)]
    unnamed x295 -> x306, local copies, waits for them, and re-layouts: 55.4 us -> 51.7 us
  transfers between devices with their start and end apart: 50 -> 50, of which waited for: 17 -> 17; matrix products, arithmetic and copies ran while one was open for 48% -> 50% of each run, Pallas kernels for 6% -> 6%
where the time goes in v9:
time: 626 us; the launch traced here: 622 us
  other arithmetic  162 us (26%)
  waiting for transfers between devices  148 us (24%)
  local copies, waits for them, and re-layouts  116 us (19%)
  matrix products  97.3 us (16%)
  starting transfers between devices  46.6 us (7%)
  Pallas kernels  35.2 us (6%)
  between operations  16.1 us (3%)
    ppermute x45, waiting for transfers between devices, send(): return lax.ppermute(values, ('x', 'core', 'z', 'y'), pairs)  148 us
    unnamed x306, local copies, waits for them, and re-layouts  51.7 us
    ppermute x45, starting transfers between devices, send(): return lax.ppermute(values, ('x', 'core', 'z', 'y'), pairs)  46 us
    dot_general x5, matrix products, dot_right(): lax.dot_general(left, right, (((1,), (1,)), ((), ())), preferred_element_...  30.7 us
    dot_general x6, matrix products, dot(): return jnp.dot(left, right, preferred_element_type=jnp.float32)  27.6 us
    convert_element_type x11, other arithmetic, add_low(): (left.astype(jnp.float32) + right.astype(jnp.float32)).astype(jnp.bfloat16)  23.6 us
    convert_element_type x5, other arithmetic, round_value(): values.astype(jnp.bfloat16)  19.4 us
    pallas_call x1, Pallas kernels, scan_backward(): pl.pallas_call(scan_backward_kernel, grid=(MH // 2,), out_shape=[jax.Shap...  18.8 us
  transfers between devices with their start and end apart: 50, of which 17 were waited for; matrix products, arithmetic and copies ran while one was open for 50% of the time, Pallas kernels for 6%

profile of v9, /device:TPU:1, one launch (start us, length us, event | category | flops | bytes accessed | tf_op | source)
XLA Modules:
  0.0 622.0 jit_solution(7926496127489664005)
XLA Ops:
  30.4 14.7 %collective-permute-done.1.refs_2_ = bf16[48,1920]{1,0:T(8,128)(2,1)S(1)} collective-permute-done((bf16[48,1920]{1,0:T(8,128)(2,1)}, bf16[48,1920]{1,0:T(8,128)(2,1)S(1)}, u32[]{:S(2)}, u32[]{:S(2)}) %collective-permute-start.1) | collective-permute-done | bytes 184352 | tf_op jit(solution)/shard_map/ppermute | solution.py:375
  58.7 20.3 %collective-permute-done.11 = bf16[48,2304]{1,0:T(8,128)(2,1)S(1)} collective-permute-done((bf16[48,2304]{1,0:T(8,128)(2,1)}, bf16[48,2304]{1,0:T(8,128)(2,1)S(1)}, u32[]{:S(2)}, u32[]{:S(2)}) %collective-permute-start.11) | collective-permute-done | bytes 221216 | tf_op jit(solution)/shard_map/ppermute | solution.py:375
  85.4 8.5 %collective-permute-done.4.refs_2_ = bf16[4,16,1920]{2,1,0:T(8,128)(2,1)S(1)} collective-permute-done((bf16[4,16,1920]{2,1,0:T(8,128)(2,1)S(1)}, bf16[4,16,1920]{2,1,0:T(8,128)(2,1)S(1)}, u32[]{:S(2)}, u32[]{:S(2)}) %collective-permute-start.4) | collective-permute-done | bytes 245792 | tf_op jit(solution)/shard_map/ppermute | solution.py:375
  100.8 8.4 %collective-permute-done.5.refs_3_ = bf16[4,16,1920]{2,1,0:T(8,128)(2,1)} collective-permute-done((bf16[4,16,1920]{2,1,0:T(8,128)(2,1)S(1)}, bf16[4,16,1920]{2,1,0:T(8,128)(2,1)}, u32[]{:S(2)}, u32[]{:S(2)}) %collective-permute-start.5) | collective-permute-done | bytes 245792 | tf_op jit(solution)/shard_map/ppermute | solution.py:375
  109.3 6.5 %collective-permute-done.13.refs_1_ = bf16[4,48,2304]{2,1,0:T(8,128)(2,1)} collective-permute-done((bf16[4,48,2304]{2,1,0:T(8,128)(2,1)S(1)}, bf16[4,48,2304]{2,1,0:T(8,128)(2,1)}, u32[]{:S(2)}, u32[]{:S(2)}) %collective-permute-start.13) | collective-permute-done | bytes 884768 | tf_op jit(solution)/shard_map/ppermute | solution.py:375
  150.9 9.2 %multiply_convert_fusion.1 = (bf16[512,1792]{1,0:T(8,128)(2,1)S(1)}, f32[512,1792]{1,0:T(8,128)}) fusion(f32[509,1792]{1,0:T(8,128)} %slice.332, pred[512]{0:T(512)(128)(4,1)} %get-tuple-element.273, f32[1792]{0:T(1024)S(1)} %mul.775, f32[510,1792]{1,0:T(8,128)} %slice.330, pred[512]{0:T(512)(128)(4,1)S(1)} %copy-done.131, f32[1792]{0:T(1024)S(1)} %mul.772, ...), kind=kLoop, calls=%fused_computation.64 | loop fusion | flops 14680064 | bytes 20179456 | tf_op jit(solution)/shard_map/jvp()/convert_element_type | solution.py:35
  170.0 7.8 %scan_forward.1.out_ref = f32[512,1536]{1,0:T(8,128)S(1)} custom-call(bf16[512,1792]{1,0:T(8,128)(2,1)S(1)} %get-tuple-element.207.x_ref.b_ref.c_ref, bf16[512,1792]{1,0:T(8,128)(2,1)S(1)} %get-tuple-element.207.x_ref.b_ref.c_ref, bf16[512,1792]{1,0:T(8,128)(2,1)S(1)} %get-tuple-element.207.x_ref.b_ref.c_ref, f32[12,512,2]{2,1,0:T(8,128)S(1)} %bitcast.304, ...), custom_call_target="tpu_custom_call" | custom-call | tf_op jit(solution)/shard_map/scan_forward/pallas_call | solution.py:271
  193.8 7.4 %fusion.137 = (f32[2,4,512]{2,1,0:T(4,128)S(1)}, f32[2,4,512,512]{2,3,1,0:T(8,128)}) fusion(pred[512,512]{0,1:T(8,128)(4,1)S(1)} %copy-done.77, bf16[512,2,4,64]{0,3,2,1:T(8,128)(2,1)} %bitcast.352, bf16[512,2,64]{0,2,1:T(8,128)(2,1)S(1)} %pad_maximum_fusion.26), kind=kOutput, calls=%fused_computation.348 | convolution fusion | flops 276824576 | bytes 9322496 | tf_op jit(solution)/shard_map/jvp()/sub | solution.py:130
  201.3 6.9 %divide_convert_fusion = bf16[2,4,512,512]{2,3,1,0:T(8,128)(2,1)} fusion(f32[2,4,512,512]{2,3,1,0:T(8,128)} %get-tuple-element.275, f32[2,4,512]{2,1,0:T(4,128)S(1)} %get-tuple-element.274), kind=kLoop, calls=%fused_computation.12 | loop fusion | flops 4194304 | bytes 12599296 | tf_op jit(solution)/shard_map/jvp()/convert_element_type | solution.py:35
  222.1 10.4 %fusion.144 = f32[512,4096]{1,0:T(8,128)} fusion(bf16[512,1024]{1,0:T(8,128)(2,1)S(1)} %multiply_convert_fusion.3, bf16[1024,4096]{1,0:T(8,128)(2,1)} %all-gather.5.cloned.1.call-done), kind=kOutput, calls=%fused_computation.351 | convolution fusion | flops 4294967296 | bytes 17825792 | tf_op jit(solution)/shard_map/dot_general | solution.py:97
  232.5 6.4 %fusion.70 = (f32[512,2048]{1,0:T(8,128)S(1)}, f32[512,2048]{1,0:T(8,128)S(1)}, bf16[512,2048]{1,0:T(8,128)(2,1)S(1)}) fusion(f32[512,4096]{1,0:T(8,128)} %fusion.144, bf16[2048,1024]{1,0:T(8,128)(2,1)S(1)} %bitcast.338, bf16[512,1024]{1,0:T(8,128)(2,1)S(1)} %copy-done.71, pred[512]{0:T(512)(128)(4,1)S(1)} %copy-done.143), kind=kOutput, calls=%fused_computation.183 | convolution fusion | flops 2162688000 | bytes 24117760 | tf_op jit(solution)/shard_map/dot_general | solution.py:105
  247.4 7.0 %convolution_convert_fusion = bf16[1024,4096]{1,0:T(8,128)(2,1)S(1)} fusion(bf16[512,1024]{1,0:T(8,128)(2,1)S(1)} %multiply_convert_fusion.3, bf16[512,4096]{1,0:T(8,128)(2,1)} %fence.11), kind=kOutput, calls=%fused_computation.14 | convolution fusion | flops 4299161600 | bytes 13631488 | tf_op jit(solution)/shard_map/dot_general | solution.py:101
  264.6 10.5 %fusion.145.refs_0_ = f32[512,1024]{1,0:T(8,128)} fusion(bf16[512,4096]{1,0:T(8,128)(2,1)} %fence.11, bf16[1024,4096]{1,0:T(8,128)(2,1)} %all-gather.5.cloned.1.call-done), kind=kOutput, calls=%fused_computation.352 | convolution fusion | flops 4294967296 | bytes 14680064 | tf_op jit(solution)/shard_map/dot_general | solution.py:105
  297.5 7.0 %add_convert_fusion.2 = bf16[512,1024]{1,0:T(8,128)(2,1)} fusion(f32[512,1024]{1,0:T(8,128)} %copy-done.23, bf16[512,2048]{1,0:T(8,128)(2,1)} %copy-done.145, bf16[2048,1024]{1,0:T(8,128)(2,1)} %bitcast.337), kind=kOutput, calls=%fused_computation.113 | convolution fusion | flops 2148532224 | bytes 9437184 | tf_op jit(solution)/shard_map/dot_general | solution.py:97
  312.6 7.2 %fusion.1 = bf16[8,64,4096]{2,1,0:T(8,128)(2,1)} fusion(bf16[8,64,4096]{2,1,0:T(8,128)(2,1)} %collective-permute-done.21, bf16[8,2,64,4096]{3,2,1,0:T(8,128)(2,1)} %bitcast.322, s32[]{:T(128)S(6)} %select_n.317), kind=kLoop, calls=%fused_computation.2 | loop fusion | flops 8388608 | bytes 12582916 | tf_op jit(solution)/shard_map/convert_element_type | solution.py:461
  365.3 18.8 %scan_backward.1 = (f32[512,1536]{1,0:T(8,128)S(1)}, f32[12,512,2]{2,1,0:T(8,128)S(1)}, f32[12,512,2]{2,1,0:T(8,128)S(1)}, f32[1,1536]{1,0:T(1,128)S(1)}, bf16[512,512]{1,0:T(8,128)(2,1)S(1)}) custom-call(f32[512,1536]{1,0:T(8,128)S(1)} %copy-done.5, f32[512,1536]{1,0:T(8,128)S(1)} %copy-done.2, bf16[512,1792]{1,0:T(8,128)(2,1)S(1)} %get-tuple-element.207.x_ref.b_ref.c_ref, ...), custom_call_target="tpu_custom_call" | custom-call | tf_op jit(solution)/shard_map/scan_backward/pallas_call | solution.py:289
  420.7 9.9 %multiply_reduce_fusion.4 = (f32[1792]{0:T(1024)S(1)}, f32[1792]{0:T(1024)S(1)}, f32[1792]{0:T(1024)S(1)}, f32[1792]{0:T(1024)S(1)}, f32[1792]{0:T(1024)S(1)}, /*index=5*/f32[512,1792]{1,0:T(8,128)S(1)}) fusion(f32[509,1792]{1,0:T(8,128)} %slice.332, pred[512]{0:T(512)(128)(4,1)S(1)} %copy-done.135, f32[512,1920]{1,0:T(8,128)} %copy-done.16, ...), kind=kLoop, calls=%fused_computation.62 | loop fusion | flops 19258624 | bytes 25684480 | tf_op jit(solution)/shard_map/transpose(jvp())/reduce_sum | solution.py:146
  438.5 6.2 %add_convert_fusion.1 = bf16[512,1792]{1,0:T(8,128)(2,1)S(1)} fusion(f32[512,1792]{1,0:T(8,128)} %copy-done.15, f32[511,1792]{1,0:T(8,128)} %fusion.21, f32[510,1792]{1,0:T(8,128)} %fusion.22, f32[509,1792]{1,0:T(8,128)} %fusion.23, f32[1792]{0:T(1024)S(1)} %copy-done.98), kind=kLoop, calls=%fused_computation.63 | loop fusion | flops 4587520 | bytes 16479232 | tf_op jit(solution)/shard_map/convert.16
  478.3 21.0 %collective-permute-done.25 = bf16[4,48,2304]{2,1,0:T(8,128)(2,1)} collective-permute-done((bf16[4,48,2304]{2,1,0:T(8,128)(2,1)S(1)}, bf16[4,48,2304]{2,1,0:T(8,128)(2,1)}, u32[]{:S(2)}, u32[]{:S(2)}) %collective-permute-start.25) | collective-permute-done | bytes 884768 | tf_op jit(solution)/shard_map/ppermute | solution.py:375
  517.7 17.2 %collective-permute-done.28 = bf16[48,2304]{1,0:T(8,128)(2,1)S(1)} collective-permute-done((bf16[48,2304]{1,0:T(8,128)(2,1)}, bf16[48,2304]{1,0:T(8,128)(2,1)S(1)}, u32[]{:S(2)}, u32[]{:S(2)}) %collective-permute-start.28) | collective-permute-done | bytes 221216 | tf_op jit(solution)/shard_map/ppermute | solution.py:375
  545.1 15.7 %collective-permute-done.32 = bf16[4,48,1920]{2,1,0:T(8,128)(2,1)S(1)} collective-permute-done((bf16[4,48,1920]{2,1,0:T(8,128)(2,1)S(1)}, bf16[4,48,1920]{2,1,0:T(8,128)(2,1)S(1)}, u32[]{:S(2)}, u32[]{:S(2)}) %collective-permute-start.32) | collective-permute-done | bytes 737312 | tf_op jit(solution)/shard_map/ppermute | solution.py:375
  566.8 11.1 %collective-permute-done.35 = bf16[48,1920]{1,0:T(8,128)(2,1)} collective-permute-done((bf16[48,1920]{1,0:T(8,128)(2,1)S(1)}, bf16[48,1920]{1,0:T(8,128)(2,1)}, u32[]{:S(2)}, u32[]{:S(2)}) %collective-permute-start.35) | collective-permute-done | bytes 184352 | tf_op jit(solution)/shard_map/ppermute | solution.py:375
  590.1 6.7 %fusion.54 = (f32[128,4120]{1,0:T(8,128)}, f32[128,4120]{1,0:T(8,128)}, f32[128,4120]{1,0:T(8,128)}) fusion(f32[128,4120]{1,0:T(8,128)} %copy.242, bf16[1816,128]{0,1:T(8,128)(2,1)} %maximum_bitcast_fusion.1, bf16[2304,128]{0,1:T(8,128)(2,1)S(1)} %maximum_bitcast_fusion, f32[128,4120]{1,0:T(8,128)} %copy.237, f32[128,4120]{1,0:T(8,128)S(1)} %copy-done.21), kind=kLoop, calls=%fused_computation.134 | loop fusion | flops 10019840 | bytes 13711360 | tf_op jit(solution)/shard_map/transpose | solution.py:792
  609.2 6.1 multiply_subtract_fusion
  (659 shorter events, 354.8 us)
Async XLA Ops:
  7.2 205.2 %all-gather.3.cloned.1.call-start = ((), (), s32[]{:S(2)}) async-start(), calls=%async_computation.3 | async-start | bytes 8650752 | tf_op jit(solution)/shard_map/all_gather | solution.py:353
  9.1 213.0 %all-gather.5.cloned.1.call-start = ((), (), s32[]{:S(2)}) async-start(), calls=%async_computation.4 | async-start | bytes 8650752 | tf_op jit(solution)/shard_map/all_gather | solution.py:345
  10.9 395.8 %reduce-scatter.8.cloned.1.call-start = ((), (), s32[]{:S(2)}) async-start(), calls=%async_computation.7 | async-start | bytes 2228224 | tf_op jit(solution)/shard_map/reduce_scatter | solution.py:512
  46.4 32.6 %collective-permute-start.11 = (bf16[48,2304]{1,0:T(8,128)(2,1)}, bf16[48,2304]{1,0:T(8,128)(2,1)S(1)}, u32[]{:S(2)}, u32[]{:S(2)}) collective-permute-start(bf16[48,2304]{1,0:T(8,128)(2,1)} %fence.10), channel_id=1, source_target_pairs={{0,4},{1,5},{2,6},{3,7},{4,0},{5,1},{6,2},{7,3},{8,12},{9,13},{10,... | collective-permute-start | bytes 663560 | tf_op jit(solution)/shard_map/ppermute | solution.py:375
  48.2 30.8 %collective-permute-start.10 = (bf16[48,2304]{1,0:T(8,128)(2,1)}, bf16[48,2304]{1,0:T(8,128)(2,1)S(1)}, u32[]{:S(2)}, u32[]{:S(2)}) collective-permute-start(bf16[48,2304]{1,0:T(8,128)(2,1)} %fence.10), channel_id=1, source_target_pairs={{0,2},{1,3},{2,4},{3,5},{4,6},{5,7},{6,0},{7,1},{8,10},{9,11},{10,... | collective-permute-start | bytes 663560 | tf_op jit(solution)/shard_map/ppermute | solution.py:375
  51.4 45.0 %collective-permute-start.3 = (bf16[4,48,1920]{2,1,0:T(8,128)(2,1)S(1)}, bf16[4,48,1920]{2,1,0:T(8,128)(2,1)S(1)}, u32[]{:S(2)}, u32[]{:S(2)}) collective-permute-start(bf16[4,48,1920]{2,1,0:T(8,128)(2,1)S(1)} %pad_maximum_fusion.13.refs_0_), channel_id=1, source_target_pairs={{0,1},{1,0},{2,3},{3,2},{4,5},{5,4},{6,7},{7,6},{8,9},{9,8},{10,11... | collective-permute-start | bytes 2211848 | tf_op jit(solution)/shard_map/ppermute | solution.py:375
  80.1 35.7 %collective-permute-start.13 = (bf16[4,48,2304]{2,1,0:T(8,128)(2,1)S(1)}, bf16[4,48,2304]{2,1,0:T(8,128)(2,1)}, u32[]{:S(2)}, u32[]{:S(2)}) collective-permute-start(bf16[4,48,2304]{2,1,0:T(8,128)(2,1)S(1)} %pad_maximum_fusion.11.refs_0_), channel_id=1, source_target_pairs={{0,1},{1,0},{2,3},{3,2},{4,5},{5,4},{6,7},{7,6},{8,9},{9,8},{10,11... | collective-permute-start | bytes 2654216 | tf_op jit(solution)/shard_map/ppermute | solution.py:375
  83.6 40.7 %collective-permute-start.6 = (bf16[4,48,1920]{2,1,0:T(8,128)(2,1)S(1)}, bf16[4,48,1920]{2,1,0:T(8,128)(2,1)}, u32[]{:S(2)}, u32[]{:S(2)}) collective-permute-start(bf16[4,48,1920]{2,1,0:T(8,128)(2,1)S(1)} %pad_maximum_fusion.13.refs_0_), channel_id=1, source_target_pairs={{0,8},{1,9},{2,10},{3,11},{4,12},{5,13},{6,14},{7,15},{8,0},{9,1},... | collective-permute-start | bytes 2211848 | tf_op jit(solution)/shard_map/ppermute | solution.py:375
  97.6 31.1 %collective-permute-start.7 = (bf16[4,48,1920]{2,1,0:T(8,128)(2,1)S(1)}, bf16[4,48,1920]{2,1,0:T(8,128)(2,1)}, u32[]{:S(2)}, u32[]{:S(2)}) collective-permute-start(bf16[4,48,1920]{2,1,0:T(8,128)(2,1)S(1)} %collective-permute-done.3.refs_1_), channel_id=1, source_target_pairs={{0,8},{1,9},{2,10},{3,11},{4,12},{5,13},{6,14},{7,15},{8,0},{9,1},... | collective-permute-start | bytes 2211848 | tf_op jit(solution)/shard_map/ppermute | solution.py:375
  124.0 53.8 %collective-permute-start.16 = (bf16[4,48,2304]{2,1,0:T(8,128)(2,1)S(1)}, bf16[4,48,2304]{2,1,0:T(8,128)(2,1)}, u32[]{:S(2)}, u32[]{:S(2)}) collective-permute-start(bf16[4,48,2304]{2,1,0:T(8,128)(2,1)S(1)} %pad_maximum_fusion.11.refs_0_), channel_id=1, source_target_pairs={{0,8},{1,9},{2,10},{3,11},{4,12},{5,13},{6,14},{7,15},{8,0},{9,1},... | collective-permute-start | bytes 2654216 | tf_op jit(solution)/shard_map/ppermute | solution.py:375
  124.3 53.4 %collective-permute-start.18 = (bf16[4,16,2304]{2,1,0:T(8,128)(2,1)S(1)}, bf16[4,16,2304]{2,1,0:T(8,128)(2,1)}, u32[]{:S(2)}, u32[]{:S(2)}) collective-permute-start(bf16[4,16,2304]{2,1,0:T(8,128)(2,1)S(1)} %collective-permute-done.14.refs_2_), channel_id=1, source_target_pairs={{0,8},{1,9},{2,10},{3,11},{4,12},{5,13},{6,14},{7,15},{8,0},{9,1},... | collective-permute-start | bytes 884744 | tf_op jit(solution)/shard_map/ppermute | solution.py:375
  124.6 53.2 %collective-permute-start.17 = (bf16[4,48,2304]{2,1,0:T(8,128)(2,1)}, bf16[4,48,2304]{2,1,0:T(8,128)(2,1)}, u32[]{:S(2)}, u32[]{:S(2)}) collective-permute-start(bf16[4,48,2304]{2,1,0:T(8,128)(2,1)} %collective-permute-done.13.refs_1_), channel_id=1, source_target_pairs={{0,8},{1,9},{2,10},{3,11},{4,12},{5,13},{6,14},{7,15},{8,0},{9,1},... | collective-permute-start | bytes 2654216 | tf_op jit(solution)/shard_map/ppermute | solution.py:375
  127.9 49.9 %collective-permute-start.19 = (bf16[4,16,2304]{2,1,0:T(8,128)(2,1)}, bf16[4,16,2304]{2,1,0:T(8,128)(2,1)}, u32[]{:S(2)}, u32[]{:S(2)}) collective-permute-start(bf16[4,16,2304]{2,1,0:T(8,128)(2,1)} %collective-permute-done.15.refs_3_), channel_id=1, source_target_pairs={{0,8},{1,9},{2,10},{3,11},{4,12},{5,13},{6,14},{7,15},{8,0},{9,1},... | collective-permute-start | bytes 884744 | tf_op jit(solution)/shard_map/ppermute | solution.py:375
  260.0 52.6 %collective-permute-start.21 = (bf16[8,64,4096]{2,1,0:T(8,128)(2,1)}, bf16[8,64,4096]{2,1,0:T(8,128)(2,1)}, u32[]{:S(2)}, u32[]{:S(2)}) collective-permute-start(bf16[8,64,4096]{2,1,0:T(8,128)(2,1)} %dynamic-slice_bitcast_fusion.refs_2_), channel_id=1, source_target_pairs={{0,8},{1,9},{2,10},{3,11},{4,12},{5,13},{6,14},{7,15},{8,0},{9,1},... | collective-permute-start | bytes 12582920 | tf_op jit(solution)/shard_map/ppermute | solution.py:375
  264.1 213.1 %reduce-scatter.4.cloned.1.call-start = ((), (), s32[]{:S(2)}) async-start(), calls=%async_computation.5 | async-start | bytes 2228224 | tf_op jit(solution)/shard_map/reduce_scatter | solution.py:512
  312.5 276.4 %reduce-scatter.6.cloned.1.call-start = ((), (), s32[]{:S(2)}) async-start(), calls=%async_computation.6 | async-start | bytes 4456448 | tf_op jit(solution)/shard_map/reduce_scatter | solution.py:512
  359.0 57.1 %collective-permute-start.23 = (bf16[4,2,64,2304]{3,2,1,0:T(8,128)(2,1)}, bf16[4,2,64,2304]{3,2,1,0:T(8,128)(2,1)}, u32[]{:S(2)}, u32[]{:S(2)}) collective-permute-start(bf16[4,2,64,2304]{3,2,1,0:T(8,128)(2,1)} %dynamic-slice_bitcast_fusion.1.refs_2_), channel_id=1, source_target_pairs={{0,8},{1,9},{2,10},{3,11},{4,12},{5,13},{6,14},{7,15},{8,0},{9,1},... | collective-permute-start | bytes 7077896 | tf_op jit(solution)/shard_map/ppermute | solution.py:375
  415.6 31.5 %collective-permute-start.44 = (bf16[128,1024]{1,0:T(8,128)(2,1)}, bf16[128,1024]{1,0:T(8,128)(2,1)}, u32[]{:S(2)}, u32[]{:S(2)}) collective-permute-start(bf16[128,1024]{1,0:T(8,128)(2,1)} %pad_maximum_fusion.22), channel_id=1, source_target_pairs={{0,8},{1,9},{2,10},{3,11},{4,12},{5,13},{6,14},{7,15},{8,0},{9,1},... | collective-permute-start | bytes 786440 | tf_op jit(solution)/shard_map/ppermute | solution.py:375
  420.0 31.3 %collective-permute-start.24 = (bf16[4,2,16,2304]{3,2,1,0:T(8,128)(2,1)}, bf16[4,2,16,2304]{3,2,1,0:T(8,128)(2,1)}, u32[]{:S(2)}, u32[]{:S(2)}) collective-permute-start(bf16[4,2,16,2304]{3,2,1,0:T(8,128)(2,1)} %constant_dynamic-slice_fusion.1.refs_1_), channel_id=1, source_target_pairs={{0,16},{1,17},{2,18},{3,19},{4,20},{5,21},{6,22},{7,23},{8,24},{9,... | collective-permute-start | bytes 1769480 | tf_op jit(solution)/shard_map/ppermute | solution.py:375
  462.2 37.1 %collective-permute-start.25 = (bf16[4,48,2304]{2,1,0:T(8,128)(2,1)S(1)}, bf16[4,48,2304]{2,1,0:T(8,128)(2,1)}, u32[]{:S(2)}, u32[]{:S(2)}) collective-permute-start(bf16[4,48,2304]{2,1,0:T(8,128)(2,1)S(1)} %copy-done.48), channel_id=1, source_target_pairs={{0,1},{1,0},{2,3},{3,2},{4,5},{5,4},{6,7},{7,6},{8,9},{9,8},{10,11... | collective-permute-start | bytes 2654216 | tf_op jit(solution)/shard_map/ppermute | solution.py:375
  475.0 30.1 %collective-permute-start.26 = (bf16[4,2,64,1920]{3,2,1,0:T(8,128)(2,1)}, bf16[4,2,64,1920]{3,2,1,0:T(8,128)(2,1)}, u32[]{:S(2)}, u32[]{:S(2)}) collective-permute-start(bf16[4,2,64,1920]{3,2,1,0:T(8,128)(2,1)} %fusion.44), channel_id=1, source_target_pairs={{0,8},{1,9},{2,10},{3,11},{4,12},{5,13},{6,14},{7,15},{8,0},{9,1},... | collective-permute-start | bytes 5898248 | tf_op jit(solution)/shard_map/ppermute | solution.py:375
  507.4 29.2 %collective-permute-start.30 = (bf16[4,2,16,1920]{3,2,1,0:T(8,128)(2,1)S(1)}, bf16[4,2,16,1920]{3,2,1,0:T(8,128)(2,1)}, u32[]{:S(2)}, u32[]{:S(2)}) collective-permute-start(bf16[4,2,16,1920]{3,2,1,0:T(8,128)(2,1)S(1)} %constant_dynamic-slice_fusion.refs_3_), channel_id=1, source_target_pairs={{0,16},{1,17},{2,18},{3,19},{4,20},{5,21},{6,22},{7,23},{8,24},{9,... | collective-permute-start | bytes 1474568 | tf_op jit(solution)/shard_map/ppermute | solution.py:375
  508.3 26.6 %collective-permute-start.28 = (bf16[48,2304]{1,0:T(8,128)(2,1)}, bf16[48,2304]{1,0:T(8,128)(2,1)S(1)}, u32[]{:S(2)}, u32[]{:S(2)}) collective-permute-start(bf16[48,2304]{1,0:T(8,128)(2,1)} %get-tuple-element.49), channel_id=1, source_target_pairs={{0,4},{1,5},{2,6},{3,7},{4,0},{5,1},{6,2},{7,3},{8,12},{9,13},{10,... | collective-permute-start | bytes 663560 | tf_op jit(solution)/shard_map/ppermute | solution.py:375
  509.7 25.1 %collective-permute-start.27 = (bf16[48,2304]{1,0:T(8,128)(2,1)}, bf16[48,2304]{1,0:T(8,128)(2,1)S(1)}, u32[]{:S(2)}, u32[]{:S(2)}) collective-permute-start(bf16[48,2304]{1,0:T(8,128)(2,1)} %get-tuple-element.48), channel_id=1, source_target_pairs={{0,2},{1,3},{2,4},{3,5},{4,6},{5,7},{6,0},{7,1},{8,10},{9,11},{10,... | collective-permute-start | bytes 663560 | tf_op jit(solution)/shard_map/ppermute | solution.py:375
  (179 other events, 1591.0 us)
Sparse Core Ops, SparseCore 0:
  11.5 117.2 all-gather.2
  132.2 74.6 all-gather.4
  264.3 69.1 reduce-scatter.7
  336.1 77.6 reduce-scatter.3
  416.0 118.4 reduce-scatter.5
